TPU v7x, 32 devices: a whole 2x2x4 slice. The times are simulated.
32 devices in a mesh: dp: 8 (over z, y), tensor: 4 (over x, core).
Axes of the slice: x: 2, y: 2, z: 4, core: 2. Of those that a mesh axis runs over, the one named last changes fastest.
Arguments:
- tokens: bfloat16 [16384, 1024], P('dp'), may hold values from -6 to 6
- prefix: int32 [8], P('dp'), may hold values from 204 to 1024
- gain_attn: bfloat16 [1024], replicated, may hold values from 0.5 to 1.5
- w_query: bfloat16 [1024, 1024], P(None, 'tensor'), may hold values from -0.1875 to 0.1875
- w_key: bfloat16 [1024, 512], P(None, 'tensor'), may hold values from -0.1875 to 0.1875
- w_value: bfloat16 [1024, 512], P(None, 'tensor'), may hold values from -0.1875 to 0.1875
- w_out: bfloat16 [1024, 1024], P('tensor'), may hold values from -3 to 3
- gain_moe: bfloat16 [1024], replicated, may hold values from 0.5 to 1.5
- w_router: bfloat16 [1024, 32], replicated, may hold values from -0.09375 to 0.09375
- routes: int32 [16384, 8], P(('dp', 'tensor')), may hold values from 0 to 31, all different within a row
- fill_order: int32 [32, 512], P(('dp', 'tensor')), may hold values from 0 to 511, each once within a row
- w_gate: bfloat16 [32, 1024, 512], P('dp', None, 'tensor'), may hold values from -0.1875 to 0.1875
- w_up: bfloat16 [32, 1024, 512], P('dp', None, 'tensor'), may hold values from -0.1875 to 0.1875
- w_down: bfloat16 [32, 512, 1024], P('dp', 'tensor'), may hold values from -1 to 1
- cotangent: bfloat16 [16384, 1024], P(('dp', 'tensor')), may hold values from -6 to 6
Outputs:
- block_output: bfloat16 [16384, 1024], P(('dp', 'tensor'))
- grad_tokens: float32 [16384, 1024], P('dp')
- grad_gain_attn: float32 [1024], replicated
- grad_query: float32 [1024, 1024], P(None, 'tensor')
- grad_key: float32 [1024, 512], P(None, 'tensor')
- grad_value: float32 [1024, 512], P(None, 'tensor')
- grad_out: float32 [1024, 1024], P('tensor')
- grad_gain_moe: float32 [1024], replicated
- grad_router: float32 [1024, 32], replicated
- grad_gate: float32 [32, 1024, 512], P('dp', None, 'tensor')
- grad_up: float32 [32, 1024, 512], P('dp', None, 'tensor')
- grad_down: float32 [32, 512, 1024], P('dp', 'tensor')
Inputs may be any that keep to these rules, and one draw needn't show every extreme that they name: `routes`: each row names 8 different experts, and every expert is named by some row. `fill_order`: each row is a permutation of 0 to 511.
All inputs are finite; a program needn't handle non-finite values.
Results may differ from a plain program's by a relative error of at most 0.023.
Values may be sent and summed in bfloat16 or wider, within the bound.
No kernel may reach another device: no remote copies, remote signals or barrier semaphores. Data moves between devices by JAX's collectives and lax.ppermute only.
A program may use at most 512 MiB of HBM per device.

v0:
```python
import jax
import jax.numpy as jnp
from jax import lax
from jax.sharding import PartitionSpec as P

HD = 64
EXPERTS = 32
TOPK = 8


EPSILON = 1e-06
THETA_BASE = 10000.0
HIGHEST = lax.Precision.HIGHEST


def rope_tables(length, width_in):
    half_width = width_in // 2
    frequency = THETA_BASE ** (-(jnp.arange(half_width, dtype=jnp.float32) / half_width))
    angles = jnp.arange(length, dtype=jnp.float32)[:, None] * frequency[None, :]
    return (jnp.cos(angles), jnp.sin(angles))


def rotate(vectors, cosine, sine, direction):
    half_width = vectors.shape[-1] // 2
    front_half = vectors[..., :half_width]
    back_half = vectors[..., half_width:]
    cos_part = cosine[:, None, :]
    sin_part = sine[:, None, :] * direction
    return jnp.concatenate(
        [
            front_half * cos_part - back_half * sin_part,
            back_half * cos_part + front_half * sin_part,
        ],
        -1,
    )


def per_device(
    tokens,
    prefix,
    gain_attn,
    w_query,
    w_key,
    w_value,
    w_out,
    gain_moe,
    w_router,
    routes,
    fill_order,
    w_gate,
    w_up,
    w_down,
    cotangent,
):
    tensor_rank = lax.axis_index("tensor")
    data_count = lax.axis_size("dp")
    length = tokens.shape[0]
    model_width = tokens.shape[1]
    own_rows = routes.shape[0]
    local_experts = w_gate.shape[0]
    capacity = own_rows * TOPK // EXPERTS
    slot_total = EXPERTS * capacity
    heads_local = w_query.shape[1] // HD
    kv_local = w_key.shape[1] // HD
    group_size = heads_local // kv_local
    block_rows = min(512, length)
    block_count = length // block_rows
    score_scale = HD ** (-0.5)
    x_full = tokens.astype(jnp.float32)
    rms_one = lax.rsqrt(jnp.mean(x_full * x_full, -1, keepdims=True) + EPSILON)
    gain_one = gain_attn.astype(jnp.float32)
    normed_one = (x_full * rms_one * gain_one).astype(jnp.bfloat16)
    query_raw = jnp.dot(normed_one, w_query, preferred_element_type=jnp.float32)
    key_raw = jnp.dot(normed_one, w_key, preferred_element_type=jnp.float32)
    values = (
        jnp.dot(normed_one, w_value, preferred_element_type=jnp.float32)
        .astype(jnp.bfloat16)
        .reshape(length, kv_local, HD)
    )
    cosine, sine = rope_tables(length, HD)
    query_rot = rotate(query_raw.reshape(length, heads_local, HD), cosine, sine, 1.0).astype(
        jnp.bfloat16
    )
    key_rot = rotate(key_raw.reshape(length, kv_local, HD), cosine, sine, 1.0).astype(jnp.bfloat16)
    query_blocks = query_rot.reshape(block_count, block_rows, kv_local, group_size, HD)
    block_starts = jnp.arange(block_count, dtype=jnp.int32) * block_rows
    positions = jnp.arange(length, dtype=jnp.int32)
    prefix_len = prefix[0]

    def block_scores(query_block, offset):
        query_pos = offset + jnp.arange(block_rows, dtype=jnp.int32)
        raw_scores = (
            jnp.einsum("igjd,kgd->gjik", query_block, key_rot, preferred_element_type=jnp.float32)
            * score_scale
        )
        visible = (positions[None, :] <= query_pos[:, None]) | (positions[None, :] < prefix_len)
        return jnp.where(visible[None, None], raw_scores, -1e30)

    def attend_block(inputs):
        query_block, offset = inputs
        scores = block_scores(query_block, offset)
        row_peak = jnp.max(scores, -1, keepdims=True)
        weights = jnp.exp(scores - row_peak)
        row_total = jnp.sum(weights, -1, keepdims=True)
        probabilities = (weights / row_total).astype(jnp.bfloat16)
        attended = jnp.einsum(
            "gjik,kgd->igjd", probabilities, values, preferred_element_type=jnp.float32
        )
        return (attended.astype(jnp.bfloat16), (row_peak + jnp.log(row_total))[..., 0])

    attended_blocks, log_totals = lax.map(attend_block, (query_blocks, block_starts))
    attended_all = attended_blocks.reshape(length, heads_local * HD)
    attention_rows = lax.psum_scatter(
        jnp.dot(attended_all, w_out, preferred_element_type=jnp.float32),
        "tensor",
        scatter_dimension=0,
        tiled=True,
    )
    x_rows = lax.dynamic_slice_in_dim(x_full, tensor_rank * own_rows, own_rows, 0)
    hidden_in = x_rows + attention_rows
    rms_two = lax.rsqrt(jnp.mean(hidden_in * hidden_in, -1, keepdims=True) + EPSILON)
    gain_two = gain_moe.astype(jnp.float32)
    normed_two = (hidden_in * rms_two * gain_two).astype(jnp.bfloat16)
    logits = jnp.dot(normed_two, w_router, preferred_element_type=jnp.float32)
    expert_ids = jnp.arange(EXPERTS, dtype=jnp.int32)
    choice_hot = (routes[:, :, None] == expert_ids[None, None, :]).astype(jnp.float32)
    chosen = jnp.sum(choice_hot * logits[:, None, :], -1)
    top_logit = jnp.max(chosen, -1, keepdims=True)
    raised = jnp.exp(chosen - top_logit)
    gate_weights = raised / jnp.sum(raised, -1, keepdims=True)
    member = jnp.sum(choice_hot, 1)
    priority = fill_order[0]
    earlier = (priority[None, :] < priority[:, None]).astype(jnp.float32)
    slot_full = jnp.dot(earlier, member, precision=HIGHEST)
    slot_pair = jnp.sum(choice_hot * slot_full[:, None, :], -1).astype(jnp.int32)
    kept_pair = slot_pair < capacity
    flat_slot = jnp.where(kept_pair, routes * capacity + slot_pair, slot_total)
    slot_ids = jnp.arange(slot_total, dtype=jnp.int32)
    slot_hot = (flat_slot[:, :, None] == slot_ids[None, None, :]).astype(jnp.float32)
    token_hot = jnp.sum(slot_hot, 1)
    filled = jnp.sum(token_hot, 0)
    token_of = jnp.dot(
        jnp.arange(own_rows, dtype=jnp.float32), token_hot, precision=HIGHEST
    ).astype(jnp.int32)
    gate_of = jnp.einsum("ik,iks->s", gate_weights, slot_hot, precision=HIGHEST)
    send_rows = jnp.take(normed_two, token_of, 0) * filled[:, None].astype(jnp.bfloat16)
    outgoing = send_rows.reshape(data_count, local_experts * capacity, model_width)
    incoming = lax.all_to_all(outgoing, "dp", split_axis=0, concat_axis=0, tiled=True)
    incoming = incoming.reshape(data_count, local_experts, capacity, model_width)
    shard_part = lax.all_gather(incoming[None], "tensor", axis=0, tiled=True)
    gate_part = jnp.einsum(
        "tsecd,edf->tsecf", shard_part, w_gate, preferred_element_type=jnp.float32
    )
    up_part = jnp.einsum("tsecd,edf->tsecf", shard_part, w_up, preferred_element_type=jnp.float32)
    rows_all = shard_part
    activated = (gate_part / (1.0 + jnp.exp(-gate_part)) * up_part).astype(jnp.bfloat16)
    part_act = activated
    expert_out = lax.psum_scatter(
        jnp.einsum("tsecf,efd->tsecd", part_act, w_down, preferred_element_type=jnp.float32),
        "tensor",
        scatter_dimension=0,
        tiled=True,
    )[0]
    back_out = expert_out.astype(jnp.bfloat16).reshape(
        data_count, local_experts * capacity, model_width
    )
    returned = lax.all_to_all(back_out, "dp", split_axis=0, concat_axis=0, tiled=True).reshape(
        slot_total, model_width
    )
    zero_row = jnp.zeros((1, model_width), jnp.bfloat16)
    picked = jnp.take(jnp.concatenate([returned, zero_row], 0), flat_slot, 0).astype(jnp.float32)
    moe_rows = jnp.sum(gate_weights[:, :, None] * picked, 1)
    block_output = (hidden_in + moe_rows).astype(jnp.bfloat16)
    grad_rows = cotangent.astype(jnp.float32)
    gate_grad = jnp.sum(grad_rows[:, None, :] * picked, -1)
    back_rows = (jnp.take(grad_rows, token_of, 0) * gate_of[:, None]).astype(jnp.bfloat16)
    back_in = lax.all_to_all(
        back_rows.reshape(data_count, local_experts * capacity, model_width),
        "dp",
        split_axis=0,
        concat_axis=0,
        tiled=True,
    )
    back_in = back_in.reshape(data_count, local_experts, capacity, model_width)
    shard_part = lax.all_gather(back_in[None], "tensor", axis=0, tiled=True)
    part_act = activated
    part_gate = gate_part
    part_up = up_part
    down_acc = jnp.einsum(
        "tsecf,tsecd->efd", part_act, shard_part, preferred_element_type=jnp.float32
    )
    hid_grad = jnp.einsum(
        "tsecd,efd->tsecf", shard_part, w_down, preferred_element_type=jnp.float32
    )
    sigmoid_g = 1.0 / (1.0 + jnp.exp(-part_gate))
    back_gate_back = (
        hid_grad * part_up * sigmoid_g * (1.0 + part_gate * (1.0 - sigmoid_g))
    ).astype(jnp.bfloat16)
    back_up_back = (hid_grad * part_gate * sigmoid_g).astype(jnp.bfloat16)
    grad_gate = jnp.einsum(
        "tsecd,tsecf->edf", rows_all, back_gate_back, preferred_element_type=jnp.float32
    )
    grad_up = jnp.einsum(
        "tsecd,tsecf->edf", rows_all, back_up_back, preferred_element_type=jnp.float32
    )
    part_gate = back_gate_back
    part_up = back_up_back
    total_in = jnp.einsum("tsecf,edf->tsecd", part_gate, w_gate, preferred_element_type=jnp.float32)
    expert_in_grad = lax.psum_scatter(
        total_in
        + jnp.einsum("tsecf,edf->tsecd", part_up, w_up, preferred_element_type=jnp.float32),
        "tensor",
        scatter_dimension=0,
        tiled=True,
    )[0]
    return_rows = expert_in_grad.astype(jnp.bfloat16).reshape(
        data_count, local_experts * capacity, model_width
    )
    came_back = lax.all_to_all(return_rows, "dp", split_axis=0, concat_axis=0, tiled=True).reshape(
        slot_total, model_width
    )
    normed_two_grad = jnp.sum(
        jnp.take(jnp.concatenate([came_back, zero_row], 0), flat_slot, 0).astype(jnp.float32), 1
    )
    chosen_grad = gate_weights * (gate_grad - jnp.sum(gate_weights * gate_grad, -1, keepdims=True))
    logit_grad = jnp.sum(chosen_grad[:, :, None] * choice_hot, 1)
    router_part = jnp.dot(normed_two.astype(jnp.float32).T, logit_grad, precision=HIGHEST)
    normed_two_grad = normed_two_grad + jnp.dot(
        logit_grad, w_router.astype(jnp.float32).T, precision=HIGHEST
    )
    gain_two_part = jnp.sum(normed_two_grad * hidden_in * rms_two, 0)
    scaled_two = normed_two_grad * gain_two
    hidden_grad = (
        grad_rows
        + rms_two * scaled_two
        - hidden_in * rms_two**3 * jnp.mean(scaled_two * hidden_in, -1, keepdims=True)
    )
    shard_part = lax.all_gather(
        hidden_grad.astype(jnp.bfloat16), "tensor", axis=0, tiled=True
    ).astype(jnp.float32)
    attended_part = jnp.einsum(
        "id,hd->ih", shard_part.astype(jnp.bfloat16), w_out, preferred_element_type=jnp.float32
    )
    attended_grad = attended_part.astype(jnp.bfloat16)
    out_grad = jnp.einsum(
        "ih,id->hd",
        attended_all,
        shard_part.astype(jnp.bfloat16),
        preferred_element_type=jnp.float32,
    )
    grad_blocks = attended_grad.reshape(block_count, block_rows, kv_local, group_size, HD)

    def back_block(running, inputs):
        key_acc, value_acc = running
        query_block, grad_block, log_block, offset = inputs
        scores = block_scores(query_block, offset)
        probabilities = jnp.exp(scores - log_block[..., None])
        prob_grad = jnp.einsum(
            "igjd,kgd->gjik", grad_block, values, preferred_element_type=jnp.float32
        )
        center = jnp.sum(prob_grad * probabilities, -1, keepdims=True)
        score_grad = (probabilities * (prob_grad - center)).astype(jnp.bfloat16)
        query_grad = (
            jnp.einsum("gjik,kgd->igjd", score_grad, key_rot, preferred_element_type=jnp.float32)
            * score_scale
        )
        key_acc = (
            key_acc
            + jnp.einsum(
                "gjik,igjd->kgd", score_grad, query_block, preferred_element_type=jnp.float32
            )
            * score_scale
        )
        value_acc = value_acc + jnp.einsum(
            "gjik,igjd->kgd",
            probabilities.astype(jnp.bfloat16),
            grad_block,
            preferred_element_type=jnp.float32,
        )
        return ((key_acc, value_acc), query_grad)

    zero_kv = jnp.zeros((length, kv_local, HD), jnp.float32)
    (key_grad, value_grad), query_grads = lax.scan(
        back_block, (zero_kv, zero_kv), (query_blocks, grad_blocks, log_totals, block_starts)
    )
    query_back = (
        rotate(query_grads.reshape(length, heads_local, HD), cosine, sine, -1.0)
        .reshape(length, heads_local * HD)
        .astype(jnp.bfloat16)
    )
    key_back = (
        rotate(key_grad, cosine, sine, -1.0).reshape(length, kv_local * HD).astype(jnp.bfloat16)
    )
    value_back = value_grad.reshape(length, kv_local * HD).astype(jnp.bfloat16)
    query_weight = jnp.einsum(
        "id,ih->dh", normed_one, query_back, preferred_element_type=jnp.float32
    )
    key_weight = jnp.einsum("id,ih->dh", normed_one, key_back, preferred_element_type=jnp.float32)
    value_weight = jnp.einsum(
        "id,ih->dh", normed_one, value_back, preferred_element_type=jnp.float32
    )
    normed_one_grad = jnp.einsum(
        "ih,dh->id", query_back, w_query, preferred_element_type=jnp.float32
    )
    normed_one_grad = normed_one_grad + jnp.einsum(
        "ih,dh->id", key_back, w_key, preferred_element_type=jnp.float32
    )
    normed_one_grad = normed_one_grad + jnp.einsum(
        "ih,dh->id", value_back, w_value, preferred_element_type=jnp.float32
    )
    total_one, gain_two_total, router_total = (
        lax.psum(normed_one_grad.astype(jnp.bfloat16), "tensor").astype(jnp.float32),
        lax.psum(gain_two_part.astype(jnp.bfloat16), "tensor").astype(jnp.float32),
        lax.psum(router_part.astype(jnp.bfloat16), "tensor").astype(jnp.float32),
    )
    gain_one_part = jnp.sum(total_one * x_full * rms_one, 0)
    scaled_one = total_one * gain_one
    input_grad = (
        shard_part
        + rms_one * scaled_one
        - x_full * rms_one**3 * jnp.mean(scaled_one * x_full, -1, keepdims=True)
    )
    summed = (
        lax.psum(query_weight.astype(jnp.bfloat16), "dp").astype(jnp.float32),
        lax.psum(key_weight.astype(jnp.bfloat16), "dp").astype(jnp.float32),
        lax.psum(value_weight.astype(jnp.bfloat16), "dp").astype(jnp.float32),
        lax.psum(out_grad.astype(jnp.bfloat16), "dp").astype(jnp.float32),
        lax.psum(router_total.astype(jnp.bfloat16), "dp").astype(jnp.float32),
        lax.psum(gain_one_part.astype(jnp.bfloat16), "dp").astype(jnp.float32),
        lax.psum(gain_two_total.astype(jnp.bfloat16), "dp").astype(jnp.float32),
    )
    return (
        block_output,
        input_grad,
        summed[5],
        summed[0],
        summed[1],
        summed[2],
        summed[3],
        summed[6],
        summed[4],
        grad_gate,
        grad_up,
        down_acc,
    )


def solution(mesh):
    return jax.shard_map(
        per_device,
        mesh=mesh,
        in_specs=(
            P("dp", None),
            P("dp"),
            P(),
            P(None, "tensor"),
            P(None, "tensor"),
            P(None, "tensor"),
            P("tensor", None),
            P(),
            P(),
            P(("dp", "tensor"), None),
            P(("dp", "tensor"), None),
            P("dp", None, "tensor"),
            P("dp", None, "tensor"),
            P("dp", "tensor", None),
            P(("dp", "tensor"), None),
        ),
        out_specs=(
            P(("dp", "tensor"), None),
            P("dp", None),
            P(),
            P(None, "tensor"),
            P(None, "tensor"),
            P(None, "tensor"),
            P("tensor", None),
            P(),
            P(),
            P("dp", None, "tensor"),
            P("dp", None, "tensor"),
            P("dp", "tensor", None),
        ),
        check_vma=False,
    )
```

profile of v0, /device:TPU:0, one launch (start us, length us, event | category | flops | bytes accessed | tf_op | source)
XLA Modules:
  0.0 4235.1 jit_solution(15372752713197686864)
XLA Ops:
  24.7 65.3 %while.30 = (s32[]{:T(128)}, bf16[4,512,2,2,64]{1,4,3,2,0:T(8,128)(2,1)}, f32[4,2,2,512]{3,2,1,0:T(2,128)}, s32[4]{0:T(128)S(1)}, s32[]{:T(128)}, /*index=5*/bf1...) while((s32[]{:T(128)}, ...), condition=%wide.region_4.5_spmd.clone.clone, body=%wide.region_1.4_spmd.clone.clone.sunk | while | flops 1126302208 | bytes 56172676 | solution.py:111
  107.4 67.1 %reduce-scatter.8.cloned.1.call-done = f32[512,1024]{1,0:T(8,128)} async-done(((f32[2048,1024]{1,0:T(8,128)}), f32[512,1024]{1,0:T(8,128)}) %reduce-scatter.8.cloned.1.call-update) | async-done | bytes 2097168 | tf_op jit(solution)/shard_map/reduce_scatter | solution.py:113
  179.9 42.6 %convert_reduce_fusion = (bf16[4096]{0:T(1024)(128)(2,1)S(1)}, f32[512,4096]{1,0:T(8,128)}) fusion(s32[512,8]{1,0:T(8,128)S(1)} %copy.114), kind=kLoop, calls=%fused_computation.71 | loop fusion | flops 65007616 | bytes 8413184 | tf_op jit(solution)/shard_map/reduce_sum | solution.py:141
  229.0 18.1 gather_fusion
  251.8 188.5 %all_to_all.20 = bf16[8,512,1024]{2,1,0:T(8,128)(2,1)} all-to-all(bf16[8,512,1024]{2,1,0:T(8,128)(2,1)S(1)} %select_multiply_fusion), channel_id=1, replica_groups=mesh['dp'=8,'tensor'=4] {'dp'}, dimensions={0} | all-to-all | bytes 16777216 | tf_op jit(solution)/shard_map/all_to_all | solution.py:148
  451.8 32.9 fusion.57
  484.7 18.6 gather_fusion.1
  510.1 187.0 %all_to_all.21 = bf16[8,512,1024]{2,1,0:T(8,128)(2,1)} all-to-all(bf16[8,512,1024]{2,1,0:T(8,128)(2,1)S(1)} %multiply_convert_fusion), channel_id=1, replica_groups=mesh['dp'=8,'tensor'=4] {'dp'}, dimensions={0} | all-to-all | bytes 16777216 | tf_op jit(solution)/shard_map/all_to_all | solution.py:177
  706.6 25.4 fusion.106
  732.0 17.3 fusion.110
  749.3 155.4 %all-gather.6.cloned.1.call-done = bf16[4,8,4,128,1024]{4,3,1,0,2:T(8,128)(2,1)} async-done(((bf16[1,8,4,128,1024]{4,3,1,0,2:T(8,128)(2,1)}), bf16[4,8,4,128,1024]{4,3,1,0,2:T(8,128)(2,1)}) %all-gather.6.cloned.1.call-update) | async-done | bytes 33554448 | tf_op jit(solution)/shard_map/all_gather | solution.py:185
  904.7 19.0 fusion.81
  923.8 23.6 fusion.108
  947.4 43.1 %add_bitcast_fusion = f32[4,8,4,128,1024]{4,3,1,0,2:T(8,128)} fusion(f32[4,4,8,128,1024]{4,3,2,1,0:T(8,128)} %fusion.108, bf16[4,8,4,128,128]{4,3,1,0,2:T(8,128)(2,1)S(1)} %get-tuple-element.397, bf16[4,1024,128]{2,1,0:T(8,128)(2,1)S(1)} %copy-done.23), kind=kOutput, calls=%fused_computation.73 | convolution fusion | flops 4311744512 | bytes 139460608 | tf_op jit(solution)/shard_map/tsecf,edf->tsecd/dot_general | solution.py:211
  990.5 23.1 convolution_bitcast_fusion.1
  1013.5 2248.3 %all-reduce.15 = (bf16[4,8,4,128,1024]{4,3,1,0,2:T(8,128)(2,1)}, bf16[4,8,4,128,1024]{4,3,1,0,2:T(8,128)(2,1)}) all-reduce(f32[4,8,4,128,1024]{4,3,1,0,2:T(8,128)} %convolution_bitcast_fusion.1, f32[4,8,4,128,1024]{4,3,1,0,2:T(8,128)} %add_bitcast_fusion), channel_id=3, replica_groups=mesh['dp'=8,'tensor'=4] {'tensor'}, use_global_device_ids=true, to_apply=%region_14.15.clone | all-reduce | flops 33554432 | bytes 201326592
  3261.9 12.7 constant_dynamic-slice_fusion
  3296.8 175.3 %all-to-all-done.3 = bf16[8,512,1024]{2,1,0:T(8,128)(2,1)} async-done(((bf16[8,512,1024]{2,1,0:T(8,128)(2,1)}), bf16[8,512,1024]{2,1,0:T(8,128)(2,1)}, u32[]{:S(2)}, u32[]{:S(2)}) %all-to-all-start.3) | async-done | bytes 8388640 | tf_op jit(solution)/shard_map/all_to_all | solution.py:219
  3485.6 174.3 %all-to-all-done.1 = bf16[8,512,1024]{2,1,0:T(8,128)(2,1)} async-done(((bf16[8,512,1024]{2,1,0:T(8,128)(2,1)}), bf16[8,512,1024]{2,1,0:T(8,128)(2,1)}, u32[]{:S(2)}, u32[]{:S(2)}) %all-to-all-start.1) | async-done | bytes 8388640 | tf_op jit(solution)/shard_map/all_to_all | solution.py:167
  3667.5 25.7 gather_fusion.3
  3693.2 25.4 gather_fusion.2
  3718.6 18.8 fusion.66
  3749.4 17.6 fusion.100
  3767.0 19.5 fusion.95
  3796.4 225.7 %while.31 = (s32[]{:T(128)}, f32[2048,2,64]{0,2,1:T(8,128)}, f32[2048,2,64]{0,2,1:T(8,128)}, f32[4,512,2,2,64]{1,0,4,3,2:T(4,128)}, bf16[4,512,2,2,64]{1,4,3,2,0...) while((s32[]{:T(128)}, f32[2048,2,64]{0,2,1:T(8,128)}, ...), condition=%wide.region_24.26_spmd.clone.clone, body=%wide.region_22.25_spmd.clone.clone.sunk | while | flops 2750808576 | bytes 181469424 | solution.py:283
  3841.6 11.1 dynamic_update_slice.25
  3898.0 11.1 dynamic_update_slice.25
  4010.9 11.1 dynamic_update_slice.25
  4035.2 20.1 fusion.90
  4075.1 45.6 %all-reduce.14.cloned.1.call-done = (bf16[2048,1024]{1,0:T(8,128)(2,1)}, bf16[1024,32]{0,1:T(8,128)(2,1)}) async-done(((bf16[2048,1024]{1,0:T(8,128)(2,1)}, bf16[1024,32]{0,1:T(8,128)(2,1)}), (bf16[2048,1024]{1,0:T(8,128)(2,1)}, bf16[1024,32]{0,1:T(8,128)(2,1)})) %all-reduce.14.cloned.1.call-update) | async-done | bytes 4259856 | tf_op jit(solution)/shard_map/psum | solution.py:312
  4126.3 22.3 all-reduce.5
  4157.9 60.6 %all-reduce.12.cloned.1.call-done = (bf16[1024,256]{1,0:T(8,128)(2,1)}, bf16[1024,128]{1,0:T(8,128)(2,1)}, bf16[1024,128]{1,0:T(8,128)(2,1)}, bf16[256,1024]{1,0:T(8,128)(2,1)}, bf16[1024,32]{0,1:T(8,128)(2,1)}) async-done(((bf16[1024,256]{1,0:T(8,128)(2,1)}, bf16[1024,128]{1,0:T(8,128)(2,1)}, bf16[1024,128]{1,0:T(8,128)(2,1)}, bf16[256,1024]{1,0:T(8,128)(2,1)}, bf16[1024,32]{0,1:T(8,128)(2,1)}), ...) | async-done | bytes 1638416 | tf_op jit(solution)/shard_map/psum | solution.py:324
  (329 shorter events, 457.5 us)
Async XLA Ops:
  7.2 897.5 %copy-start = (bf16[4,128,1024]{2,1,0:T(8,128)(2,1)S(1)}, bf16[4,128,1024]{2,1,0:T(8,128)(2,1)}, u32[]{:S(2)}) copy-start(bf16[4,128,1024]{2,1,0:T(8,128)(2,1)} %param.34) | copy-start | bytes 3145732
  7.2 167.3 %reduce-scatter.8.cloned.1.call-start = ((), (), s32[]{:S(2)}) async-start(), calls=%async_computation.5 | async-start | bytes 10485760 | tf_op jit(solution)/shard_map/reduce_scatter | solution.py:113
  100.0 606.6 %all-gather.4.cloned.1.call-start = ((), (), s32[]{:S(2)}) async-start(), calls=%async_computation.6 | async-start | bytes 41943040 | tf_op jit(solution)/shard_map/all_gather | solution.py:150
  100.0 78.5 %copy-start.35 = (bf16[1024,32]{0,1:T(8,128)(2,1)S(1)}, bf16[1024,32]{0,1:T(8,128)(2,1)}, u32[]{:S(2)}) copy-start(bf16[1024,32]{0,1:T(8,128)(2,1)} %param.29) | copy-start | bytes 196612
  106.6 115.9 %copy-start.46 = (f32[1024]{0:T(1024)}, f32[1024]{0:T(1024)S(1)}, u32[]{:S(2)}) copy-start(f32[1024]{0:T(1024)S(1)} %convert_element_type.182) | copy-start | bytes 12292
  178.6 50.4 %copy-start.4 = (bf16[512,1024]{1,0:T(8,128)(2,1)}, bf16[512,1024]{1,0:T(8,128)(2,1)S(1)}, u32[]{:S(2)}) copy-start(bf16[512,1024]{1,0:T(8,128)(2,1)S(1)} %multiply_convert_fusion.1) | copy-start | bytes 3145732
  179.2 271.1 %copy-start.30 = (f32[512,8]{0,1:T(8,128)}, f32[512,8]{0,1:T(8,128)S(1)}, u32[]{:S(2)}) copy-start(f32[512,8]{0,1:T(8,128)S(1)} %get-tuple-element.339) | copy-start | bytes 49156
  179.8 42.7 %copy-start.38 = (s32[512,8]{0,1:T(8,128)}, s32[512,8]{0,1:T(8,128)S(1)}, u32[]{:S(2)}) copy-start(s32[512,8]{0,1:T(8,128)S(1)} %get-tuple-element.390) | copy-start | bytes 49156
  448.7 456.0 %all-gather.6.cloned.1.call-start = ((), (), s32[]{:S(2)}) async-start(), calls=%async_computation.7 | async-start | bytes 41943040 | tf_op jit(solution)/shard_map/all_gather | solution.py:185
  450.2 34.5 copy-start.2
  450.2 34.4 copy-start.42
  706.6 25.5 copy-start.22
  923.7 23.6 copy-start.17
  923.7 23.6 copy-start.15
  923.8 66.7 %copy-start.18 = (bf16[4,8,4,128,128]{4,3,1,0,2:T(8,128)(2,1)}, bf16[4,8,4,128,128]{4,3,1,0,2:T(8,128)(2,1)S(1)}, u32[]{:S(2)}) copy-start(bf16[4,8,4,128,128]{4,3,1,0,2:T(8,128)(2,1)S(1)} %get-tuple-element.399) | copy-start | bytes 12582916
  3282.8 189.2 %all-to-all-start.3 = ((bf16[8,512,1024]{2,1,0:T(8,128)(2,1)}), bf16[8,512,1024]{2,1,0:T(8,128)(2,1)}, u32[]{:S(2)}, u32[]{:S(2)}) async-start(bf16[8,512,1024]{2,1,0:T(8,128)(2,1)} %bitcast.359), calls=%async_computation.4 | async-start | bytes 16777216 | tf_op jit(solution)/shard_map/all_to_all | solution.py:219
  3472.1 187.8 %all-to-all-start.1 = ((bf16[8,512,1024]{2,1,0:T(8,128)(2,1)}), bf16[8,512,1024]{2,1,0:T(8,128)(2,1)}, u32[]{:S(2)}, u32[]{:S(2)}) async-start(bf16[8,512,1024]{2,1,0:T(8,128)(2,1)} %bitcast.358), calls=%async_computation.2 | async-start | bytes 16777216 | tf_op jit(solution)/shard_map/all_to_all | solution.py:167
  3477.2 310.5 %all-gather.8.cloned.1.call-start = ((), (), s32[]{:S(2)}) async-start(), calls=%async_computation.8 | async-start | bytes 5242880 | tf_op jit(solution)/shard_map/all_gather | solution.py:238
  3693.2 25.4 copy-start.3
  3718.6 22.1 copy-start.36
  3718.6 26.4 copy-start.24
  3749.4 371.4 %all-reduce.14.cloned.1.call-start = ((), (), s32[]{:S(2)}) async-start(), calls=%async_computation.10 | async-start | bytes 8519680 | tf_op jit(solution)/shard_map/psum | solution.py:312
  3767.0 19.5 copy-start.5
  3767.0 20.8 copy-start.32
  3953.9 11.7 copy-start.8
  4010.3 11.7 copy-start.8
  4035.1 20.2 copy-start.52
  4035.1 183.4 %all-reduce.12.cloned.1.call-start = ((), (), s32[]{:S(2)}) async-start(), calls=%async_computation.9 | async-start | bytes 3276800 | tf_op jit(solution)/shard_map/psum | solution.py:324
  4070.9 49.9 %copy-start.41 = (f32[2048]{0:T(1024)S(1)}, f32[2048]{0:T(1024)}, u32[]{:S(2)}) copy-start(f32[2048]{0:T(1024)} %copy-done.40) | copy-start | bytes 24580
  4070.9 49.9 %copy-start.45 = (f32[1024]{0:T(1024)S(1)}, f32[1024]{0:T(1024)}, u32[]{:S(2)}) copy-start(f32[1024]{0:T(1024)} %copy-done.44) | copy-start | bytes 12292
  4073.0 76.7 %copy-start.49 = (f32[2048]{0:T(1024)S(1)}, f32[2048]{0:T(1024)}, u32[]{:S(2)}) copy-start(f32[2048]{0:T(1024)} %get-tuple-element.410) | copy-start | bytes 24580
  4149.8 78.0 %copy-start.1 = (bf16[4,128,1024]{2,1,0:T(8,128)(2,1)S(1)}, bf16[4,128,1024]{2,1,0:T(8,128)(2,1)}, u32[]{:S(2)}) copy-start(bf16[4,128,1024]{2,1,0:T(8,128)(2,1)} %param.34) | copy-start | bytes 3145732
  (43 other events, 263.1 us)
Sparse Core Ops, SparseCore 0:
  100.0 74.3 reduce-scatter.7
  448.8 199.5 all-gather.3
  705.5 199.1 all-gather.5
  3749.5 33.2 all-gather.7
  4035.2 85.4 all-reduce.13
  4125.3 93.1 all-reduce.11
where the time goes:
time: 4240 us
  blocking collectives  2650 us (62%)
  waiting for transfers between devices  678 us (16%)
  matrix products  444 us (10%)
  local copies, waits for them, and re-layouts  221 us (5%)
  other arithmetic  211 us (5%)
    unnamed x1, blocking collectives  2250 us
    all_to_all x1, blocking collectives, per_device(): lax.all_to_all(outgoing, 'dp', split_axis=0, concat_axis=0, tiled=True)  188 us
    all_to_all x1, blocking collectives, per_device(): lax.all_to_all(back_rows.reshape(data_count, local_experts * capacity, mo...  187 us
    all_to_all x1, waiting for transfers between devices, per_device(): lax.all_to_all(return_rows, 'dp', split_axis=0, concat_axis=0, tiled=True)  175 us
    all_to_all x1, waiting for transfers between devices, per_device(): lax.all_to_all(back_out, 'dp', split_axis=0, concat_axis=0, tiled=True)  174 us
    all_gather x1, waiting for transfers between devices, per_device(): shard_part = lax.all_gather(back_in[None], 'tensor', axis=0, tiled=True)  155 us
  transfers between devices with their start and end apart: 8, of which 6 were waited for; matrix products, arithmetic and copies ran while one was open for 5% of the time, Pallas kernels for 0%

commit v1 on v0

v1 whole, which is shorter than its diff:
```python
import jax
import jax.numpy as jnp
from jax import lax
from jax.sharding import PartitionSpec as P

HD = 64
EXPERTS = 32
TOPK = 8


EPSILON = 1e-06
THETA_BASE = 10000.0
HIGHEST = lax.Precision.HIGHEST


def rope_tables(length, width_in):
    half_width = width_in // 2
    frequency = THETA_BASE ** (-(jnp.arange(half_width, dtype=jnp.float32) / half_width))
    angles = jnp.arange(length, dtype=jnp.float32)[:, None] * frequency[None, :]
    return (jnp.cos(angles), jnp.sin(angles))


def rotate(vectors, cosine, sine, direction):
    half_width = vectors.shape[-1] // 2
    front_half = vectors[..., :half_width]
    back_half = vectors[..., half_width:]
    cos_part = cosine[:, None, :]
    sin_part = sine[:, None, :] * direction
    return jnp.concatenate(
        [
            front_half * cos_part - back_half * sin_part,
            back_half * cos_part + front_half * sin_part,
        ],
        -1,
    )


def group_gather(x, axes):
    return lax.all_gather(x, axes, axis=0, tiled=False)


def per_device(
    tokens,
    prefix,
    gain_attn,
    w_query,
    w_key,
    w_value,
    w_out,
    gain_moe,
    w_router,
    routes,
    fill_order,
    w_gate,
    w_up,
    w_down,
    cotangent,
):
    f32 = jnp.float32
    bf16 = jnp.bfloat16
    z_count = lax.axis_size("z")
    y_count = lax.axis_size("y")
    shards = lax.axis_size("x") * lax.axis_size("c")
    z_rank = lax.axis_index("z")
    tensor_rank = lax.axis_index("x") * lax.axis_size("c") + lax.axis_index("c")
    length = tokens.shape[0]
    model_width = tokens.shape[1]
    own_rows = routes.shape[0]
    local_experts = w_gate.shape[0]
    group_experts = local_experts * y_count
    capacity = own_rows * TOPK // EXPERTS
    heads_local = w_query.shape[1] // HD
    kv_local = w_key.shape[1] // HD
    group_size = heads_local // kv_local
    block_rows = min(512, length)
    block_count = length // block_rows
    score_scale = HD ** (-0.5)
    hidden = w_gate.shape[2] * shards

    expert_ids = jnp.arange(EXPERTS, dtype=jnp.int32)
    member = jnp.sum((routes[:, :, None] == expert_ids[None, None, :]).astype(f32), 1)
    priority = fill_order[0]
    earlier = (priority[None, :] < priority[:, None]).astype(bf16)
    slot_full = jnp.dot(earlier, member.astype(bf16), preferred_element_type=f32)
    slot_code = jnp.where(member > 0, jnp.minimum(slot_full, float(capacity)), -1.0).astype(bf16)

    weights_gate = group_gather(w_gate, ("y", "x", "c")).reshape(
        y_count, shards, local_experts, model_width, -1
    )
    weights_up = group_gather(w_up, ("y", "x", "c")).reshape(
        y_count, shards, local_experts, model_width, -1
    )
    weights_down = group_gather(w_down, ("y", "x", "c")).reshape(
        y_count, shards, local_experts, -1, model_width
    )
    weights_gate = weights_gate.transpose(0, 2, 3, 1, 4).reshape(group_experts, model_width, hidden)
    weights_up = weights_up.transpose(0, 2, 3, 1, 4).reshape(group_experts, model_width, hidden)
    weights_down = weights_down.transpose(0, 2, 1, 3, 4).reshape(group_experts, hidden, model_width)
    cot_all = lax.all_gather(cotangent, "z", axis=0, tiled=False)
    code_all = lax.all_gather(slot_code, "z", axis=0, tiled=False)

    x_full = tokens.astype(f32)
    rms_one = lax.rsqrt(jnp.mean(x_full * x_full, -1, keepdims=True) + EPSILON)
    gain_one = gain_attn.astype(f32)
    normed_one = (x_full * rms_one * gain_one).astype(bf16)
    query_raw = jnp.dot(normed_one, w_query, preferred_element_type=f32)
    key_raw = jnp.dot(normed_one, w_key, preferred_element_type=f32)
    values = (
        jnp.dot(normed_one, w_value, preferred_element_type=f32)
        .astype(bf16)
        .reshape(length, kv_local, HD)
    )
    cosine, sine = rope_tables(length, HD)
    query_rot = rotate(query_raw.reshape(length, heads_local, HD), cosine, sine, 1.0).astype(bf16)
    key_rot = rotate(key_raw.reshape(length, kv_local, HD), cosine, sine, 1.0).astype(bf16)
    query_blocks = query_rot.reshape(block_count, block_rows, kv_local, group_size, HD)
    block_starts = jnp.arange(block_count, dtype=jnp.int32) * block_rows
    positions = jnp.arange(length, dtype=jnp.int32)
    prefix_len = prefix[0]

    def block_scores(query_block, offset):
        query_pos = offset + jnp.arange(block_rows, dtype=jnp.int32)
        raw_scores = (
            jnp.einsum("igjd,kgd->gjik", query_block, key_rot, preferred_element_type=jnp.float32)
            * score_scale
        )
        visible = (positions[None, :] <= query_pos[:, None]) | (positions[None, :] < prefix_len)
        return jnp.where(visible[None, None], raw_scores, -1e30)

    def attend_block(inputs):
        query_block, offset = inputs
        scores = block_scores(query_block, offset)
        row_peak = jnp.max(scores, -1, keepdims=True)
        weights = jnp.exp(scores - row_peak)
        row_total = jnp.sum(weights, -1, keepdims=True)
        probabilities = (weights / row_total).astype(jnp.bfloat16)
        attended = jnp.einsum(
            "gjik,kgd->igjd", probabilities, values, preferred_element_type=jnp.float32
        )
        return (attended.astype(jnp.bfloat16), (row_peak + jnp.log(row_total))[..., 0])

    attended_blocks, log_totals = lax.map(attend_block, (query_blocks, block_starts))
    attended_all = attended_blocks.reshape(length, heads_local * HD)
    attention_rows = lax.psum_scatter(
        jnp.dot(attended_all, w_out, preferred_element_type=f32).astype(bf16),
        ("x", "c"),
        scatter_dimension=0,
        tiled=True,
    ).astype(f32)
    x_rows = lax.dynamic_slice_in_dim(tokens, tensor_rank * own_rows, own_rows, 0).astype(f32)
    hidden_in = x_rows + attention_rows
    rms_two = lax.rsqrt(jnp.mean(hidden_in * hidden_in, -1, keepdims=True) + EPSILON)
    gain_two = gain_moe.astype(f32)
    normed_two = (hidden_in * rms_two * gain_two).astype(bf16)
    normed_all = lax.all_gather(normed_two, "z", axis=0, tiled=False)

    def gates(rows, code):
        logits = jnp.dot(rows, w_router, preferred_element_type=f32)
        chosen = jnp.where(code >= 0, logits, -jnp.inf)
        raised = jnp.exp(chosen - jnp.max(chosen, -1, keepdims=True))
        return raised / jnp.sum(raised, -1, keepdims=True)

    gate_own = gates(normed_two, slot_code)
    first = z_rank * group_experts
    gate_all = jax.vmap(gates)(normed_all, code_all)
    gate_group = lax.dynamic_slice_in_dim(gate_all, first, group_experts, 2)
    code_group = lax.dynamic_slice_in_dim(code_all, first, group_experts, 2).astype(jnp.int32)
    slot_ids = jnp.arange(capacity, dtype=jnp.int32)
    hot = code_group.transpose(2, 0, 1)[:, :, None, :] == slot_ids[None, None, :, None]
    pick = hot.astype(bf16)
    pick_gate = jnp.where(hot, gate_group.transpose(2, 0, 1)[:, :, None, :], 0.0)
    gate_slot = jnp.sum(pick_gate, -1)
    rows_in = jnp.einsum("esci,sid->escd", pick, normed_all, preferred_element_type=f32).astype(bf16)
    rows_dy = jnp.einsum("esci,sid->escd", pick, cot_all, preferred_element_type=f32)
    gate_pre = jnp.einsum("escd,edf->escf", rows_in, weights_gate, preferred_element_type=f32)
    up_pre = jnp.einsum("escd,edf->escf", rows_in, weights_up, preferred_element_type=f32)
    activated = (gate_pre / (1.0 + jnp.exp(-gate_pre)) * up_pre).astype(bf16)
    expert_out = jnp.einsum(
        "escf,efd->escd", activated, weights_down, preferred_element_type=f32
    ).astype(bf16)
    out_grad_rows = (rows_dy * gate_slot[..., None]).astype(bf16)
    gate_grad_slot = jnp.sum(rows_dy * expert_out.astype(f32), -1)
    gate_grad = jnp.einsum("esci,esc->sie", pick.astype(f32), gate_grad_slot, precision=HIGHEST)
    moe_part = jnp.einsum(
        "esci,escd->sid", pick_gate.astype(bf16), expert_out, preferred_element_type=f32
    ).astype(bf16)
    hid_grad = jnp.einsum("escd,efd->escf", out_grad_rows, weights_down, preferred_element_type=f32)
    sigmoid_g = 1.0 / (1.0 + jnp.exp(-gate_pre))
    back_gate = (hid_grad * up_pre * sigmoid_g * (1.0 + gate_pre * (1.0 - sigmoid_g))).astype(bf16)
    back_up = (hid_grad * gate_pre * sigmoid_g).astype(bf16)
    rows_grad = (
        jnp.einsum("escf,edf->escd", back_gate, weights_gate, preferred_element_type=f32)
        + jnp.einsum("escf,edf->escd", back_up, weights_up, preferred_element_type=f32)
    ).astype(bf16)
    rows_part = jnp.einsum("esci,escd->sid", pick, rows_grad, preferred_element_type=f32).astype(bf16)
    down_part = jnp.einsum("escf,escd->efd", activated, out_grad_rows, preferred_element_type=f32)
    gate_part = jnp.einsum("escd,escf->edf", rows_in, back_gate, preferred_element_type=f32)
    up_part = jnp.einsum("escd,escf->edf", rows_in, back_up, preferred_element_type=f32)

    gate_grad_wide = lax.dynamic_update_slice_in_dim(
        jnp.zeros((z_count, own_rows, EXPERTS), f32), gate_grad, first, 2
    )
    back_pack = jnp.concatenate([rows_part, gate_grad_wide.astype(bf16)], -1)
    back_own = lax.psum_scatter(back_pack, "z", scatter_dimension=0, tiled=False).astype(f32)
    moe_own = lax.psum_scatter(moe_part, "z", scatter_dimension=0, tiled=False).astype(f32)
    block_output = (hidden_in + moe_own).astype(bf16)

    def shard_sum(part, dim):
        width = part.shape[dim] // shards
        split = part.reshape((y_count, local_experts) + part.shape[1:dim] + (shards, width) + part.shape[dim + 1 :])
        split = jnp.moveaxis(split, dim + 1, 1).astype(bf16)
        split = split.reshape((y_count * shards,) + split.shape[2:])
        return lax.psum_scatter(split, ("y", "x", "c"), scatter_dimension=0, tiled=False).astype(f32)

    grad_gate = shard_sum(gate_part, 2)
    grad_up = shard_sum(up_part, 2)
    grad_down = shard_sum(down_part, 1)

    normed_two_grad = back_own[:, :model_width]
    gate_grad_own = back_own[:, model_width:]
    logit_grad = gate_own * (
        gate_grad_own - jnp.sum(gate_own * gate_grad_own, -1, keepdims=True)
    )
    router_part = jnp.dot(normed_two.astype(f32).T, logit_grad, precision=HIGHEST)
    normed_two_grad = normed_two_grad + jnp.dot(
        logit_grad, w_router.astype(f32).T, precision=HIGHEST
    )
    gain_two_part = jnp.sum(normed_two_grad * hidden_in * rms_two, 0)
    scaled_two = normed_two_grad * gain_two
    grad_rows = cotangent.astype(f32)
    hidden_grad = (
        grad_rows
        + rms_two * scaled_two
        - hidden_in * rms_two**3 * jnp.mean(scaled_two * hidden_in, -1, keepdims=True)
    )
    shard_part = lax.all_gather(
        hidden_grad.astype(bf16), ("x", "c"), axis=0, tiled=True
    ).astype(f32)
    attended_part = jnp.einsum(
        "id,hd->ih", shard_part.astype(jnp.bfloat16), w_out, preferred_element_type=jnp.float32
    )
    attended_grad = attended_part.astype(jnp.bfloat16)
    out_grad = jnp.einsum(
        "ih,id->hd",
        attended_all,
        shard_part.astype(jnp.bfloat16),
        preferred_element_type=jnp.float32,
    )
    grad_blocks = attended_grad.reshape(block_count, block_rows, kv_local, group_size, HD)

    def back_block(running, inputs):
        key_acc, value_acc = running
        query_block, grad_block, log_block, offset = inputs
        scores = block_scores(query_block, offset)
        probabilities = jnp.exp(scores - log_block[..., None])
        prob_grad = jnp.einsum(
            "igjd,kgd->gjik", grad_block, values, preferred_element_type=jnp.float32
        )
        center = jnp.sum(prob_grad * probabilities, -1, keepdims=True)
        score_grad = (probabilities * (prob_grad - center)).astype(jnp.bfloat16)
        query_grad = (
            jnp.einsum("gjik,kgd->igjd", score_grad, key_rot, preferred_element_type=jnp.float32)
            * score_scale
        )
        key_acc = (
            key_acc
            + jnp.einsum(
                "gjik,igjd->kgd", score_grad, query_block, preferred_element_type=jnp.float32
            )
            * score_scale
        )
        value_acc = value_acc + jnp.einsum(
            "gjik,igjd->kgd",
            probabilities.astype(jnp.bfloat16),
            grad_block,
            preferred_element_type=jnp.float32,
        )
        return ((key_acc, value_acc), query_grad)

    zero_kv = jnp.zeros((length, kv_local, HD), jnp.float32)
    (key_grad, value_grad), query_grads = lax.scan(
        back_block, (zero_kv, zero_kv), (query_blocks, grad_blocks, log_totals, block_starts)
    )
    query_back = (
        rotate(query_grads.reshape(length, heads_local, HD), cosine, sine, -1.0)
        .reshape(length, heads_local * HD)
        .astype(jnp.bfloat16)
    )
    key_back = (
        rotate(key_grad, cosine, sine, -1.0).reshape(length, kv_local * HD).astype(jnp.bfloat16)
    )
    value_back = value_grad.reshape(length, kv_local * HD).astype(jnp.bfloat16)
    query_weight = jnp.einsum(
        "id,ih->dh", normed_one, query_back, preferred_element_type=jnp.float32
    )
    key_weight = jnp.einsum("id,ih->dh", normed_one, key_back, preferred_element_type=jnp.float32)
    value_weight = jnp.einsum(
        "id,ih->dh", normed_one, value_back, preferred_element_type=jnp.float32
    )
    normed_one_grad = jnp.einsum(
        "ih,dh->id", query_back, w_query, preferred_element_type=jnp.float32
    )
    normed_one_grad = normed_one_grad + jnp.einsum(
        "ih,dh->id", key_back, w_key, preferred_element_type=jnp.float32
    )
    normed_one_grad = normed_one_grad + jnp.einsum(
        "ih,dh->id", value_back, w_value, preferred_element_type=jnp.float32
    )
    total_one = lax.psum(normed_one_grad.astype(bf16), ("x", "c")).astype(f32)
    gain_one_part = jnp.sum(normed_one_grad * x_full * rms_one, 0)
    scaled_one = total_one * gain_one
    input_grad = (
        shard_part
        + rms_one * scaled_one
        - x_full * rms_one**3 * jnp.mean(scaled_one * x_full, -1, keepdims=True)
    )
    dp = ("z", "y")
    everyone = ("z", "y", "x", "c")
    summed = [
        lax.psum(part.astype(bf16), dp).astype(f32)
        for part in (query_weight, key_weight, value_weight, out_grad)
    ]
    router_total, gain_one_total, gain_two_total = (
        lax.psum(part.astype(bf16), everyone).astype(f32)
        for part in (router_part, gain_one_part, gain_two_part)
    )
    return (
        block_output,
        input_grad,
        gain_one_total,
        summed[0],
        summed[1],
        summed[2],
        summed[3],
        gain_two_total,
        router_total,
        grad_gate,
        grad_up,
        grad_down,
    )


def solution(mesh):
    dp_count, tensor_count = mesh.devices.shape
    mesh = jax.sharding.Mesh(
        mesh.devices.reshape(dp_count // 2, 2, tensor_count // 2, 2), ("z", "y", "x", "c")
    )
    dp = ("z", "y")
    tensor = ("x", "c")
    both = dp + tensor
    return jax.shard_map(
        per_device,
        mesh=mesh,
        in_specs=(
            P(dp, None),
            P(dp),
            P(),
            P(None, tensor),
            P(None, tensor),
            P(None, tensor),
            P(tensor, None),
            P(),
            P(),
            P(both, None),
            P(both, None),
            P(dp, None, tensor),
            P(dp, None, tensor),
            P(dp, tensor, None),
            P(both, None),
        ),
        out_specs=(
            P(both, None),
            P(dp, None),
            P(),
            P(None, tensor),
            P(None, tensor),
            P(None, tensor),
            P(tensor, None),
            P(),
            P(),
            P(dp, None, tensor),
            P(dp, None, tensor),
            P(dp, tensor, None),
        ),
        check_vma=False,
    )
```

time: 4240 us -> 1340 us (0.32)
  blocking collectives: 2650 us -> 62.1 us
  waiting for transfers between devices: 678 us -> 509 us
  local copies, waits for them, and re-layouts: 221 us -> 170 us
  other arithmetic: 211 us -> 162 us
    unnamed x1 -> x0, blocking collectives: 2250 us -> none
    all_to_all x2 -> x0, blocking collectives: 375 us -> none  [the longest x1 188 us: per_device(): lax.all_to_all(outgoing, 'dp', split_axis=0, concat_axis=0, tiled=True)]
    all_to_all x2 -> x0, waiting for transfers between devices: 350 us -> none  [the longest x1 175 us: per_device(): lax.all_to_all(return_rows, 'dp', split_axis=0, concat_axis=0, tiled=True)]
    reduce_scatter x1 -> x6, waiting for transfers between devices: 67.1 us -> 194 us  [the longest x1 75.9 us: per_device(): lax.psum_scatter(back_pack, 'z', scatter_dimension=0, tiled=False)]
    gather x4 -> x0, local copies, waits for them, and re-layouts: 87.8 us -> none  [the longest x1 25.7 us: per_device(): jnp.take(jnp.concatenate([came_back, zero_row], 0), flat_slot, 0)]
    dot_general x19 -> x23, matrix products: 265 us -> 195 us  [the longest x1 22.9 us: per_device(): jnp.einsum('escd,efd->escf', out_grad_rows, weights_down, preferred_eleme...]
    reshape x0 -> x5, local copies, waits for them, and re-layouts: none -> 58.7 us  [the longest x1 13.1 us: per_device(): weights_gate.transpose(0, 2, 3, 1, 4)]
    reduce_sum x8 -> x6, other arithmetic: 68.7 us -> 13.8 us  [the longest x1 7.48 us: per_device(): gain_one_part = jnp.sum(normed_one_grad * x_full * rms_one, 0)]
  transfers between devices with their start and end apart: 8 -> 15, of which waited for: 6 -> 9; matrix products, arithmetic and copies ran while one was open for 5% -> 40% of each run, Pallas kernels for 0% -> 0%
where the time goes in v1:
time: 1340 us; the launch traced here: 1330 us
  waiting for transfers between devices  509 us (38%)
  matrix products  407 us (30%)
  local copies, waits for them, and re-layouts  170 us (13%)
  other arithmetic  162 us (12%)
  blocking collectives  62.1 us (5%)
  between operations  16.3 us (1%)
    psum x1, waiting for transfers between devices, per_device(): total_one = lax.psum(normed_one_grad.astype(bf16), ('x', 'c')).astype(f32)  79.4 us
    all_gather x3, waiting for transfers between devices, group_gather(): return lax.all_gather(x, axes, axis=0, tiled=False)  76.5 us
    reduce_scatter x1, waiting for transfers between devices, per_device(): lax.psum_scatter(back_pack, 'z', scatter_dimension=0, tiled=False)  75.9 us
    psum x1, waiting for transfers between devices, per_device(): lax.psum(part.astype(bf16), dp).astype(f32)  72.1 us
    reduce_scatter x1, waiting for transfers between devices, per_device(): lax.psum_scatter(moe_part, 'z', scatter_dimension=0, tiled=False)  71.9 us
    all_gather x1, waiting for transfers between devices, per_device(): normed_all = lax.all_gather(normed_two, 'z', axis=0, tiled=False)  70 us
    dynamic_update_slice x8, local copies, waits for them, and re-layouts, per_device(): lax.scan(back_block, (zero_kv, zero_kv), (query_blocks, grad_blocks, log_...  50 us
    dot_general x4, matrix products, back_block(): jnp.einsum('gjik,igjd->kgd', probabilities.astype(jnp.bfloat16), grad_blo...  48 us
  transfers between devices with their start and end apart: 15, of which 9 were waited for; matrix products, arithmetic and copies ran while one was open for 40% of the time, Pallas kernels for 0%

profile of v1, /device:TPU:0, one launch (start us, length us, event | category | flops | bytes accessed | tf_op | source)
XLA Modules:
  0.0 1328.7 jit_solution(10371422543559029803)
XLA Ops:
  26.0 65.3 %while.30 = (s32[]{:T(128)}, bf16[4,512,2,2,64]{1,4,3,2,0:T(8,128)(2,1)}, f32[4,2,2,512]{3,2,1,0:T(2,128)}, s32[4]{0:T(128)S(1)}, s32[]{:T(128)}, /*index=5*/bf1...) while((s32[]{:T(128)}, ...), condition=%wide.region_4.5_spmd.clone.clone, body=%wide.region_1.4_spmd.clone.clone.sunk | while | flops 1126302208 | bytes 56173684 | solution.py:142
  99.4 46.7 %reduce-scatter.7.cloned.1.call-done = bf16[512,1024]{1,0:T(8,128)(2,1)} async-done(((bf16[2048,1024]{1,0:T(8,128)(2,1)}), bf16[512,1024]{1,0:T(8,128)(2,1)}) %reduce-scatter.7.cloned.1.call-update) | async-done | bytes 1048592 | tf_op jit(solution)/shard_map/reduce_scatter | solution.py:144
  154.9 22.5 %all-gather = bf16[2048,32]{1,0:T(8,128)(2,1)S(1)} all-gather(bf16[512,32]{1,0:T(8,128)(2,1)S(1)} %fusion.104), channel_id=2, replica_groups=mesh['z'=4,'y'=2,'x'=2,'c'=2] {'z'}, dimensions={0}, use_global_device_ids=true | all-gather | bytes 163840 | tf_op jit(solution)/shard_map/all_gather | solution.py:100
  178.2 14.4 %all-gather.23.cloned.1.call-done = bf16[2048,1024]{1,0:T(8,128)(2,1)} async-done(((bf16[512,1024]{1,0:T(8,128)(2,1)}), bf16[2048,1024]{1,0:T(8,128)(2,1)}) %all-gather.23.cloned.1.call-update) | async-done | bytes 4194320 | tf_op jit(solution)/shard_map/all_gather | solution.py:99
  203.8 70.0 %all-gather.15.cloned.1.call-done = bf16[2048,1024]{1,0:T(8,128)(2,1)} async-done(((bf16[512,1024]{1,0:T(8,128)(2,1)}), bf16[2048,1024]{1,0:T(8,128)(2,1)}) %all-gather.15.cloned.1.call-update) | async-done | bytes 4194320 | tf_op jit(solution)/shard_map/all_gather | solution.py:155
  283.1 45.4 %all-gather.19.cloned.1.call-done = bf16[32,1024,128]{2,1,0:T(8,128)(2,1)} async-done(((bf16[4,1024,128]{2,1,0:T(8,128)(2,1)}), bf16[32,1024,128]{2,1,0:T(8,128)(2,1)}) %all-gather.19.cloned.1.call-update) | async-done | bytes 8388624 | tf_op jit(solution)/shard_map/all_gather | solution.py:39
  328.6 12.2 copy.224
  340.7 13.1 reshape.367
  353.8 31.1 %all-gather.17.cloned.1.call-done = bf16[32,1024,128]{2,1,0:T(8,128)(2,1)} async-done(((bf16[4,1024,128]{2,1,0:T(8,128)(2,1)}), bf16[32,1024,128]{2,1,0:T(8,128)(2,1)}) %all-gather.17.cloned.1.call-update) | async-done | bytes 8388624 | tf_op jit(solution)/shard_map/all_gather | solution.py:39
  384.9 12.2 copy.225
  397.0 13.1 reshape.366
  419.6 13.8 %fusion.68 = f32[8,4,128,512]{3,2,1,0:T(8,128)} fusion(bf16[8,1024,512,1]{2,1,0,3:T(8,128)(2,1)} %reshape.367, bf16[8,4,128,1024]{2,3,0,1:T(8,128)(2,1)} %convert_bitcast_fusion), kind=kOutput, calls=%fused_computation.93 | convolution fusion | flops 4294967296 | bytes 25165824 | tf_op jit(solution)/shard_map/escd,edf->escf/dot_general | solution.py:176
  433.4 13.8 %fusion.70 = f32[8,4,128,512]{3,2,1,0:T(8,128)} fusion(bf16[8,1024,512,1]{2,1,0,3:T(8,128)(2,1)} %reshape.366, bf16[8,4,128,1024]{2,3,0,1:T(8,128)(2,1)} %convert_bitcast_fusion), kind=kOutput, calls=%fused_computation.95 | convolution fusion | flops 4294967296 | bytes 25165824 | tf_op jit(solution)/shard_map/escd,edf->escf/dot_general | solution.py:175
  455.4 22.9 %multiply_convert_fusion = (bf16[8,4,128,512]{3,2,1,0:T(8,128)(2,1)}, bf16[8,4,128,512]{3,2,1,0:T(8,128)(2,1)}, bf16[8,4,128,512]{3,2,1,0:T(8,128)(2,1)}) fusion(f32[8,4,128,512]{3,2,1,0:T(8,128)} %fusion.70, f32[8,4,128,512]{3,2,1,0:T(8,128)} %fusion.68, bf16[8,512,1024,1]{2,1,3,0:T(8,128)(2,1)} %bitcast.347, f32[4,8,128,1024]{3,2,0,1:T(8,128)} %fusion.77, ...), kind=kOutput, calls=%fused_computation.103 | convolution fusion | flops 4336910336 | bytes 54542336 | tf_op jit(solution)/shard_map/escd,efd->escf/dot_general | solution.py:187
  478.3 15.1 %fusion.93 = f32[8,4,128,1024]{3,2,0,1:T(8,128)} fusion(bf16[8,1024,512,1]{2,1,0,3:T(8,128)(2,1)} %reshape.366, bf16[8,4,128,512]{3,2,1,0:T(8,128)(2,1)} %get-tuple-element.364), kind=kOutput, calls=%fused_computation.129 | convolution fusion | flops 4294967296 | bytes 29360128 | tf_op jit(solution)/shard_map/escf,edf->escd/dot_general | solution.py:192
  493.4 14.3 %add_convert_fusion.11 = bf16[8,4,128,1024]{3,2,0,1:T(8,128)(2,1)} fusion(f32[8,4,128,1024]{3,2,0,1:T(8,128)} %fusion.93, bf16[8,1024,512,1]{2,1,0,3:T(8,128)(2,1)} %reshape.367, bf16[8,4,128,512]{3,2,1,0:T(8,128)(2,1)} %get-tuple-element.363), kind=kOutput, calls=%fused_computation.74.clone.clone.clone.clone.2 | convolution fusion | flops 4303355904 | bytes 37748736 | tf_op jit(solution)/shard_map/escf,edf->escd/dot_general | solution.py:193
  516.4 12.7 fusion.58
  553.5 75.9 %reduce-scatter.11.cloned.1.call-done = bf16[1,512,1056]{2,1,0:T(8,128)(2,1)} async-done(((bf16[4,512,1056]{2,1,0:T(8,128)(2,1)}), bf16[1,512,1056]{2,1,0:T(8,128)(2,1)}) %reduce-scatter.11.cloned.1.call-update) | async-done | bytes 1081360 | tf_op jit(solution)/shard_map/reduce_scatter | solution.py:204
  637.0 71.9 %reduce-scatter.9.cloned.1.call-done = bf16[1,512,1024]{2,1,0:T(8,128)(2,1)} async-done(((bf16[4,512,1024]{2,1,0:T(8,128)(2,1)}), bf16[1,512,1024]{2,1,0:T(8,128)(2,1)}) %reduce-scatter.9.cloned.1.call-update) | async-done | bytes 1048592 | tf_op jit(solution)/shard_map/reduce_scatter | solution.py:205
  716.3 13.1 bitcast_convert_fusion
  748.6 12.0 copy.141
  771.7 11.9 copy.138
  797.4 274.2 %while.31 = (s32[]{:T(128)}, f32[2048,2,64]{0,2,1:T(8,128)}, f32[2048,2,64]{0,2,1:T(8,128)}, f32[4,512,2,2,64]{1,0,4,3,2:T(4,128)}, bf16[4,512,2,2,64]{1,4,3,2,0...) while((s32[]{:T(128)}, f32[2048,2,64]{0,2,1:T(8,128)}, ...), condition=%wide.region_20.21_spmd.clone.clone, body=%wide.region_18.20_spmd.clone.clone.sunk | while | flops 2750808576 | bytes 219220240 | solution.py:281
  806.3 11.9 fusion.210
  818.2 12.6 fusion.211
  924.3 12.4 fusion.213
  945.4 12.1 fusion.210
  992.3 11.9 fusion.213
  1059.3 11.9 fusion.213
  1105.9 72.1 %all-reduce.10.cloned.1.call-done = (bf16[1024,256]{1,0:T(8,128)(2,1)}, bf16[1024,128]{1,0:T(8,128)(2,1)}, bf16[1024,128]{1,0:T(8,128)(2,1)}, bf16[256,1024]{1,0:T(8,128)(2,1)}) async-done(((bf16[1024,256]{1,0:T(8,128)(2,1)}, bf16[1024,128]{1,0:T(8,128)(2,1)}, bf16[1024,128]{1,0:T(8,128)(2,1)}, bf16[256,1024]{1,0:T(8,128)(2,1)}), (bf16[1024,256]{1,0:T(8,128)(2,1)}, bf16[1024,128]{1,0:T(8,128)(2,1)}, ...) | async-done | bytes 1572880 | tf_op jit(solution)/shard_map/psum | solution.py:320
  1185.8 79.4 %all-reduce.6.cloned.1.call-done = bf16[2048,1024]{1,0:T(8,128)(2,1)} async-done(((bf16[2048,1024]{1,0:T(8,128)(2,1)}), bf16[2048,1024]{1,0:T(8,128)(2,1)}) %all-reduce.6.cloned.1.call-update) | async-done | bytes 4194320 | tf_op jit(solution)/shard_map/psum | solution.py:309
  1272.7 39.6 %all-reduce = (bf16[1024]{0:T(1024)(128)(2,1)S(1)}, bf16[1024]{0:T(1024)(128)(2,1)S(1)}) all-reduce(bf16[1024]{0:T(1024)(128)(2,1)S(1)} %get-tuple-element.311, bf16[1024]{0:T(1024)(128)(2,1)S(1)} %copy-done.43), channel_id=1, replica_groups=mesh['z'=4,'y'=2,'x'=2,'c'=2] {'z','y','x','c'}, use_global_device_ids=true, to_apply=%region_24.25 | all-reduce | flops 2048 | bytes 8192 | tf_op jit(solution)/shard_map/psum | solution.py:324
  (322 shorter events, 489.5 us)
Async XLA Ops:
  8.0 138.1 %reduce-scatter.7.cloned.1.call-start = ((), (), s32[]{:S(2)}) async-start(), calls=%async_computation.6 | async-start | bytes 5242880 | tf_op jit(solution)/shard_map/reduce_scatter | solution.py:144
  26.0 69.4 %copy-start.26 = (bf16[256,1024]{1,0:T(8,128)(2,1)S(1)}, bf16[256,1024]{1,0:T(8,128)(2,1)}, u32[]{:S(2)}) copy-start(bf16[256,1024]{1,0:T(8,128)(2,1)} %param.25) | copy-start | bytes 1572868
  98.7 55.6 %copy-start.40 = (s32[512,8]{0,1:T(8,128)S(1)}, s32[512,8]{0,1:T(8,128)}, u32[]{:S(2)}) copy-start(s32[512,8]{0,1:T(8,128)} %param.28) | copy-start | bytes 49156
  98.7 55.8 %copy-start.44 = (s32[1,512]{1,0:T(1,128)S(1)}, s32[1,512]{1,0:T(1,128)}, u32[]{:S(2)}) copy-start(s32[1,512]{1,0:T(1,128)} %param.29) | copy-start | bytes 6148
  98.8 93.7 %all-gather.23.cloned.1.call-start = ((), (), s32[]{:S(2)}) async-start(), calls=%async_computation.19 | async-start | bytes 5242880 | tf_op jit(solution)/shard_map/all_gather | solution.py:99
  99.3 174.4 %all-gather.15.cloned.1.call-start = ((), (), s32[]{:S(2)}) async-start(), calls=%async_computation.15 | async-start | bytes 5242880 | tf_op jit(solution)/shard_map/all_gather | solution.py:155
  99.4 54.9 %copy-start.35 = (f32[1024]{0:T(1024)}, f32[1024]{0:T(1024)S(1)}, u32[]{:S(2)}) copy-start(f32[1024]{0:T(1024)S(1)} %convert_element_type.245) | copy-start | bytes 12292
  152.2 176.4 %all-gather.19.cloned.1.call-start = ((), (), s32[]{:S(2)}) async-start(), calls=%async_computation.17 | async-start | bytes 9437184 | tf_op jit(solution)/shard_map/all_gather | solution.py:39
  152.8 232.1 %all-gather.17.cloned.1.call-start = ((), (), s32[]{:S(2)}) async-start(), calls=%async_computation.16 | async-start | bytes 9437184 | tf_op jit(solution)/shard_map/all_gather | solution.py:39
  153.5 293.7 %all-gather.21.cloned.1.call-start = ((), (), s32[]{:S(2)}) async-start(), calls=%async_computation.18 | async-start | bytes 9437184 | tf_op jit(solution)/shard_map/all_gather | solution.py:39
  154.3 475.0 %reduce-scatter.11.cloned.1.call-start = ((), (), s32[]{:S(2)}) async-start(), calls=%async_computation.8 | async-start | bytes 5898240 | tf_op jit(solution)/shard_map/reduce_scatter | solution.py:204
  154.9 22.5 %copy-start.30 = (bf16[512,32]{1,0:T(8,128)(2,1)}, bf16[512,32]{1,0:T(8,128)(2,1)S(1)}, u32[]{:S(2)}) copy-start(bf16[512,32]{1,0:T(8,128)(2,1)S(1)} %fusion.104) | copy-start | bytes 98308
  192.5 81.3 %copy-start.32 = (bf16[1024,32]{0,1:T(8,128)(2,1)S(1)}, bf16[1024,32]{0,1:T(8,128)(2,1)}, u32[]{:S(2)}) copy-start(bf16[1024,32]{0,1:T(8,128)(2,1)} %param.27) | copy-start | bytes 196612
  542.3 166.6 %reduce-scatter.9.cloned.1.call-start = ((), (), s32[]{:S(2)}) async-start(), calls=%async_computation.7 | async-start | bytes 5242880 | tf_op jit(solution)/shard_map/reduce_scatter | solution.py:205
  552.6 79.6 %copy-start.12 = (bf16[512,1024]{1,0:T(8,128)(2,1)S(1)}, bf16[512,1024]{1,0:T(8,128)(2,1)}, u32[]{:S(2)}) copy-start(bf16[512,1024]{1,0:T(8,128)(2,1)} %reduce-scatter.7.cloned.1.call-done) | copy-start | bytes 3145732
  552.6 79.6 %copy-start.36 = (f32[1024]{0:T(1024)S(1)}, f32[1024]{0:T(1024)}, u32[]{:S(2)}) copy-start(f32[1024]{0:T(1024)} %copy-done.35) | copy-start | bytes 12292
  552.6 79.6 %copy-start.39 = (f32[512]{0:T(512)S(1)}, f32[512]{0:T(512)}, u32[]{:S(2)}) copy-start(f32[512]{0:T(512)} %copy-done.38) | copy-start | bytes 6148
  552.6 156.3 %copy-start.41 = (f32[512]{0:T(512)S(1)}, f32[512]{0:T(512)}, u32[]{:S(2)}) copy-start(f32[512]{0:T(512)} %get-tuple-element.378) | copy-start | bytes 6148
  552.6 231.0 %all-gather.13.cloned.1.call-start = ((), (), s32[]{:S(2)}) async-start(), calls=%async_computation.9 | async-start | bytes 5242880 | tf_op jit(solution)/shard_map/all_gather | solution.py:236
  713.6 382.6 %all-reduce.8.cloned.1.call-start = ((), (), s32[]{:S(2)}) async-start(), calls=%async_computation.11 | async-start | bytes 131072 | tf_op jit(solution)/shard_map/psum | solution.py:324
  716.2 381.5 %reduce-scatter.17.cloned.1.call-start = ((), (), s32[]{:S(2)}) async-start(), calls=%async_computation.14 | async-start | bytes 9437184 | tf_op jit(solution)/shard_map/reduce_scatter | solution.py:213
  737.7 362.8 %reduce-scatter.15.cloned.1.call-start = ((), (), s32[]{:S(2)}) async-start(), calls=%async_computation.13 | async-start | bytes 9437184 | tf_op jit(solution)/shard_map/reduce_scatter | solution.py:213
  760.6 342.6 %reduce-scatter.13.cloned.1.call-start = ((), (), s32[]{:S(2)}) async-start(), calls=%async_computation.12 | async-start | bytes 9437184 | tf_op jit(solution)/shard_map/reduce_scatter | solution.py:213
  783.6 394.4 %all-reduce.10.cloned.1.call-start = ((), (), s32[]{:S(2)}) async-start(), calls=%async_computation.20 | async-start | bytes 3145728 | tf_op jit(solution)/shard_map/psum | solution.py:320
  830.8 18.7 %copy-start.3 = (f32[2048,2,64]{0,2,1:T(8,128)S(1)}, f32[2048,2,64]{0,2,1:T(8,128)}, u32[]{:S(2)}) copy-start(f32[2048,2,64]{0,2,1:T(8,128)} %get-tuple-element.557) | copy-start | bytes 3145732 | tf_op jit(solution)/shard_map/while
  898.7 20.1 %copy-start.3 = (f32[2048,2,64]{0,2,1:T(8,128)S(1)}, f32[2048,2,64]{0,2,1:T(8,128)}, u32[]{:S(2)}) copy-start(f32[2048,2,64]{0,2,1:T(8,128)} %get-tuple-element.557) | copy-start | bytes 3145732 | tf_op jit(solution)/shard_map/while
  968.5 18.6 %copy-start.3 = (f32[2048,2,64]{0,2,1:T(8,128)S(1)}, f32[2048,2,64]{0,2,1:T(8,128)}, u32[]{:S(2)}) copy-start(f32[2048,2,64]{0,2,1:T(8,128)} %get-tuple-element.557) | copy-start | bytes 3145732 | tf_op jit(solution)/shard_map/while
  1035.5 18.6 %copy-start.3 = (f32[2048,2,64]{0,2,1:T(8,128)S(1)}, f32[2048,2,64]{0,2,1:T(8,128)}, u32[]{:S(2)}) copy-start(f32[2048,2,64]{0,2,1:T(8,128)} %get-tuple-element.557) | copy-start | bytes 3145732 | tf_op jit(solution)/shard_map/while
  1087.4 177.8 %all-reduce.6.cloned.1.call-start = ((), (), s32[]{:S(2)}) async-start(), calls=%async_computation.10 | async-start | bytes 8388608 | tf_op jit(solution)/shard_map/psum | solution.py:309
  1096.2 169.0 %copy-start.29 = (f32[2048]{0:T(1024)S(1)}, f32[2048]{0:T(1024)}, u32[]{:S(2)}) copy-start(f32[2048]{0:T(1024)} %copy-done.28) | copy-start | bytes 24580
  1096.2 169.0 %copy-start.34 = (f32[1024]{0:T(1024)S(1)}, f32[1024]{0:T(1024)}, u32[]{:S(2)}) copy-start(f32[1024]{0:T(1024)} %copy-done.33) | copy-start | bytes 12292
  1265.2 48.2 %copy-start.37 = (f32[2048]{0:T(1024)S(1)}, f32[2048]{0:T(1024)}, u32[]{:S(2)}) copy-start(f32[2048]{0:T(1024)} %get-tuple-element.376) | copy-start | bytes 24580
  (42 other events, 361.6 us)
Sparse Core Ops, SparseCore 0:
  98.8 47.2 reduce-scatter.6
  713.8 34.9 all-gather.12
  755.0 143.1 all-reduce.7
  1087.5 90.4 all-reduce.9
  1180.2 84.8 all-reduce.5
Sparse Core Ops, SparseCore 1:
  100.9 91.6 all-gather.22
  194.6 79.1 all-gather.14
  275.7 52.8 all-gather.18
  330.6 54.2 all-gather.16
  387.0 54.2 all-gather.20
  542.4 86.8 reduce-scatter.10
  631.6 77.3 reduce-scatter.8
  737.8 71.8 reduce-scatter.16
  812.9 71.3 reduce-scatter.14
  888.1 71.1 reduce-scatter.12

commit v2 on v1

--- a/solution.py
+++ b/solution.py
@@ -1,6 +1,11 @@
+import functools
+
 import jax
 import jax.numpy as jnp
+import numpy as np
 from jax import lax
+from jax.experimental import pallas as pl
+from jax.experimental.pallas import tpu as pltpu
 from jax.sharding import PartitionSpec as P
 
 HD = 64
@@ -35,11 +40,800 @@
     )
 
 
+NT = (((1,), (1,)), ((), ()))
+TN = (((0,), (0,)), ((), ()))
+f32 = jnp.float32
+bf16 = jnp.bfloat16
+BQ = 512
+BK = 1024
+BK_BACK = 512
+
+def busy(us):
+    return pl.CostEstimate(flops=int(us * 1e8), bytes_accessed=0, transcendentals=0)
+
+
+def lanes(shape):
+    return lax.broadcasted_iota(jnp.int32, shape, len(shape) - 1)
+
+def rope_wide(v, cos, sin):
+    low = lanes(v.shape) % HD < HD // 2
+    swapped = jnp.where(low, pltpu.roll(v, 128 - HD // 2, 1), pltpu.roll(v, HD // 2, 1))
+    return v * cos + swapped * sin
+
+def project_kernel(x_ref, gain_ref, wq_ref, wk_ref, wv_ref, cos_ref, sin_ref, a_ref, q_ref, k_ref, v_ref):
+    x = x_ref[...].astype(f32)
+    r = lax.rsqrt(jnp.mean(x * x, -1, keepdims=True) + EPSILON)
+    a = (x * r * gain_ref[...].astype(f32)).astype(bf16)
+    a_ref[...] = a
+    cos, sin = cos_ref[...], sin_ref[...]
+    k = jnp.dot(a, wk_ref[...], preferred_element_type=f32)
+    k_ref[...] = rope_wide(k, cos, sin).astype(bf16)
+    v = jnp.dot(a, wv_ref[...], preferred_element_type=f32).astype(bf16)
+    v_ref[:, :128] = v
+    v_ref[:, 128:] = jnp.ones_like(v)
+    low = lanes(k.shape) < HD
+    for pair in range(2):
+        q = jnp.dot(a, wq_ref[:, pair * 128 : pair * 128 + 128], preferred_element_type=f32)
+        q = rope_wide(q, cos, sin) * HD ** (-0.5)
+        other = pltpu.roll(q, HD, 1)
+        mine = low if pair == 0 else ~low
+        first, second = (q, other) if pair == 0 else (other, q)
+        q_ref[2 * pair] = jnp.where(mine, first, 0.0).astype(bf16)
+        q_ref[2 * pair + 1] = jnp.where(mine, second, 0.0).astype(bf16)
+
+def project(tokens, gain, wq, wk, wv, cos, sin):
+    L, D = tokens.shape
+    B = 256
+    full = lambda a: pl.BlockSpec(a.shape, lambda i: (0,) * a.ndim)
+    rows = lambda w: pl.BlockSpec((B, w), lambda i: (i, 0))
+    return pl.pallas_call(
+        project_kernel, grid=(L // B,),
+        in_specs=[rows(D), full(gain), full(wq), full(wk), full(wv), rows(128), rows(128)],
+        out_specs=[rows(D), pl.BlockSpec((4, B, 128), lambda i: (0, i, 0)), rows(128), rows(256)],
+        out_shape=[jax.ShapeDtypeStruct((L, D), bf16), jax.ShapeDtypeStruct((4, L, 128), bf16),
+                   jax.ShapeDtypeStruct((L, 128), bf16), jax.ShapeDtypeStruct((L, 256), bf16)],
+        compiler_params=pltpu.CompilerParams(vmem_limit_bytes=40 << 20),
+        cost_estimate=busy(9),
+        name="project",
+    )(tokens, gain, wq, wk, wv, cos, sin)
+
+def attend_kernel(bq, bk, kv, prefix_ref, q_ref, k_ref, v_ref, *refs):
+    o_ref, lse_ref, s_ref = refs[-3:]
+    i = pl.program_id(0)
+    start = i * bq
+    prefix = prefix_ref[0]
+    full_blocks = jnp.maximum(start + 1, prefix) // bk
+    all_blocks = (jnp.maximum(start + bq, prefix) + bk - 1) // bk
+    rows = 2 * bq
+    pos = start + lax.broadcasted_iota(jnp.int32, (rows, 1), 0) % bq
+    limit = jnp.maximum(pos, prefix - 1)
+    low = lanes((bq, 128)) < HD
+    q = jnp.concatenate([q_ref[0], q_ref[1]], 0)
+
+    def tile_max(s, peak):
+        for c in range(bk // 128):
+            peak = jnp.maximum(peak, s[:, c * 128 : c * 128 + 128])
+        return peak
+
+    def plain(j, peak):
+        off = pl.multiple_of(j * bk, bk)
+        s = lax.dot_general(q, k_ref[pl.ds(off, bk), :], NT, preferred_element_type=f32)
+        s_ref[:, pl.ds(off, bk)] = s
+        return tile_max(s, peak)
+
+    def masked(j, peak):
+        off = pl.multiple_of(j * bk, bk)
+        s = lax.dot_general(q, k_ref[pl.ds(off, bk), :], NT, preferred_element_type=f32)
+        s = jnp.where(lanes((rows, bk)) <= limit - off, s, -1e30)
+        s_ref[:, pl.ds(off, bk)] = s
+        return tile_max(s, peak)
+
+    peak = jnp.full((rows, 128), -1e30, f32)
+    peak = lax.fori_loop(0, full_blocks, plain, peak)
+    peak = lax.fori_loop(full_blocks, all_blocks, masked, peak)
+    peak = jnp.max(peak, -1, keepdims=True)
+
+    def weigh(j, acc):
+        off = pl.multiple_of(j * bk, bk)
+        p = jnp.exp(s_ref[:, pl.ds(off, bk)] - peak).astype(bf16)
+        return acc + jnp.dot(p, v_ref[pl.ds(off, bk), :], preferred_element_type=f32)
+
+    acc = lax.fori_loop(0, all_blocks, weigh, jnp.zeros((rows, 256), f32))
+    total = acc[:, 128:]
+    out = acc[:, :128] / total
+    one, two = out[:bq], out[bq:]
+    if kv == 0:
+        merged = jnp.where(low, one, pltpu.roll(two, HD, 1))
+    else:
+        merged = jnp.where(low, pltpu.roll(one, HD, 1), two)
+    o_ref[...] = merged.astype(bf16)
+    lse = (peak + jnp.log(total)).T
+    lse_ref[0] = lse[:8]
+
+
+def attend(prefix, q, k, v, kv, bq, bk, before=()):
+    L = k.shape[0]
+    return pl.pallas_call(
+        functools.partial(attend_kernel, bq, bk, kv),
+        grid_spec=pltpu.PrefetchScalarGridSpec(
+            num_scalar_prefetch=1, grid=(L // bq,),
+            in_specs=[pl.BlockSpec((2, bq, 128), lambda i, p: (kv, i, 0)),
+                      pl.BlockSpec((L, 128), lambda i, p: (0, 0)),
+                      pl.BlockSpec((L, 256), lambda i, p: (0, 0))]
+            + [pl.BlockSpec(memory_space=pl.ANY)] * len(before),
+            out_specs=[pl.BlockSpec((bq, 128), lambda i, p: (i, kv)),
+                       pl.BlockSpec((1, 8, 2 * bq), lambda i, p: (kv, 0, i))],
+            scratch_shapes=[pltpu.VMEM((2 * bq, L), f32)]),
+        out_shape=[jax.ShapeDtypeStruct((L, 256), bf16), jax.ShapeDtypeStruct((2, 8, 2 * L), f32)],
+        input_output_aliases={4 + i: i for i in range(len(before))},
+        compiler_params=pltpu.CompilerParams(vmem_limit_bytes=48 << 20),
+        cost_estimate=busy(14),
+        name="attend",
+    )(prefix, q, k, v, *before)
+
+
+def attend_back_kernel(bq, bk, prefix_ref, q_ref, k_ref, v_ref, o_ref, do_ref, lse_ref, cos_ref, sin_ref, cosa_ref, sina_ref,
+                       out_ref, dk_acc, dv_acc):
+    i = pl.program_id(0)
+    start = i * bq
+    prefix = prefix_ref[0]
+    full_blocks = jnp.maximum(start + 1, prefix) // bk
+    all_blocks = (jnp.maximum(start + bq, prefix) + bk - 1) // bk
+    rows = 2 * bq
+    pos = start + lax.broadcasted_iota(jnp.int32, (1, rows), 1) % bq
+    limit = jnp.maximum(pos, prefix - 1)
+    low = lanes((bq, 128)) < HD
+
+    @pl.when(i == 0)
+    def _():
+        dk_acc[...] = jnp.zeros_like(dk_acc)
+        dv_acc[...] = jnp.zeros_like(dv_acc)
+
+    for kv in range(2):
+        q = jnp.concatenate([q_ref[2 * kv], q_ref[2 * kv + 1]], 0)
+        mine = low if kv == 0 else ~low
+        pair = do_ref[:, kv * 128 : kv * 128 + 128].astype(f32)
+        swap = pltpu.roll(pair, HD, 1)
+        first, second = (pair, swap) if kv == 0 else (swap, pair)
+        do = jnp.concatenate([jnp.where(mine, first, 0.0), jnp.where(mine, second, 0.0)], 0).astype(bf16)
+        prod = pair * o_ref[:, kv * 128 : kv * 128 + 128].astype(f32)
+        one = jnp.sum(jnp.where(low, prod, 0.0), -1, keepdims=True)
+        two = jnp.sum(jnp.where(low, 0.0, prod), -1, keepdims=True)
+        center = jnp.broadcast_to(jnp.concatenate([one, two], 0), (rows, 128)).T[:1]
+        lse = lse_ref[kv, :1, :]
+
+        def step(j, dq, mask):
+            off = pl.multiple_of(j * bk, bk)
+            kb = k_ref[pl.ds(off, bk), :]
+            s = lax.dot_general(kb, q, NT, preferred_element_type=f32)
+            if mask:
+                s = jnp.where(off + lax.broadcasted_iota(jnp.int32, (bk, rows), 0) <= limit, s, -1e30)
+            p = jnp.exp(s - lse)
+            dp = lax.dot_general(v_ref[pl.ds(off, bk), :128], do, NT, preferred_element_type=f32)
+            ds = (p * (dp - center)).astype(bf16)
+            dv_acc[pl.ds(off, bk), :] += jnp.dot(p.astype(bf16), do, preferred_element_type=f32)
+            dk_acc[pl.ds(off, bk), :] += jnp.dot(ds, q, preferred_element_type=f32)
+            return dq + lax.dot_general(ds, kb, TN, preferred_element_type=f32)
+
+        dq = jnp.zeros((rows, 128), f32)
+        dq = lax.fori_loop(0, full_blocks, functools.partial(step, mask=False), dq)
+        dq = lax.fori_loop(full_blocks, all_blocks, functools.partial(step, mask=True), dq)
+        dq = dq * HD ** (-0.5)
+        one, two = dq[:bq], dq[bq:]
+        if kv == 0:
+            merged = jnp.where(low, one, pltpu.roll(two, HD, 1))
+        else:
+            merged = jnp.where(low, pltpu.roll(one, HD, 1), two)
+        out_ref[pl.ds(pl.multiple_of(start, bq), bq), kv * 128 : kv * 128 + 128] = rope_wide(merged, cos_ref[...], -sin_ref[...]).astype(bf16)
+
+    @pl.when(i == pl.num_programs(0) - 1)
+    def _():
+        for b in range(dk_acc.shape[0] // bq):
+            r = pl.ds(b * bq, bq)
+            out_ref[r, 256:384] = rope_wide(dk_acc[r, :], cosa_ref[r, :], -sina_ref[r, :]).astype(bf16)
+            out_ref[r, 384:] = dv_acc[r, :].astype(bf16)
+
+def attend_back(prefix, q, k, v, o, do, lse, cos, sin, bq=256, bk=256):
+    L = k.shape[0]
+    fullL = pl.BlockSpec((L, 128), lambda i, p: (0, 0))
+    return pl.pallas_call(
+        functools.partial(attend_back_kernel, bq, bk),
+        grid_spec=pltpu.PrefetchScalarGridSpec(
+            num_scalar_prefetch=1, grid=(L // bq,),
+            in_specs=[pl.BlockSpec((4, bq, 128), lambda i, p: (0, i, 0)), fullL,
+                      pl.BlockSpec((L, 256), lambda i, p: (0, 0)),
+                      pl.BlockSpec((bq, 256), lambda i, p: (i, 0)),
+                      pl.BlockSpec((bq, 256), lambda i, p: (i, 0)),
+                      pl.BlockSpec((2, 8, 2 * bq), lambda i, p: (0, 0, i)),
+                      pl.BlockSpec((bq, 128), lambda i, p: (i, 0)),
+                      pl.BlockSpec((bq, 128), lambda i, p: (i, 0)), fullL, fullL],
+            out_specs=pl.BlockSpec((L, 512), lambda i, p: (0, 0)),
+            scratch_shapes=[pltpu.VMEM((L, 128), f32), pltpu.VMEM((L, 128), f32)]),
+        out_shape=jax.ShapeDtypeStruct((L, 512), bf16),
+        compiler_params=pltpu.CompilerParams(vmem_limit_bytes=48 << 20),
+        cost_estimate=busy(46),
+        name="attend_back",
+    )(prefix, q, k, v, o, do, lse, cos, sin, cos, sin)
+
+
+def pick_kernel(experts, per, cap, pairs, shift_ref, *refs):
+    in_ref, dyo_ref, gs_ref, gate_ref, code_ref, code_t, gate_t, rows_s, dy_s = refs[-9:]
+    tokens, width = rows_s.shape
+
+    @pl.when(pl.program_id(0) == 0)
+    def _():
+        if pairs:
+            rows_ref, rows_other, side_ref, side_other, router_ref = refs[:5]
+            first = shift_ref[experts] != 0
+            rows = jnp.where(first, rows_ref[...], rows_other[...])
+            side = jnp.where(first, side_ref[...], side_other[...])
+        else:
+            rows_ref, side_ref, router_ref = refs[:3]
+            rows, side = rows_ref[...], side_ref[...]
+        rows_s[...] = rows
+        dy_s[...] = side[:, :width]
+        code = side[:, width:].astype(f32)
+        code_ref[...] = code
+        logits = jnp.dot(rows, router_ref[...], preferred_element_type=f32)
+        chosen = jnp.where(code >= 0, logits, -1e30)
+        raised = jnp.where(code >= 0, jnp.exp(chosen - jnp.max(chosen, -1, keepdims=True)), 0.0)
+        gate = raised / jnp.sum(raised, -1, keepdims=True)
+        gate_ref[...] = gate
+        gate_t[...] = gate.T
+        code_t[...] = code.T
+
+    hots = []
+    for e in range(per):
+        row = pl.ds(shift_ref[pl.program_id(0) * per + e], 1)
+        hot = code_t[row, :] == lax.broadcasted_iota(jnp.int32, (cap, tokens), 0).astype(f32)
+        gs = jnp.sum(jnp.where(hot, gate_t[row, :], 0.0), -1, keepdims=True)
+        gs_ref[e] = jnp.broadcast_to(gs, (cap, 128))
+        hots.append(hot.astype(bf16))
+    hot = jnp.concatenate(hots, 0)
+    in_ref[...] = jnp.dot(hot, rows_s[...], preferred_element_type=f32).astype(bf16).reshape(in_ref.shape)
+    dyo_ref[...] = jnp.dot(hot, dy_s[...], preferred_element_type=f32).astype(bf16).reshape(dyo_ref.shape)
+
+
+def pick(shift, rows, sides, router, cap):
+    R, D = rows[0].shape
+    E = shift.shape[0] - 1
+    W = router.shape[1]
+    per = 2
+    operands = [*rows, *sides, router]
+    whole = lambda a: pl.BlockSpec(a.shape, lambda e: (0, 0))
+    some = lambda w: pl.BlockSpec((per, cap, w), lambda e: (e, 0, 0))
+    wide = pl.BlockSpec((R, W), lambda e: (0, 0))
+    return pl.pallas_call(
+        functools.partial(pick_kernel, E, per, cap, len(rows) == 2),
+        grid=(E // per,),
+        in_specs=[pl.BlockSpec(memory_space=pltpu.SMEM)] + [whole(a) for a in operands],
+        out_specs=[some(D), some(D), some(128), wide, wide],
+        out_shape=[pltpu.HBM((E, cap, D), bf16), pltpu.HBM((E, cap, D), bf16),
+                   pltpu.HBM((E, cap, 128), f32), jax.ShapeDtypeStruct((R, W), f32), jax.ShapeDtypeStruct((R, W), f32)],
+        scratch_shapes=[pltpu.VMEM((W, R), f32), pltpu.VMEM((W, R), f32), pltpu.VMEM((R, D), bf16), pltpu.VMEM((R, D), bf16)],
+        compiler_params=pltpu.CompilerParams(vmem_limit_bytes=40 << 20),
+        cost_estimate=busy(4),
+        name="pick",
+    )(shift, *operands)
+
+
+def ffn_kernel(n, blocks, *refs):
+    rows_refs, dy_refs, gs_refs = refs[:n], refs[n : 2 * n], refs[2 * n : 3 * n]
+    w_ref, eout_ref, drows_ref, dgs_ref, act_ref, dgu_ref = refs[3 * n :]
+    cap, D = rows_refs[0].shape[1:]
+    M = n * cap
+    rows = jnp.concatenate([r[0] for r in rows_refs], 0)
+    dy = jnp.concatenate([r[0] for r in dy_refs], 0)
+    gs = jnp.concatenate([r[0] for r in gs_refs], 0)
+    dout = (dy.astype(f32) * gs[:, :1]).astype(bf16)
+    F = w_ref.shape[-1]
+    eout = jnp.zeros((M, D), f32)
+    drows = jnp.zeros((M, D), f32)
+    for pair in range(0, blocks, 2):
+        acts = []
+        wd2 = jnp.concatenate([w_ref[0, pair, 2, 0], w_ref[0, pair + 1, 2, 0]], 1)
+        dact2 = jnp.dot(dout, wd2, preferred_element_type=f32)
+        for b in (pair, pair + 1):
+            w = jnp.concatenate([w_ref[0, b, 0, 0], w_ref[0, b, 1, 0]], 1)
+            gu = jnp.dot(rows, w, preferred_element_type=f32)
+            g, u = gu[:, :F], gu[:, F:]
+            sg = 1.0 / (1.0 + jnp.exp(-g))
+            gsg = g * sg
+            acts.append((gsg * u).astype(bf16))
+            dact = dact2[:, (b - pair) * F : (b - pair + 1) * F]
+            dg = dact * u * (sg + gsg * (1.0 - sg))
+            du = dact * gsg
+            dgu = jnp.concatenate([dg, du], 1).astype(bf16)
+            dgu_ref[0, :, b * 2 * F : (b + 1) * 2 * F] = dgu
+            drows = drows + lax.dot_general(dgu, w, NT, preferred_element_type=f32)
+        act = jnp.concatenate(acts, 1)
+        act_ref[0, :, pair * F : (pair + 2) * F] = act
+        eout = eout + lax.dot_general(act, wd2, NT, preferred_element_type=f32)
+    eout = eout.astype(bf16)
+    eout_ref[0] = eout
+    drows_ref[0] = drows.astype(bf16)
+    dgs = jnp.sum(dy.astype(f32) * eout.astype(f32), -1, keepdims=True)
+    dgs_ref[0] = jnp.broadcast_to(dgs, (M, 128))
+
+
+def ffn(picked, weights):
+    n = len(picked)
+    total, cap, D = picked[0][0].shape
+    groups, blocks, _, E, _, F = weights.shape
+    H = blocks * F
+    M = n * cap
+    spec = lambda w: pl.BlockSpec((1, cap, w), lambda e: (e, 0, 0))
+    outs = lambda w: pl.BlockSpec((1, M, w), lambda e: (e, 0, 0))
+    wsp = pl.BlockSpec((1, blocks, 3, 1, D, F), lambda e: (e // E, 0, 0, e % E, 0, 0))
+    sh = lambda w, t: jax.ShapeDtypeStruct((total, M, w), t)
+    return pl.pallas_call(
+        functools.partial(ffn_kernel, n, blocks), grid=(total,),
+        in_specs=[spec(D)] * (2 * n) + [spec(128)] * n + [wsp],
+        out_specs=[outs(D), outs(D), outs(128), outs(H), outs(2 * H)],
+        out_shape=[sh(D, bf16), sh(D, bf16), sh(128, f32), sh(H, bf16), sh(2 * H, bf16)],
+        compiler_params=pltpu.CompilerParams(vmem_limit_bytes=56 << 20),
+        cost_estimate=busy(40),
+        name="ffn",
+    )(*[p[i] for i in range(3) for p in picked], weights)
+
+
+def wgrad_kernel(n, blocks, *refs):
+    rows_refs, dy_refs, gs_refs = refs[:n], refs[n : 2 * n], refs[2 * n : 3 * n]
+    act_ref, dgu_ref, out_ref = refs[3 * n :]
+    rows = jnp.concatenate([r[0] for r in rows_refs], 0)
+    dy = jnp.concatenate([r[0] for r in dy_refs], 0)
+    gs = jnp.concatenate([r[0] for r in gs_refs], 0)
+    dout = (dy.astype(f32) * gs[:, :1]).astype(bf16)
+    F = act_ref.shape[2] // blocks
+    for b in range(blocks):
+        dgu = dgu_ref[0, :, b * 2 * F : (b + 1) * 2 * F]
+        g = lax.dot_general(rows, dgu, TN, preferred_element_type=f32).astype(bf16)
+        out_ref[0, b, 0, 0] = g[:, :F]
+        out_ref[0, b, 1, 0] = g[:, F:]
+    for pair in range(0, blocks, 2):
+        gd = lax.dot_general(dout, act_ref[0, :, pair * F : (pair + 2) * F], TN, preferred_element_type=f32).astype(bf16)
+        out_ref[0, pair, 2, 0] = gd[:, :F]
+        out_ref[0, pair + 1, 2, 0] = gd[:, F:]
+
+
+def wgrad(picked, act, dgu, blocks, groups):
+    n = len(picked)
+    total, cap, D = picked[0][0].shape
+    M, H = act.shape[1:]
+    F = H // blocks
+    E = total // groups
+    spec = lambda w: pl.BlockSpec((1, cap, w), lambda e: (e, 0, 0))
+    wide = lambda w: pl.BlockSpec((1, M, w), lambda e: (e, 0, 0))
+    return pl.pallas_call(
+        functools.partial(wgrad_kernel, n, blocks),
+        grid=(total,),
+        in_specs=[spec(D)] * (2 * n) + [spec(128)] * n + [wide(H), wide(2 * H)],
+        out_specs=pl.BlockSpec((1, blocks, 3, 1, D, F), lambda e: (e // E, 0, 0, e % E, 0, 0)),
+        out_shape=jax.ShapeDtypeStruct((groups, blocks, 3, E, D, F), bf16),
+        compiler_params=pltpu.CompilerParams(vmem_limit_bytes=56 << 20),
+        cost_estimate=busy(26),
+        name="wgrad",
+    )(*[p[i] for i in range(3) for p in picked], act, dgu)
+
+
+def hot_columns(code, shift, cap):
+    col = jnp.sum(jnp.where(lanes(code.shape) == shift, code, 0.0), -1, keepdims=True)
+    return col == lanes((code.shape[0], cap)).astype(f32)
+
+
+def merge_back_kernel(n, E, cap, shift_ref, *refs):
+    sides, (d_ref, g_ref), outs = refs[:n], refs[n : n + 2], refs[n + 2 :]
+    D = d_ref.shape[2]
+    lane = lanes((cap, 128))
+    for source in range(n):
+
+        @pl.when(pl.program_id(0) == source)
+        def _():
+            code = sides[source][...]
+            total = jnp.zeros((code.shape[0], D), f32)
+            gates = jnp.zeros((code.shape[0], 128), f32)
+            for e0 in range(0, E, 4):
+                some = range(e0, min(e0 + 4, E))
+                hot = jnp.concatenate([hot_columns(code, shift_ref[e], cap).astype(bf16) for e in some], 1)
+                rows = jnp.concatenate([d_ref[e] for e in some], 0)
+                side = jnp.concatenate([jnp.where(lane == shift_ref[e], g_ref[e], 0.0).astype(bf16) for e in some], 0)
+                total = total + jnp.dot(hot, rows, preferred_element_type=f32)
+                gates = gates + jnp.dot(hot, side, preferred_element_type=f32)
+            outs[source][:, :D] = total.astype(bf16)
+            outs[source][:, D:] = gates.astype(bf16)
+
+
+def merge_back(shift, codes, first, drows, dgs, cap):
+    n = len(codes)
+    R, W = codes[0].shape
+    E, _, D = drows.shape
+    part = lambda w: pl.BlockSpec((E, cap, w), lambda i: (0, i + first, 0))
+    whole = lambda w: pl.BlockSpec((R, w), lambda i: (0, 0))
+    return pl.pallas_call(
+        functools.partial(merge_back_kernel, n, E, cap),
+        grid=(n,),
+        in_specs=[pl.BlockSpec(memory_space=pltpu.SMEM)] + [whole(W)] * n + [part(D), part(128)],
+        out_specs=[whole(D + 128)] * n,
+        out_shape=[jax.ShapeDtypeStruct((R, D + 128), bf16)] * n,
+        compiler_params=pltpu.CompilerParams(vmem_limit_bytes=48 << 20),
+        cost_estimate=busy(3 * n),
+        name="merge_back",
+    )(shift, *codes, drows, dgs)
+
+
+def merge_out_kernel(n, E, cap, shift_ref, *refs):
+    sides, gates, e_ref, outs = refs[:n], refs[n : 2 * n], refs[2 * n], refs[2 * n + 1 :]
+    D = e_ref.shape[2]
+    for source in range(n):
+
+        @pl.when(pl.program_id(0) == source)
+        def _():
+            code = sides[source][...]
+            gate = gates[source][...]
+            total = jnp.zeros((code.shape[0], D), f32)
+            for e0 in range(0, E, 4):
+                some = range(e0, min(e0 + 4, E))
+                parts = []
+                for e in some:
+                    g = jnp.sum(jnp.where(lanes(gate.shape) == shift_ref[e], gate, 0.0), -1, keepdims=True)
+                    parts.append(jnp.where(hot_columns(code, shift_ref[e], cap), g, 0.0).astype(bf16))
+                rows = jnp.concatenate([e_ref[e] for e in some], 0)
+                total = total + jnp.dot(jnp.concatenate(parts, 1), rows, preferred_element_type=f32)
+            outs[source][...] = total.astype(bf16)
+
+
+def merge_out(shift, codes, gates, eout, cap):
+    n = len(codes)
+    R, W = codes[0].shape
+    E, _, D = eout.shape
+    whole = lambda w: pl.BlockSpec((R, w), lambda i: (0, 0))
+    return pl.pallas_call(
+        functools.partial(merge_out_kernel, n, E, cap),
+        grid=(n,),
+        in_specs=[pl.BlockSpec(memory_space=pltpu.SMEM)] + [whole(W)] * (2 * n)
+        + [pl.BlockSpec((E, cap, D), lambda i: (0, i, 0))],
+        out_specs=[whole(D)] * n,
+        out_shape=[jax.ShapeDtypeStruct((R, D), bf16)] * n,
+        compiler_params=pltpu.CompilerParams(vmem_limit_bytes=48 << 20),
+        cost_estimate=busy(11),
+        name="merge_out",
+    )(shift, *codes, *gates, eout)
+
+
+def finish_kernel(core_ref, sum_ref, x_ref, dh_ref, gain_ref, *refs):
+    out_ref = refs[-1]
+    x = x_ref[...].astype(f32)
+    r = lax.rsqrt(jnp.mean(x * x, -1, keepdims=True) + EPSILON)
+    scaled = sum_ref[...].astype(f32) * gain_ref[...].astype(f32)
+    out_ref[...] = dh_ref[...].astype(f32) + r * scaled - x * (r * r * r * jnp.mean(scaled * x, -1, keepdims=True))
+
+
+def finish(core, summed, tokens, hidden, gain, rows, before=()):
+    L, D = tokens.shape
+    half = rows // 2
+    place = lambda i, p: ((i // 2) * 4 + p[0] * 2 + i % 2, 0)
+    return pl.pallas_call(
+        finish_kernel,
+        grid_spec=pltpu.PrefetchScalarGridSpec(
+            num_scalar_prefetch=1, grid=(L // rows,),
+            in_specs=[pl.BlockSpec((half, D), lambda i, p: (i, 0)), pl.BlockSpec((half, D), place), pl.BlockSpec((half, D), place),
+                      pl.BlockSpec((1, D), lambda i, p: (0, 0))] + [pl.BlockSpec(memory_space=pl.ANY)] * len(before),
+            out_specs=pl.BlockSpec((half, D), place)),
+        out_shape=jax.ShapeDtypeStruct((L, D), f32),
+        input_output_aliases={5 + i: i for i in range(len(before))},
+        compiler_params=pltpu.CompilerParams(vmem_limit_bytes=48 << 20),
+        cost_estimate=busy(4),
+        name="finish",
+    )(core, summed, tokens, hidden, gain, *before)
+
+
+def spread_kernel(n, more, rank_ref, att_ref, w_ref, *refs):
+    blocks = refs[:n]
+    hidden_ref, do_ref, og_ref = refs[-3:]
+    i = pl.program_id(0)
+
+    @pl.when(i == 0)
+    def _():
+        og_ref[...] = refs[n][...] if more else jnp.zeros_like(og_ref)
+
+    for b in range(n):
+
+        @pl.when(i == b)
+        def _():
+            block = blocks[b][...]
+            hidden_ref[...] = block
+            do_ref[...] = lax.dot_general(block, w_ref[...], NT, preferred_element_type=f32).astype(bf16)
+            og_ref[...] += lax.dot_general(att_ref[...], block, TN, preferred_element_type=f32)
+
+
+def spread(rank, first, blocks, attended, w_out, before=None):
+    n = len(blocks)
+    R, D = blocks[0].shape
+    L, H = attended.shape
+    place = lambda i, p: (p[0] ^ (i + first), 0)
+    whole = lambda a: pl.BlockSpec(a.shape, lambda i, p: (0, 0))
+    total = jax.ShapeDtypeStruct((H, D), f32)
+    operands = [attended, w_out, *blocks]
+    specs = [pl.BlockSpec((R, H), place), whole(w_out)] + [whole(b) for b in blocks]
+    aliases = {}
+    if before is not None:
+        hidden, do, og = before
+        operands += [og, hidden, do]
+        specs += [whole(og)] + [pl.BlockSpec(memory_space=pl.ANY)] * 2
+        aliases = {len(operands) - 1: 0, len(operands): 1}
+    return pl.pallas_call(
+        functools.partial(spread_kernel, n, before is not None),
+        grid_spec=pltpu.PrefetchScalarGridSpec(
+            num_scalar_prefetch=1, grid=(n,), in_specs=specs,
+            out_specs=[pl.BlockSpec((R, D), place), pl.BlockSpec((R, H), place), whole(total)]),
+        out_shape=[pltpu.HBM((L, D), bf16), pltpu.HBM((L, H), bf16), total],
+        input_output_aliases=aliases,
+        compiler_params=pltpu.CompilerParams(vmem_limit_bytes=32 << 20),
+        cost_estimate=busy(3),
+        name="spread",
+    )(rank, *operands)
+
+
+def swap(x, axis, bit=1):
+    count = lax.axis_size(axis)
+    return lax.ppermute(x, axis, [(i, i ^ bit) for i in range(count)])
+
+
+def total_over(x, axes):
+    for axis in axes:
+        bit = 1
+        while bit < lax.axis_size(axis):
+            x = x + swap(x, axis, bit)
+            bit *= 2
+    return x
+
+
+def wide_tables(length):
+    half = HD // 2
+    angles = np.arange(length)[:, None] * THETA_BASE ** (-(np.arange(half) / half))[None, :]
+    cos, sin = np.cos(angles), np.sin(angles)
+    return (
+        jnp.asarray(np.concatenate([cos, cos, cos, cos], 1), f32),
+        jnp.asarray(np.concatenate([-sin, sin, -sin, sin], 1), f32),
+    )
+
+
+NEAR = [(0, 1), (1, 0), (2, 3), (3, 2)]
+MIDDLE = [(1, 2), (2, 1)]
+TO_ENDS = [(1, 0), (2, 3)]
+FROM_ENDS = [(0, 1), (3, 2)]
+
+
+def line_first(x):
+    return lax.ppermute(x, "z", NEAR), lax.ppermute(x, "z", MIDDLE)
+
+
+def line_second(near, across):
+    return lax.ppermute(near, "z", MIDDLE), lax.ppermute(across, "z", TO_ENDS)
+
+
+def line_third(across_far):
+    return lax.ppermute(across_far, "z", TO_ENDS)
+
+
+def hold(*arrays):
+    return lax.optimization_barrier(arrays)
+
+
+def line_out(parts):
+    return lax.ppermute(parts[3], "z", FROM_ENDS), lax.ppermute(parts[2], "z", FROM_ENDS)
+
+
+def add_low(a, b):
+    return (a.astype(f32) + b.astype(f32)).astype(a.dtype)
+
+
+def line_over(part, from_end):
+    return lax.ppermute(add_low(part, from_end), "z", MIDDLE)
+
+
+def line_in(part, across_far):
+    return lax.ppermute(add_low(part, across_far), "z", NEAR)
+
+
+def line_sum(parts, from_end_far, from_end):
+    own, near, two, three = parts
+    across_far = line_over(two, from_end_far)
+    across = line_over(three, from_end)
+    got = line_in(near, across_far)
+    return own.astype(f32) + across.astype(f32) + got.astype(f32)
+
+
+def per_device_fast(
+    tokens,
+    prefix,
+    gain_attn,
+    w_query,
+    w_key,
+    w_value,
+    w_out,
+    gain_moe,
+    w_router,
+    routes,
+    fill_order,
+    w_gate,
+    w_up,
+    w_down,
+    cotangent,
+):
+    z, y, x, c = (lax.axis_index(a) for a in ("z", "y", "x", "c"))
+    shards = lax.axis_size("x") * lax.axis_size("c")
+    groups = lax.axis_size("y")
+    rank = x * lax.axis_size("c") + c
+    at_end = (z == 0) | (z == lax.axis_size("z") - 1)
+    length, width = tokens.shape
+    own_rows = routes.shape[0]
+    local = w_gate.shape[0]
+    cap = own_rows * TOPK // EXPERTS
+
+    expert_ids = jnp.arange(EXPERTS, dtype=jnp.int32)
+    member = jnp.sum((routes[:, :, None] == expert_ids[None, None, :]).astype(f32), 1)
+    priority = fill_order[0]
+    earlier = (priority[None, :] < priority[:, None]).astype(bf16)
+    slot_full = jnp.dot(earlier, member.astype(bf16), preferred_element_type=f32)
+    code = jnp.where(member > 0, jnp.minimum(slot_full, float(cap)), -1.0).astype(bf16)
+    code = jnp.pad(code, ((0, 0), (0, 128 - EXPERTS)), constant_values=-1)
+    side_own = jnp.concatenate([cotangent, code], 1)
+    side_near, side_across = line_first(side_own)
+    router_wide = jnp.pad(w_router, ((0, 0), (0, 128 - EXPERTS)))
+    shift = z * groups * local + jnp.arange(groups * local, dtype=jnp.int32)
+    shift_end = jnp.concatenate([shift, at_end.astype(jnp.int32)[None]])
+
+    own_weights = jnp.stack([w_gate, w_up, w_down.transpose(0, 2, 1)])
+    weights = lax.all_gather(own_weights, ("y", "x", "c"), axis=0, tiled=False)
+    weights = weights.reshape((groups, shards) + own_weights.shape)
+
+    cos, sin = wide_tables(length)
+    normed_one, query, key, value = project(tokens, gain_attn[None], w_query, w_key, w_value, cos, sin)
+    first_half = attend(prefix, query, key, value, 0, BQ, BK)
+    *first_half, side_near, side_across = hold(*first_half, side_near, side_across)
+    side_far, side_relay = line_second(side_near, side_across)
+    attended, log_total = attend(prefix, query, key, value, 1, BQ, BK, first_half)
+    attended, side_far = hold(attended, side_far)
+    side_last = line_third(side_far)
+
+
+    def out_block(place):
+        rows = lax.dynamic_slice_in_dim(attended, place * own_rows, own_rows, 0)
+        return jnp.dot(rows, w_out, preferred_element_type=f32)
+
+    far_sum = out_block(rank ^ 2) + swap(out_block(rank ^ 3).astype(bf16), "c").astype(f32)
+    far_got = swap(far_sum.astype(bf16), "x").astype(f32)
+    near_got = swap(out_block(rank ^ 1).astype(bf16), "c").astype(f32)
+    x_rows = lax.dynamic_slice_in_dim(tokens, rank * own_rows, own_rows, 0).astype(f32)
+    hidden_in = x_rows + out_block(rank) + near_got + far_got
+    rms_two = lax.rsqrt(jnp.mean(hidden_in * hidden_in, -1, keepdims=True) + EPSILON)
+    gain_two = gain_moe.astype(f32)
+    normed_two = (hidden_in * rms_two * gain_two).astype(bf16)
+
+    near, across = line_first(normed_two)
+    near, across, side_last = hold(near, across, side_last)
+    far, relay = line_second(near, across)
+    last = line_third(far)
+    picked = [
+        pick(shift_end, rows, sides, router_wide, cap)
+        for rows, sides in (
+            ((normed_two,), (side_own,)),
+            ((near,), (side_near,)),
+            ((relay, far), (side_relay, side_far)),
+            ((last, across), (side_last, side_across)),
+        )
+    ]
+    gates = [p[3] for p in picked]
+    codes = [p[4] for p in picked]
+    expert_out, rows_grad, gate_slots, act, hidden_grads = ffn(picked, weights)
+    far_back = merge_back(shift, codes[2:], 2, rows_grad, gate_slots, cap)
+    late_grad, *far_back = hold(rows_grad, *far_back)
+    back = [*merge_back(shift, codes[:2], 0, late_grad, gate_slots, cap), *far_back]
+    back_out = line_out(back)
+    late_act, *_ = hold(act, *back)
+    parts = wgrad(picked, late_act, hidden_grads, shards, groups)
+    back_far_out, parts = hold(back_out[0], parts)
+    back_out = (back_far_out, back_out[1])
+    back_own = line_sum(back, *back_out)
+    part_sum = lax.psum_scatter(
+        parts.reshape((groups * shards,) + parts.shape[2:]), ("y", "x", "c"), scatter_dimension=0, tiled=False
+    )
+
+    gate_own = gates[0]
+    gate_grad = back_own[:, width:]
+    logit_grad = gate_own * (gate_grad - jnp.sum(gate_own * gate_grad, -1, keepdims=True))
+    logit_low = logit_grad.astype(bf16)
+    normed_two_grad = back_own[:, :width] + lax.dot_general(
+        logit_low, router_wide, (((1,), (1,)), ((), ())), preferred_element_type=f32
+    )
+    router_part = lax.dot_general(
+        logit_low, normed_two, (((0,), (0,)), ((), ())), preferred_element_type=f32
+    )[:EXPERTS]
+    gain_two_part = jnp.sum(normed_two_grad * hidden_in * rms_two, 0)
+    scaled_two = normed_two_grad * gain_two
+    hidden_grad = (
+        cotangent.astype(f32)
+        + rms_two * scaled_two
+        - hidden_in * rms_two**3 * jnp.mean(scaled_two * hidden_in, -1, keepdims=True)
+    ).astype(bf16)
+    small = jnp.concatenate([router_part, gain_two_part[None], jnp.zeros((7, width), f32)], 0)
+    small = total_over(small.reshape(-1, width // 2).astype(bf16), ("c", "x"))
+    hidden_over_x = swap(hidden_grad, "x")
+    late_out, *_ = hold(expert_out, hidden_grad)
+    out_parts = merge_out(shift, codes, gates, late_out, cap)
+    hidden_over_x, *out_parts = hold(hidden_over_x, *out_parts)
+    out_end_far, out_end = line_out(out_parts)
+    rank_row = rank.astype(jnp.int32)[None]
+    near_done = spread(rank_row, 0, [hidden_grad, swap(hidden_grad, "c")], attended, w_out)
+    hidden_over_x, *near_done = hold(hidden_over_x, *near_done)
+    hidden_all, attended_grad, out_grad = spread(
+        rank_row, 2, [hidden_over_x, swap(hidden_over_x, "c")], attended, w_out, near_done
+    )
+    attended_grad, small, out_low, out_end_far = hold(attended_grad, small, out_grad.astype(bf16), out_end_far)
+    out_far = line_over(out_parts[2], out_end_far)
+    heads_back = attend_back(
+        prefix, query, key, value, attended, attended_grad, log_total, cos, sin, BQ, BK_BACK
+    )
+    heads_in = jnp.concatenate([w_query, w_key, w_value], 1)
+    heads_grad = jnp.einsum("id,ih->dh", normed_one, heads_back, preferred_element_type=f32)
+    low = jnp.concatenate([heads_grad.astype(bf16), out_low.reshape(-1, heads_grad.shape[1]), small], 0)
+    heads_back, low, part_sum, out_far, out_end = hold(heads_back, low, part_sum, out_far, out_end)
+
+    low_all = lax.psum(low, ("z", "y"))
+
+    out_across = line_over(out_parts[3], out_end)
+    out_got = line_in(out_parts[1], out_far)
+    moe_own = out_parts[0].astype(f32) + out_across.astype(f32) + out_got.astype(f32)
+    block_output = (hidden_in + moe_own).astype(bf16)
+
+    by_core = heads_back.reshape(shards // 2, 2, own_rows, -1)
+
+    def rows_of(which):
+        rows = lax.dynamic_index_in_dim(by_core, which, 1, keepdims=False)
+        return lax.dot_general(rows, heads_in, (((2,), (1,)), ((), ())), preferred_element_type=f32)
+
+    from_core = swap(rows_of(1 - c).astype(bf16), "c")
+    core_sum = (rows_of(c) + from_core.astype(f32)).astype(bf16)
+    chip_sum = (core_sum.astype(f32) + swap(core_sum, "x").astype(f32)).astype(bf16)
+    chip_sum, low_all = hold(chip_sum, low_all)
+    other_sum = swap(chip_sum, "c")
+    core = c.astype(jnp.int32)[None]
+    gain_row = gain_attn[None]
+    input_grad = finish(core, chip_sum.reshape(-1, width), tokens, hidden_all, gain_row, own_rows)
+    other_sum, input_grad = hold(other_sum, input_grad)
+    input_grad = finish(
+        1 - core, other_sum.reshape(-1, width), tokens, hidden_all, gain_row, own_rows, (input_grad,)
+    )
+    low_all = low_all.astype(f32)
+    split = width + out_grad.size // low.shape[1]
+    heads_total = low_all[:width]
+    out_total = low_all[width:split].reshape(out_grad.shape)
+    small_total = low_all[split:].reshape(-1, width)
+    gain_one_part = jnp.sum(heads_total * heads_in.astype(f32), 1) / gain_attn.astype(f32)
+    gain_one_total = total_over(gain_one_part.reshape(8, -1), ("c", "x")).reshape(-1)
+    cut = w_query.shape[1]
+    return (
+        block_output,
+        input_grad,
+        gain_one_total,
+        heads_total[:, :cut],
+        heads_total[:, cut : cut + w_key.shape[1]],
+        heads_total[:, cut + w_key.shape[1] :],
+        out_total,
+        small_total[EXPERTS],
+        small_total[:EXPERTS].T,
+        part_sum[0].astype(f32),
+        part_sum[1].astype(f32),
+        part_sum[2].astype(f32).transpose(0, 2, 1),
+    )
+
+
 def group_gather(x, axes):
     return lax.all_gather(x, axes, axis=0, tiled=False)
 
 
-def per_device(
+def per_device_general(
     tokens,
     prefix,
     gain_attn,
@@ -345,11 +1139,12 @@
     mesh = jax.sharding.Mesh(
         mesh.devices.reshape(dp_count // 2, 2, tensor_count // 2, 2), ("z", "y", "x", "c")
     )
+    fast = mesh.devices.shape == (4, 2, 2, 2)
     dp = ("z", "y")
     tensor = ("x", "c")
     both = dp + tensor
     return jax.shard_map(
-        per_device,
+        per_device_fast if fast else per_device_general,
         mesh=mesh,
         in_specs=(
             P(dp, None),

time: 1340 us -> 689 us (0.51)
  matrix products: 407 us -> 19 us
  Pallas kernels: 0 us -> 213 us
  waiting for transfers between devices: 509 us -> 303 us
  other arithmetic: 162 us -> 30.2 us
  local copies, waits for them, and re-layouts: 170 us -> 40.4 us
  blocking collectives: 62.1 us -> 0 us
  starting transfers between devices: 0.63 us -> 58.9 us
    dot_general x59 -> x10, matrix products: 407 us -> 19 us  [the longest x2 7.04 us: rows_of(): lax.dot_general(rows, heads_in, (((2,), (1,)), ((), ())), preferred_eleme...]
    ppermute x0 -> x33, waiting for transfers between devices: none -> 245 us  [the longest x13 127 us: swap(): return lax.ppermute(x, axis, [(i, i ^ bit) for i in range(count)])]
    pallas_call x0 -> x17, Pallas kernels: none -> 213 us  [the longest x1 48.5 us: attend_back(): pl.pallas_call(functools.partial(attend_back_kernel, bq, bk), grid_spec=p...]
    reduce_scatter x6 -> x1, waiting for transfers between devices: 194 us -> 0.02 us  [per_device_fast(): lax.psum_scatter(parts.reshape((groups * shards,) + parts.shape[2:]), ('y...]
    all_gather x6 -> x1, waiting for transfers between devices: 161 us -> 0.01 us  [per_device_fast(): weights = lax.all_gather(own_weights, ('y', 'x', 'c'), axis=0, tiled=False)]
    psum x3 -> x1, waiting for transfers between devices: 151 us -> 58.1 us  [per_device_fast(): low_all = lax.psum(low, ('z', 'y'))]
    reshape x7 -> x2, local copies, waits for them, and re-layouts: 65.4 us -> 1.48 us  [the longest x1 1.31 us: per_device_fast(): out_total = low_all[width:split].reshape(out_grad.shape)]
    convert_element_type x21 -> x14, other arithmetic: 78.8 us -> 17.6 us  [the longest x6 9.46 us: add_low(): return (a.astype(f32) + b.astype(f32)).astype(a.dtype)]
  transfers between devices with their start and end apart: 15 -> 36, of which waited for: 9 -> 15; matrix products, arithmetic and copies ran while one was open for 40% -> 7% of each run, Pallas kernels for 0% -> 24%
where the time goes in v2:
time: 689 us; the launch traced here: 680 us
  waiting for transfers between devices  303 us (44%)
  Pallas kernels  213 us (31%)
  starting transfers between devices  58.9 us (9%)
  local copies, waits for them, and re-layouts  40.4 us (6%)
  other arithmetic  30.2 us (4%)
  matrix products  19 us (3%)
  between operations  15.9 us (2%)
    ppermute x13, waiting for transfers between devices, swap(): return lax.ppermute(x, axis, [(i, i ^ bit) for i in range(count)])  127 us
    psum x1, waiting for transfers between devices, per_device_fast(): low_all = lax.psum(low, ('z', 'y'))  58.1 us
    pallas_call x1, Pallas kernels, attend_back(): pl.pallas_call(functools.partial(attend_back_kernel, bq, bk), grid_spec=p...  48.5 us
    pallas_call x1, Pallas kernels, ffn(): pl.pallas_call(functools.partial(ffn_kernel, n, blocks), grid=(total,), i...  38.4 us
    ppermute x4, waiting for transfers between devices, line_second(): return (lax.ppermute(near, 'z', MIDDLE), lax.ppermute(across, 'z', TO_ENDS))  36.7 us
    unnamed x181, local copies, waits for them, and re-layouts  34.9 us
    pallas_call x2, Pallas kernels, attend(): pl.pallas_call(functools.partial(attend_kernel, bq, bk, kv), grid_spec=pl...  27.8 us
    pallas_call x1, Pallas kernels, wgrad(): pl.pallas_call(functools.partial(wgrad_kernel, n, blocks), grid=(total,),...  26.2 us
  transfers between devices with their start and end apart: 36, of which 15 were waited for; matrix products, arithmetic and copies ran while one was open for 7% of the time, Pallas kernels for 24%

profile of v2, /device:TPU:0, one launch (start us, length us, event | category | flops | bytes accessed | tf_op | source)
XLA Modules:
  0.0 680.0 jit_solution(89194058127192100)
XLA Ops:
  20.1 9.6 %project.1 = (bf16[2048,1024]{1,0:T(8,128)(2,1)S(1)}, bf16[4,2048,128]{2,1,0:T(8,128)(2,1)S(1)}, bf16[2048,128]{1,0:T(8,128)(2,1)S(1)}, bf16[2048,256]{1,0:T(8,128)(2,1)S(1)}) custom-call(bf16[2048,1024]{1,0:T(8,128)(2,1)} %x_ref.5, bf16[1,1024]{1,0:T(2,128)(2,1)S(1)} %broadcast_in_dim.34.gain_ref, bf16[1024,256]{1,0:T(8,128)(2,1)S(1)} %copy-done.4, ...), custom_call_target="tpu_custom_call" | custom-call | flops 900000000 | tf_op jit(solution)/shard_map/project/pallas_call | solution.py:89
  31.8 13.9 %attend.2 = (bf16[2048,256]{1,0:T(8,128)(2,1)S(1)}, f32[2,8,4096]{2,1,0:T(8,128)S(1)}) custom-call(s32[1]{0:T(128)S(6)} %copy.68.prefix_ref, bf16[4,2048,128]{2,1,0:T(8,128)(2,1)S(1)} %get-tuple-element.97.q_ref, bf16[2048,128]{1,0:T(8,128)(2,1)S(1)} %get-tuple-element.98.k_ref, bf16[2048,256]{1,0:T(8,128)(2,1)S(1)} %get-tuple-element.99.v_ref), custom_call_target="tpu_custom_call" | custom-call | flops 1400000000 | tf_op jit(solution)/shard_map/attend/pallas_call | solution.py:156
  51.3 13.9 %attend.3 = (bf16[2048,256]{1,0:T(8,128)(2,1)S(1)}, f32[2,8,4096]{2,1,0:T(8,128)S(1)}) custom-call(s32[1]{0:T(128)S(6)} %copy.68.prefix_ref, bf16[4,2048,128]{2,1,0:T(8,128)(2,1)S(1)} %copy-done.55, bf16[2048,128]{1,0:T(8,128)(2,1)S(1)} %copy-done.60, bf16[2048,256]{1,0:T(8,128)(2,1)S(1)} %copy-done.57, ...), custom_call_target="tpu_custom_call", output_to_operand_aliasing={{0}: (4, {}), {1}: (5, {})} | custom-call | flops 1400000000 | tf_op jit(solution)/shard_map/attend/pallas_call | solution.py:156
  76.8 44.8 %collective-permute-done.5 = bf16[512,1024]{1,0:T(8,128)(2,1)S(1)} collective-permute-done((bf16[512,1024]{1,0:T(8,128)(2,1)}, bf16[512,1024]{1,0:T(8,128)(2,1)S(1)}, u32[]{:S(2)}, u32[]{:S(2)}) %collective-permute-start.5) | collective-permute-done | bytes 1048608 | tf_op jit(solution)/shard_map/ppermute | solution.py:579
  124.7 10.8 %collective-permute-start.6 = (bf16[512,1024]{1,0:T(8,128)(2,1)S(1)}, bf16[512,1024]{1,0:T(8,128)(2,1)S(1)}, u32[]{:S(2)}, u32[]{:S(2)}) collective-permute-start(bf16[512,1024]{1,0:T(8,128)(2,1)S(1)} %multiply_convert_fusion.refs_0_), channel_id=1, source_target_pairs={{0,8},{8,0},{16,24},{24,16},{1,9},{9,1},{17,25},{25,17},{2,10},{10... | collective-permute-start | bytes 3145736 | tf_op jit(solution)/shard_map/ppermute | solution.py:608
  138.2 20.0 %collective-permute-done.6.refs_0_ = bf16[512,1024]{1,0:T(8,128)(2,1)S(1)} collective-permute-done((bf16[512,1024]{1,0:T(8,128)(2,1)S(1)}, bf16[512,1024]{1,0:T(8,128)(2,1)S(1)}, u32[]{:S(2)}, u32[]{:S(2)}) %collective-permute-start.6) | collective-permute-done | bytes 1048608 | tf_op jit(solution)/shard_map/ppermute | solution.py:608
  167.1 5.3 pick.4
  173.1 5.3 pick.5
  179.8 14.2 %collective-permute-done.11.refs_2_ = bf16[512,1152]{1,0:T(8,128)(2,1)} collective-permute-done((bf16[512,1152]{1,0:T(8,128)(2,1)}, bf16[512,1152]{1,0:T(8,128)(2,1)}, u32[]{:S(2)}, u32[]{:S(2)}) %collective-permute-start.11) | collective-permute-done | bytes 1179680 | tf_op jit(solution)/shard_map/ppermute | solution.py:612
  194.0 22.5 %collective-permute-done.9.refs_0_ = bf16[512,1024]{1,0:T(8,128)(2,1)} collective-permute-done((bf16[512,1024]{1,0:T(8,128)(2,1)}, bf16[512,1024]{1,0:T(8,128)(2,1)}, u32[]{:S(2)}, u32[]{:S(2)}) %collective-permute-start.9) | collective-permute-done | bytes 1048608 | tf_op jit(solution)/shard_map/ppermute | solution.py:612
  216.4 7.1 %pick.6 = (bf16[8,128,1024]{2,1,0:T(8,128)(2,1)}, bf16[8,128,1024]{2,1,0:T(8,128)(2,1)}, f32[8,128,128]{2,1,0:T(8,128)}, f32[512,128]{1,0:T(8,128)S(1)}, f32[512,128]{1,0:T(8,128)S(1)}) custom-call(s32[9]{0:T(128)S(1)} %pad_add_fusion.shift_ref, bf16[512,1024]{1,0:T(8,128)(2,1)} %collective-permute-done.9.refs_0_, ...), custom_call_target="tpu_custom_call" | custom-call | flops 400000000 | tf_op jit(solution)/shard_map/pick/pallas_call | solution.py:306
  224.9 11.4 %collective-permute-done.12.refs_0_ = bf16[512,1024]{1,0:T(8,128)(2,1)} collective-permute-done((bf16[512,1024]{1,0:T(8,128)(2,1)}, bf16[512,1024]{1,0:T(8,128)(2,1)}, u32[]{:S(2)}, u32[]{:S(2)}) %collective-permute-start.12) | collective-permute-done | bytes 1048608 | tf_op jit(solution)/shard_map/ppermute | solution.py:616
  236.3 6.8 %pick.7 = (bf16[8,128,1024]{2,1,0:T(8,128)(2,1)}, bf16[8,128,1024]{2,1,0:T(8,128)(2,1)}, f32[8,128,128]{2,1,0:T(8,128)}, f32[512,128]{1,0:T(8,128)S(1)}, f32[512,128]{1,0:T(8,128)S(1)}) custom-call(s32[9]{0:T(128)S(1)} %pad_add_fusion.shift_ref, bf16[512,1024]{1,0:T(8,128)(2,1)} %collective-permute-done.12.refs_0_, ...), custom_call_target="tpu_custom_call" | custom-call | flops 400000000 | tf_op jit(solution)/shard_map/pick/pallas_call | solution.py:306
  244.6 38.4 %ffn.1 = (bf16[8,512,1024]{2,1,0:T(8,128)(2,1)}, bf16[8,512,1024]{2,1,0:T(8,128)(2,1)}, f32[8,512,128]{2,1,0:T(8,128)}, bf16[8,512,512]{2,1,0:T(8,128)(2,1)}, bf16[8,512,1024]{2,1,0:T(8,128)(2,1)}) custom-call(bf16[8,128,1024]{2,1,0:T(8,128)(2,1)} %get-tuple-element.111.refs_0_, bf16[8,128,1024]{2,1,0:T(8,128)(2,1)} %get-tuple-element.112.refs_1_, ...), custom_call_target="tpu_custom_call" | custom-call | flops 4000000000 | tf_op jit(solution)/shard_map/ffn/pallas_call | solution.py:369
  285.6 5.3 merge_back.2
  294.3 4.9 merge_back.3
  300.2 26.2 %wgrad.1 = bf16[2,4,3,4,1024,128]{5,4,3,2,1,0:T(8,128)(2,1)} custom-call(bf16[8,128,1024]{2,1,0:T(8,128)(2,1)} %get-tuple-element.111.refs_0_, bf16[8,128,1024]{2,1,0:T(8,128)(2,1)} %get-tuple-element.112.refs_1_, bf16[8,128,1024]{2,1,0:T(8,128)(2,1)} %get-tuple-element.115.refs_2_, bf16[8,128,1024]{2,1,0:T(8,128)(2,1)} %get-tuple-element.117.refs_3_, ...), custom_call_target="tpu_custom_call" | custom-call | flops 2600000000 | tf_op jit(solution)/shard_map/wgrad/pallas_call | solution.py:407
  330.8 20.5 %collective-permute-done.13 = bf16[512,1152]{1,0:T(8,128)(2,1)S(1)} collective-permute-done((bf16[512,1152]{1,0:T(8,128)(2,1)}, bf16[512,1152]{1,0:T(8,128)(2,1)S(1)}, u32[]{:S(2)}, u32[]{:S(2)}) %collective-permute-start.13) | collective-permute-done | bytes 1179680 | tf_op jit(solution)/shard_map/ppermute | solution.py:624
  352.8 5.0 collective-permute-start.17
  357.8 22.6 %collective-permute-done.17 = bf16[512,1152]{1,0:T(8,128)(2,1)S(1)} collective-permute-done((bf16[512,1152]{1,0:T(8,128)(2,1)S(1)}, bf16[512,1152]{1,0:T(8,128)(2,1)S(1)}, u32[]{:S(2)}, u32[]{:S(2)}) %collective-permute-start.17) | collective-permute-done | bytes 1179680 | tf_op jit(solution)/shard_map/ppermute | solution.py:636
  384.9 9.4 %merge_out.1 = (bf16[512,1024]{1,0:T(8,128)(2,1)S(1)}, bf16[512,1024]{1,0:T(8,128)(2,1)S(1)}, bf16[512,1024]{1,0:T(8,128)(2,1)S(1)}, bf16[512,1024]{1,0:T(8,128)(2,1)}) custom-call(s32[8]{0:T(128)S(1)} %iota_add_fusion.shift_ref, f32[512,128]{1,0:T(8,128)S(1)} %copy-done.37, f32[512,128]{1,0:T(8,128)S(1)} %copy-done.40, f32[512,128]{1,0:T(8,128)S(1)} %copy-done.43, ...), custom_call_target="tpu_custom_call" | custom-call | flops 1100000000 | tf_op jit(solution)/shard_map/merge_out/pallas_call | solution.py:490
  397.2 33.0 %collective-permute-done.18.refs_0_ = bf16[512,1024]{1,0:T(8,128)(2,1)} collective-permute-done((bf16[512,1024]{1,0:T(8,128)(2,1)S(1)}, bf16[512,1024]{1,0:T(8,128)(2,1)}, u32[]{:S(2)}, u32[]{:S(2)}) %collective-permute-start.18) | collective-permute-done | bytes 1048608 | tf_op jit(solution)/shard_map/ppermute | solution.py:579
  433.8 4.7 collective-permute-start.23
  455.0 6.3 collective-permute-done.23
  464.6 48.5 %attend_back.1 = bf16[2048,512]{1,0:T(8,128)(2,1)} custom-call(s32[1]{0:T(128)S(6)} %copy.68.prefix_ref, bf16[4,2048,128]{2,1,0:T(8,128)(2,1)} %copy-done.54, bf16[2048,128]{1,0:T(8,128)(2,1)S(1)} %copy-done.61, bf16[2048,256]{1,0:T(8,128)(2,1)S(1)} %copy-done.58, bf16[2048,256]{1,0:T(8,128)(2,1)S(1)} %get-tuple-element.106.att_ref.o_ref, ...), custom_call_target="tpu_custom_call" | custom-call | flops 4600000000 | tf_op jit(solution)/shard_map/attend_back/pallas_call | solution.py:239
  513.3 5.2 convolution_convert_fusion.3
  524.1 4.5 collective-permute-done.28
  543.0 36.6 %collective-permute-done.29 = bf16[2,512,1024]{2,1,0:T(8,128)(2,1)} collective-permute-done((bf16[2,512,1024]{2,1,0:T(8,128)(2,1)S(1)}, bf16[2,512,1024]{2,1,0:T(8,128)(2,1)}, u32[]{:S(2)}, u32[]{:S(2)}) %collective-permute-start.29) | collective-permute-done | bytes 2097184 | tf_op jit(solution)/shard_map/ppermute | solution.py:579
  582.3 58.1 %all-reduce.4.cloned.1.call-done = bf16[1616,512]{1,0:T(8,128)(2,1)} async-done(((bf16[1616,512]{1,0:T(8,128)(2,1)}), bf16[1616,512]{1,0:T(8,128)(2,1)}) %all-reduce.4.cloned.1.call-update) | async-done | bytes 1654800 | tf_op jit(solution)/shard_map/psum | solution.py:783
  640.5 4.7 convert_bitcast_fusion
  657.2 5.6 finish.2.refs_0_
  667.1 5.9 finish.3
  (300 shorter events, 133.2 us)
Async XLA Ops:
  7.2 237.4 %all-gather.3.cloned.1.call-start = ((), (), s32[]{:S(2)}) async-start(), calls=%async_computation.3 | async-start | bytes 28311552 | tf_op jit(solution)/shard_map/all_gather | solution.py:688
  11.1 508.7 %reduce-scatter.2.cloned.1.call-start = ((), (), s32[]{:S(2)}) async-start(), calls=%async_computation.1 | async-start | bytes 28311552 | tf_op jit(solution)/shard_map/reduce_scatter | solution.py:739
  12.4 33.3 %collective-permute-start = (bf16[512,1152]{1,0:T(8,128)(2,1)S(1)}, bf16[512,1152]{1,0:T(8,128)(2,1)S(1)}, u32[]{:S(2)}, u32[]{:S(2)}) collective-permute-start(bf16[512,1152]{1,0:T(8,128)(2,1)S(1)} %fusion.2.refs_1_), channel_id=1, source_target_pairs={{0,8},{8,0},{16,24},{24,16},{1,9},{9,1},{17,25},{25,17},{2,10},{10... | collective-permute-start | bytes 3538952 | tf_op jit(solution)/shard_map/ppermute | solution.py:608
  15.5 30.2 %collective-permute-start.1 = (bf16[512,1152]{1,0:T(8,128)(2,1)S(1)}, bf16[512,1152]{1,0:T(8,128)(2,1)}, u32[]{:S(2)}, u32[]{:S(2)}) collective-permute-start(bf16[512,1152]{1,0:T(8,128)(2,1)S(1)} %fusion.2.refs_1_), channel_id=1, source_target_pairs={{8,16},{16,8},{9,17},{17,9},{10,18},{18,10},{11,19},{19,11},{12,20... | collective-permute-start | bytes 3538952 | tf_op jit(solution)/shard_map/ppermute | solution.py:608
  45.8 19.5 %collective-permute-start.2 = (bf16[512,1152]{1,0:T(8,128)(2,1)S(1)}, bf16[512,1152]{1,0:T(8,128)(2,1)}, u32[]{:S(2)}, u32[]{:S(2)}) collective-permute-start(bf16[512,1152]{1,0:T(8,128)(2,1)S(1)} %collective-permute-done.refs_1_), channel_id=1, source_target_pairs={{8,16},{16,8},{9,17},{17,9},{10,18},{18,10},{11,19},{19,11},{12,20... | collective-permute-start | bytes 3538952 | tf_op jit(solution)/shard_map/ppermute | solution.py:612
  68.1 8.7 %collective-permute-start.3 = (bf16[512,1024]{1,0:T(8,128)(2,1)}, bf16[512,1024]{1,0:T(8,128)(2,1)}, u32[]{:S(2)}, u32[]{:S(2)}) collective-permute-start(bf16[512,1024]{1,0:T(8,128)(2,1)} %convolution_convert_fusion.2), channel_id=1, source_target_pairs={{0,1},{1,0},{2,3},{3,2},{4,5},{5,4},{6,7},{7,6},{8,9},{9,8},{10,11... | collective-permute-start | bytes 3145736 | tf_op jit(solution)/shard_map/ppermute | solution.py:579
  73.3 48.4 %collective-permute-start.5 = (bf16[512,1024]{1,0:T(8,128)(2,1)}, bf16[512,1024]{1,0:T(8,128)(2,1)S(1)}, u32[]{:S(2)}, u32[]{:S(2)}) collective-permute-start(bf16[512,1024]{1,0:T(8,128)(2,1)} %add_convert_fusion.9), channel_id=1, source_target_pairs={{0,2},{2,0},{1,3},{3,1},{4,6},{6,4},{5,7},{7,5},{8,10},{10,8},{9,1... | collective-permute-start | bytes 3145736 | tf_op jit(solution)/shard_map/ppermute | solution.py:579
  74.9 62.3 %collective-permute-start.8 = (bf16[512,1152]{1,0:T(8,128)(2,1)}, bf16[512,1152]{1,0:T(8,128)(2,1)S(1)}, u32[]{:S(2)}, u32[]{:S(2)}) collective-permute-start(bf16[512,1152]{1,0:T(8,128)(2,1)} %collective-permute-done.2.refs_3_), channel_id=1, source_target_pairs={{8,0},{16,24},{9,1},{17,25},{10,2},{18,26},{11,3},{19,27},{12,4},{... | collective-permute-start | bytes 3538952 | tf_op jit(solution)/shard_map/ppermute | solution.py:616
  124.7 33.5 %collective-permute-start.6 = (bf16[512,1024]{1,0:T(8,128)(2,1)S(1)}, bf16[512,1024]{1,0:T(8,128)(2,1)S(1)}, u32[]{:S(2)}, u32[]{:S(2)}) collective-permute-start(bf16[512,1024]{1,0:T(8,128)(2,1)S(1)} %multiply_convert_fusion.refs_0_), channel_id=1, source_target_pairs={{0,8},{8,0},{16,24},{24,16},{1,9},{9,1},{17,25},{25,17},{2,10},{10... | collective-permute-start | bytes 3145736 | tf_op jit(solution)/shard_map/ppermute | solution.py:608
  135.5 22.7 %collective-permute-start.7 = (bf16[512,1024]{1,0:T(8,128)(2,1)S(1)}, bf16[512,1024]{1,0:T(8,128)(2,1)}, u32[]{:S(2)}, u32[]{:S(2)}) collective-permute-start(bf16[512,1024]{1,0:T(8,128)(2,1)S(1)} %multiply_convert_fusion.refs_0_), channel_id=1, source_target_pairs={{8,16},{16,8},{9,17},{17,9},{10,18},{18,10},{11,19},{19,11},{12,20... | collective-permute-start | bytes 3145736 | tf_op jit(solution)/shard_map/ppermute | solution.py:608
  158.2 5.2 collective-permute-start.10
  160.8 33.1 %collective-permute-start.11 = (bf16[512,1152]{1,0:T(8,128)(2,1)}, bf16[512,1152]{1,0:T(8,128)(2,1)}, u32[]{:S(2)}, u32[]{:S(2)}) collective-permute-start(bf16[512,1152]{1,0:T(8,128)(2,1)} %collective-permute-done.1.refs_3_), channel_id=1, source_target_pairs={{8,0},{16,24},{9,1},{17,25},{10,2},{18,26},{11,3},{19,27},{12,4},{... | collective-permute-start | bytes 3538952 | tf_op jit(solution)/shard_map/ppermute | solution.py:612
  162.1 54.3 %collective-permute-start.9 = (bf16[512,1024]{1,0:T(8,128)(2,1)}, bf16[512,1024]{1,0:T(8,128)(2,1)}, u32[]{:S(2)}, u32[]{:S(2)}) collective-permute-start(bf16[512,1024]{1,0:T(8,128)(2,1)} %collective-permute-done.7.refs_1_), channel_id=1, source_target_pairs={{8,0},{16,24},{9,1},{17,25},{10,2},{18,26},{11,3},{19,27},{12,4},{... | collective-permute-start | bytes 3145736 | tf_op jit(solution)/shard_map/ppermute | solution.py:612
  163.4 72.9 %collective-permute-start.12 = (bf16[512,1024]{1,0:T(8,128)(2,1)}, bf16[512,1024]{1,0:T(8,128)(2,1)}, u32[]{:S(2)}, u32[]{:S(2)}) collective-permute-start(bf16[512,1024]{1,0:T(8,128)(2,1)} %collective-permute-done.10.refs_1_), channel_id=1, source_target_pairs={{8,0},{16,24},{9,1},{17,25},{10,2},{18,26},{11,3},{19,27},{12,4},{... | collective-permute-start | bytes 3145736 | tf_op jit(solution)/shard_map/ppermute | solution.py:616
  291.9 34.6 %collective-permute-start.15 = (bf16[512,1152]{1,0:T(8,128)(2,1)S(1)}, bf16[512,1152]{1,0:T(8,128)(2,1)}, u32[]{:S(2)}, u32[]{:S(2)}) collective-permute-start(bf16[512,1152]{1,0:T(8,128)(2,1)S(1)} %get-tuple-element.134), channel_id=1, source_target_pairs={{0,8},{24,16},{1,9},{25,17},{2,10},{26,18},{3,11},{27,19},{4,12},{... | collective-permute-start | bytes 3538952 | tf_op jit(solution)/shard_map/ppermute | solution.py:624
  326.5 314.0 %all-reduce.4.cloned.1.call-start = ((), (), s32[]{:S(2)}) async-start(), calls=%async_computation.2 | async-start | bytes 3309568 | tf_op jit(solution)/shard_map/psum | solution.py:783
  326.5 24.8 %collective-permute-start.13 = (bf16[512,1152]{1,0:T(8,128)(2,1)}, bf16[512,1152]{1,0:T(8,128)(2,1)S(1)}, u32[]{:S(2)}, u32[]{:S(2)}) collective-permute-start(bf16[512,1152]{1,0:T(8,128)(2,1)} %copy-done.11), channel_id=1, source_target_pairs={{0,8},{24,16},{1,9},{25,17},{2,10},{26,18},{3,11},{27,19},{4,12},{... | collective-permute-start | bytes 3538952 | tf_op jit(solution)/shard_map/ppermute | solution.py:624
  330.0 22.5 %collective-permute-start.16 = (bf16[512,1152]{1,0:T(8,128)(2,1)S(1)}, bf16[512,1152]{1,0:T(8,128)(2,1)S(1)}, u32[]{:S(2)}, u32[]{:S(2)}) collective-permute-start(bf16[512,1152]{1,0:T(8,128)(2,1)S(1)} %add_convert_fusion.3), channel_id=1, source_target_pairs={{8,16},{16,8},{9,17},{17,9},{10,18},{18,10},{11,19},{19,11},{12,20... | collective-permute-start | bytes 3538952 | tf_op jit(solution)/shard_map/ppermute | solution.py:632
  351.6 6.2 collective-permute-start.14
  352.8 27.6 %collective-permute-start.17 = (bf16[512,1152]{1,0:T(8,128)(2,1)S(1)}, bf16[512,1152]{1,0:T(8,128)(2,1)S(1)}, u32[]{:S(2)}, u32[]{:S(2)}) collective-permute-start(bf16[512,1152]{1,0:T(8,128)(2,1)S(1)} %add_convert_fusion.2), channel_id=1, source_target_pairs={{0,8},{8,0},{16,24},{24,16},{1,9},{9,1},{17,25},{25,17},{2,10},{10... | collective-permute-start | bytes 3538952 | tf_op jit(solution)/shard_map/ppermute | solution.py:636
  383.2 47.0 %collective-permute-start.18 = (bf16[512,1024]{1,0:T(8,128)(2,1)S(1)}, bf16[512,1024]{1,0:T(8,128)(2,1)}, u32[]{:S(2)}, u32[]{:S(2)}) collective-permute-start(bf16[512,1024]{1,0:T(8,128)(2,1)S(1)} %subtract_convert_fusion.refs_0_), channel_id=1, source_target_pairs={{0,2},{2,0},{1,3},{3,1},{4,6},{6,4},{5,7},{7,5},{8,10},{10,8},{9,1... | collective-permute-start | bytes 3145736 | tf_op jit(solution)/shard_map/ppermute | solution.py:579
  384.8 45.4 %collective-permute-start.19 = (bf16[512,1024]{1,0:T(8,128)(2,1)S(1)}, bf16[512,1024]{1,0:T(8,128)(2,1)S(1)}, u32[]{:S(2)}, u32[]{:S(2)}) collective-permute-start(bf16[512,1024]{1,0:T(8,128)(2,1)S(1)} %subtract_convert_fusion.refs_0_), channel_id=1, source_target_pairs={{0,1},{1,0},{2,3},{3,2},{4,5},{5,4},{6,7},{7,6},{8,9},{9,8},{10,11... | collective-permute-start | bytes 3145736 | tf_op jit(solution)/shard_map/ppermute | solution.py:579
  433.7 16.7 %collective-permute-start.20 = (bf16[512,1024]{1,0:T(8,128)(2,1)}, bf16[512,1024]{1,0:T(8,128)(2,1)}, u32[]{:S(2)}, u32[]{:S(2)}) collective-permute-start(bf16[512,1024]{1,0:T(8,128)(2,1)} %collective-permute-done.18.refs_0_), channel_id=1, source_target_pairs={{0,1},{1,0},{2,3},{3,2},{4,5},{5,4},{6,7},{7,6},{8,9},{9,8},{10,11... | collective-permute-start | bytes 3145736 | tf_op jit(solution)/shard_map/ppermute | solution.py:579
  433.8 27.5 %collective-permute-start.23 = (bf16[512,1024]{1,0:T(8,128)(2,1)}, bf16[512,1024]{1,0:T(8,128)(2,1)}, u32[]{:S(2)}, u32[]{:S(2)}) collective-permute-start(bf16[512,1024]{1,0:T(8,128)(2,1)} %get-tuple-element.152), channel_id=1, source_target_pairs={{0,8},{24,16},{1,9},{25,17},{2,10},{26,18},{3,11},{27,19},{4,12},{... | collective-permute-start | bytes 3145736 | tf_op jit(solution)/shard_map/ppermute | solution.py:624
  441.3 6.8 %collective-permute-start.22 = (bf16[80,512]{1,0:T(8,128)(2,1)S(1)}, bf16[80,512]{1,0:T(8,128)(2,1)S(1)}, u32[]{:S(2)}, u32[]{:S(2)}) collective-permute-start(bf16[80,512]{1,0:T(8,128)(2,1)S(1)} %add.141), channel_id=1, source_target_pairs={{0,2},{2,0},{1,3},{3,1},{4,6},{6,4},{5,7},{7,5},{8,10},{10,8},{9,1... | collective-permute-start | bytes 245768 | tf_op jit(solution)/shard_map/ppermute | solution.py:579
  448.2 71.7 %collective-permute-start.25 = (bf16[512,1024]{1,0:T(8,128)(2,1)}, bf16[512,1024]{1,0:T(8,128)(2,1)}, u32[]{:S(2)}, u32[]{:S(2)}) collective-permute-start(bf16[512,1024]{1,0:T(8,128)(2,1)} %copy-done.22), channel_id=1, source_target_pairs={{0,8},{24,16},{1,9},{25,17},{2,10},{26,18},{3,11},{27,19},{4,12},{... | collective-permute-start | bytes 3145736 | tf_op jit(solution)/shard_map/ppermute | solution.py:624
  463.8 56.0 %collective-permute-start.24 = (bf16[512,1024]{1,0:T(8,128)(2,1)}, bf16[512,1024]{1,0:T(8,128)(2,1)S(1)}, u32[]{:S(2)}, u32[]{:S(2)}) collective-permute-start(bf16[512,1024]{1,0:T(8,128)(2,1)} %add_convert_fusion.8), channel_id=1, source_target_pairs={{8,16},{16,8},{9,17},{17,9},{10,18},{18,10},{11,19},{19,11},{12,20... | collective-permute-start | bytes 3145736 | tf_op jit(solution)/shard_map/ppermute | solution.py:632
  531.8 47.8 %collective-permute-start.29 = (bf16[2,512,1024]{2,1,0:T(8,128)(2,1)S(1)}, bf16[2,512,1024]{2,1,0:T(8,128)(2,1)}, u32[]{:S(2)}, u32[]{:S(2)}) collective-permute-start(bf16[2,512,1024]{2,1,0:T(8,128)(2,1)S(1)} %add_convert_fusion.1), channel_id=1, source_target_pairs={{0,2},{2,0},{1,3},{3,1},{4,6},{6,4},{5,7},{7,5},{8,10},{10,8},{9,1... | collective-permute-start | bytes 6291464 | tf_op jit(solution)/shard_map/ppermute | solution.py:579
  536.4 111.8 %collective-permute-start.26 = (bf16[512,1024]{1,0:T(8,128)(2,1)}, bf16[512,1024]{1,0:T(8,128)(2,1)}, u32[]{:S(2)}, u32[]{:S(2)}) collective-permute-start(bf16[512,1024]{1,0:T(8,128)(2,1)} %add_convert_fusion.7), channel_id=1, source_target_pairs={{8,16},{16,8},{9,17},{17,9},{10,18},{18,10},{11,19},{19,11},{12,20... | collective-permute-start | bytes 3145736 | tf_op jit(solution)/shard_map/ppermute | solution.py:632
  539.4 108.8 %collective-permute-start.27 = (bf16[512,1024]{1,0:T(8,128)(2,1)}, bf16[512,1024]{1,0:T(8,128)(2,1)}, u32[]{:S(2)}, u32[]{:S(2)}) collective-permute-start(bf16[512,1024]{1,0:T(8,128)(2,1)} %add_convert_fusion.6), channel_id=1, source_target_pairs={{0,8},{8,0},{16,24},{24,16},{1,9},{9,1},{17,25},{25,17},{2,10},{10... | collective-permute-start | bytes 3145736 | tf_op jit(solution)/shard_map/ppermute | solution.py:636
  640.5 26.7 %collective-permute-start.30 = (bf16[2,512,1024]{2,1,0:T(8,128)(2,1)S(1)}, bf16[2,512,1024]{2,1,0:T(8,128)(2,1)}, u32[]{:S(2)}, u32[]{:S(2)}) collective-permute-start(bf16[2,512,1024]{2,1,0:T(8,128)(2,1)S(1)} %add_convert_fusion), channel_id=1, source_target_pairs={{0,1},{1,0},{2,3},{3,2},{4,5},{5,4},{6,7},{7,6},{8,9},{9,8},{10,11... | collective-permute-start | bytes 6291464 | tf_op jit(solution)/shard_map/ppermute | solution.py:579
  655.7 10.9 %collective-permute-start.32 = (f32[8,128]{1,0:T(8,128)S(1)}, f32[8,128]{1,0:T(8,128)S(1)}, u32[]{:S(2)}, u32[]{:S(2)}) collective-permute-start(f32[8,128]{1,0:T(8,128)S(1)} %fusion.45), channel_id=1, source_target_pairs={{0,2},{2,0},{1,3},{3,1},{4,6},{6,4},{5,7},{7,5},{8,10},{10,8},{9,1... | collective-permute-start | bytes 12296 | tf_op jit(solution)/shard_map/ppermute | solution.py:579
  (91 other events, 741.9 us)
Sparse Core Ops, SparseCore 0:
  11.2 149.3 all-gather.2
  326.6 180.9 reduce-scatter.1
  533.5 106.9 all-reduce.3

commit v3 on v2

--- a/solution.py
+++ b/solution.py
@@ -90,8 +90,7 @@
         project_kernel, grid=(L // B,),
         in_specs=[rows(D), full(gain), full(wq), full(wk), full(wv), rows(128), rows(128)],
         out_specs=[rows(D), pl.BlockSpec((4, B, 128), lambda i: (0, i, 0)), rows(128), rows(256)],
-        out_shape=[jax.ShapeDtypeStruct((L, D), bf16), jax.ShapeDtypeStruct((4, L, 128), bf16),
-                   jax.ShapeDtypeStruct((L, 128), bf16), jax.ShapeDtypeStruct((L, 256), bf16)],
+        out_shape=[pltpu.HBM((L, D), bf16), pltpu.HBM((4, L, 128), bf16), pltpu.HBM((L, 128), bf16), pltpu.HBM((L, 256), bf16)],
         compiler_params=pltpu.CompilerParams(vmem_limit_bytes=40 << 20),
         cost_estimate=busy(9),
         name="project",
@@ -164,7 +163,7 @@
             out_specs=[pl.BlockSpec((bq, 128), lambda i, p: (i, kv)),
                        pl.BlockSpec((1, 8, 2 * bq), lambda i, p: (kv, 0, i))],
             scratch_shapes=[pltpu.VMEM((2 * bq, L), f32)]),
-        out_shape=[jax.ShapeDtypeStruct((L, 256), bf16), jax.ShapeDtypeStruct((2, 8, 2 * L), f32)],
+        out_shape=[pltpu.HBM((L, 256), bf16), pltpu.HBM((2, 8, 2 * L), f32)],
         input_output_aliases={4 + i: i for i in range(len(before))},
         compiler_params=pltpu.CompilerParams(vmem_limit_bytes=48 << 20),
         cost_estimate=busy(14),
@@ -173,7 +172,7 @@
 
 
 def attend_back_kernel(bq, bk, prefix_ref, q_ref, k_ref, v_ref, o_ref, do_ref, lse_ref, cos_ref, sin_ref, cosa_ref, sina_ref,
-                       out_ref, dk_acc, dv_acc):
+                       out_ref, dk_acc, dv_acc, dq_acc):
     i = pl.program_id(0)
     start = i * bq
     prefix = prefix_ref[0]
@@ -189,6 +188,7 @@
         dk_acc[...] = jnp.zeros_like(dk_acc)
         dv_acc[...] = jnp.zeros_like(dv_acc)
 
+    heads = []
     for kv in range(2):
         q = jnp.concatenate([q_ref[2 * kv], q_ref[2 * kv + 1]], 0)
         mine = low if kv == 0 else ~low
@@ -200,25 +200,32 @@
         one = jnp.sum(jnp.where(low, prod, 0.0), -1, keepdims=True)
         two = jnp.sum(jnp.where(low, 0.0, prod), -1, keepdims=True)
         center = jnp.broadcast_to(jnp.concatenate([one, two], 0), (rows, 128)).T[:1]
-        lse = lse_ref[kv, :1, :]
-
-        def step(j, dq, mask):
-            off = pl.multiple_of(j * bk, bk)
-            kb = k_ref[pl.ds(off, bk), :]
+        heads.append((q, do, center, lse_ref[kv, :1, :]))
+    dq_acc[...] = jnp.zeros_like(dq_acc)
+
+    def step(j, _, mask):
+        off = pl.multiple_of(j * bk, bk)
+        kb = k_ref[pl.ds(off, bk), :]
+        vb = v_ref[pl.ds(off, bk), :128]
+        dvs, dks = [], []
+        for kv, (q, do, center, lse) in enumerate(heads):
             s = lax.dot_general(kb, q, NT, preferred_element_type=f32)
+            dp = lax.dot_general(vb, do, NT, preferred_element_type=f32)
             if mask:
                 s = jnp.where(off + lax.broadcasted_iota(jnp.int32, (bk, rows), 0) <= limit, s, -1e30)
             p = jnp.exp(s - lse)
-            dp = lax.dot_general(v_ref[pl.ds(off, bk), :128], do, NT, preferred_element_type=f32)
             ds = (p * (dp - center)).astype(bf16)
-            dv_acc[pl.ds(off, bk), :] += jnp.dot(p.astype(bf16), do, preferred_element_type=f32)
-            dk_acc[pl.ds(off, bk), :] += jnp.dot(ds, q, preferred_element_type=f32)
-            return dq + lax.dot_general(ds, kb, TN, preferred_element_type=f32)
-
-        dq = jnp.zeros((rows, 128), f32)
-        dq = lax.fori_loop(0, full_blocks, functools.partial(step, mask=False), dq)
-        dq = lax.fori_loop(full_blocks, all_blocks, functools.partial(step, mask=True), dq)
-        dq = dq * HD ** (-0.5)
+            dvs.append(jnp.dot(p.astype(bf16), do, preferred_element_type=f32))
+            dks.append(jnp.dot(ds, q, preferred_element_type=f32))
+            dq_acc[kv] += lax.dot_general(ds, kb, TN, preferred_element_type=f32)
+        dv_acc[pl.ds(off, bk), :] += dvs[0] + dvs[1]
+        dk_acc[pl.ds(off, bk), :] += dks[0] + dks[1]
+        return 0
+
+    lax.fori_loop(0, full_blocks, functools.partial(step, mask=False), 0)
+    lax.fori_loop(full_blocks, all_blocks, functools.partial(step, mask=True), 0)
+    for kv in range(2):
+        dq = dq_acc[kv] * HD ** (-0.5)
         one, two = dq[:bq], dq[bq:]
         if kv == 0:
             merged = jnp.where(low, one, pltpu.roll(two, HD, 1))
@@ -248,7 +255,7 @@
                       pl.BlockSpec((bq, 128), lambda i, p: (i, 0)),
                       pl.BlockSpec((bq, 128), lambda i, p: (i, 0)), fullL, fullL],
             out_specs=pl.BlockSpec((L, 512), lambda i, p: (0, 0)),
-            scratch_shapes=[pltpu.VMEM((L, 128), f32), pltpu.VMEM((L, 128), f32)]),
+            scratch_shapes=[pltpu.VMEM((L, 128), f32), pltpu.VMEM((L, 128), f32), pltpu.VMEM((2, 2 * bq, 128), f32)]),
         out_shape=jax.ShapeDtypeStruct((L, 512), bf16),
         compiler_params=pltpu.CompilerParams(vmem_limit_bytes=48 << 20),
         cost_estimate=busy(46),
@@ -319,7 +326,8 @@
 
 def ffn_kernel(n, blocks, *refs):
     rows_refs, dy_refs, gs_refs = refs[:n], refs[n : 2 * n], refs[2 * n : 3 * n]
-    w_ref, eout_ref, drows_ref, dgs_ref, act_ref, dgu_ref = refs[3 * n :]
+    w_ref = refs[3 * n]
+    eout_ref, drows_ref, dgs_ref, act_ref, dgu_ref = refs[-5:]
     cap, D = rows_refs[0].shape[1:]
     M = n * cap
     rows = jnp.concatenate([r[0] for r in rows_refs], 0)
@@ -356,64 +364,71 @@
     dgs_ref[0] = jnp.broadcast_to(dgs, (M, 128))
 
 
-def ffn(picked, weights):
+def ffn(picked, weights, groups, before=()):
     n = len(picked)
     total, cap, D = picked[0][0].shape
-    groups, blocks, _, E, _, F = weights.shape
+    _, blocks, _, E, _, F = weights.shape
     H = blocks * F
     M = n * cap
-    spec = lambda w: pl.BlockSpec((1, cap, w), lambda e: (e, 0, 0))
-    outs = lambda w: pl.BlockSpec((1, M, w), lambda e: (e, 0, 0))
-    wsp = pl.BlockSpec((1, blocks, 3, 1, D, F), lambda e: (e // E, 0, 0, e % E, 0, 0))
-    sh = lambda w, t: jax.ShapeDtypeStruct((total, M, w), t)
+    first = groups[0] * E
+    spec = lambda w: pl.BlockSpec((1, cap, w), lambda e: (e + first, 0, 0))
+    outs = lambda w: pl.BlockSpec((1, M, w), lambda e: (e + first, 0, 0))
+    wsp = pl.BlockSpec((1, blocks, 3, 1, D, F), lambda e: ((e + first) // E, 0, 0, (e + first) % E, 0, 0))
+    sh = lambda w, t: pltpu.HBM((total, M, w), t)
+    operands = [p[i] for i in range(3) for p in picked] + [weights]
     return pl.pallas_call(
-        functools.partial(ffn_kernel, n, blocks), grid=(total,),
-        in_specs=[spec(D)] * (2 * n) + [spec(128)] * n + [wsp],
+        functools.partial(ffn_kernel, n, blocks), grid=(len(groups) * E,),
+        in_specs=[spec(D)] * (2 * n) + [spec(128)] * n + [wsp] + [pl.BlockSpec(memory_space=pl.ANY)] * len(before),
         out_specs=[outs(D), outs(D), outs(128), outs(H), outs(2 * H)],
         out_shape=[sh(D, bf16), sh(D, bf16), sh(128, f32), sh(H, bf16), sh(2 * H, bf16)],
+        input_output_aliases={len(operands) + i: i for i in range(len(before))},
         compiler_params=pltpu.CompilerParams(vmem_limit_bytes=56 << 20),
-        cost_estimate=busy(40),
+        cost_estimate=busy(12 * len(groups)),
         name="ffn",
-    )(*[p[i] for i in range(3) for p in picked], weights)
-
-
-def wgrad_kernel(n, blocks, *refs):
+    )(*operands, *before)
+
+
+def wgrad_kernel(n, halves, blocks, *refs):
     rows_refs, dy_refs, gs_refs = refs[:n], refs[n : 2 * n], refs[2 * n : 3 * n]
-    act_ref, dgu_ref, out_ref = refs[3 * n :]
+    act_refs, dgu_refs, out_ref = refs[3 * n : 3 * n + halves], refs[3 * n + halves : 3 * n + 2 * halves], refs[-1]
     rows = jnp.concatenate([r[0] for r in rows_refs], 0)
     dy = jnp.concatenate([r[0] for r in dy_refs], 0)
     gs = jnp.concatenate([r[0] for r in gs_refs], 0)
     dout = (dy.astype(f32) * gs[:, :1]).astype(bf16)
-    F = act_ref.shape[2] // blocks
+    F = act_refs[0].shape[2] // blocks
     for b in range(blocks):
-        dgu = dgu_ref[0, :, b * 2 * F : (b + 1) * 2 * F]
+        dgu = jnp.concatenate([r[0, :, b * 2 * F : (b + 1) * 2 * F] for r in dgu_refs], 0)
         g = lax.dot_general(rows, dgu, TN, preferred_element_type=f32).astype(bf16)
         out_ref[0, b, 0, 0] = g[:, :F]
         out_ref[0, b, 1, 0] = g[:, F:]
     for pair in range(0, blocks, 2):
-        gd = lax.dot_general(dout, act_ref[0, :, pair * F : (pair + 2) * F], TN, preferred_element_type=f32).astype(bf16)
+        act = jnp.concatenate([r[0, :, pair * F : (pair + 2) * F] for r in act_refs], 0)
+        gd = lax.dot_general(dout, act, TN, preferred_element_type=f32).astype(bf16)
         out_ref[0, pair, 2, 0] = gd[:, :F]
         out_ref[0, pair + 1, 2, 0] = gd[:, F:]
 
 
-def wgrad(picked, act, dgu, blocks, groups):
+def wgrad(picked, acts, dgus, blocks, groups, group, before=()):
     n = len(picked)
     total, cap, D = picked[0][0].shape
-    M, H = act.shape[1:]
+    H = acts[0].shape[2]
     F = H // blocks
     E = total // groups
-    spec = lambda w: pl.BlockSpec((1, cap, w), lambda e: (e, 0, 0))
-    wide = lambda w: pl.BlockSpec((1, M, w), lambda e: (e, 0, 0))
+    spec = lambda w: pl.BlockSpec((1, cap, w), lambda e: (e + group * E, 0, 0))
+    wide = lambda a: pl.BlockSpec((1,) + a.shape[1:], lambda e: (e + group * E, 0, 0))
+    operands = [*[p[i] for i in range(3) for p in picked], *acts, *dgus]
     return pl.pallas_call(
-        functools.partial(wgrad_kernel, n, blocks),
-        grid=(total,),
-        in_specs=[spec(D)] * (2 * n) + [spec(128)] * n + [wide(H), wide(2 * H)],
-        out_specs=pl.BlockSpec((1, blocks, 3, 1, D, F), lambda e: (e // E, 0, 0, e % E, 0, 0)),
-        out_shape=jax.ShapeDtypeStruct((groups, blocks, 3, E, D, F), bf16),
+        functools.partial(wgrad_kernel, n, len(acts), blocks),
+        grid=(E,),
+        in_specs=[spec(D)] * (2 * n) + [spec(128)] * n + [wide(a) for a in (*acts, *dgus)]
+        + [pl.BlockSpec(memory_space=pl.ANY)] * len(before),
+        out_specs=pl.BlockSpec((1, blocks, 3, 1, D, F), lambda e: (group, 0, 0, e, 0, 0)),
+        out_shape=pltpu.HBM((groups, blocks, 3, E, D, F), bf16),
+        input_output_aliases={len(operands) + i: i for i in range(len(before))},
         compiler_params=pltpu.CompilerParams(vmem_limit_bytes=56 << 20),
-        cost_estimate=busy(26),
+        cost_estimate=busy(13),
         name="wgrad",
-    )(*[p[i] for i in range(3) for p in picked], act, dgu)
+    )(*operands, *before)
 
 
 def hot_columns(code, shift, cap):
@@ -443,11 +458,11 @@
             outs[source][:, D:] = gates.astype(bf16)
 
 
-def merge_back(shift, codes, first, drows, dgs, cap):
+def merge_back(shift, codes, drows, dgs, cap):
     n = len(codes)
     R, W = codes[0].shape
     E, _, D = drows.shape
-    part = lambda w: pl.BlockSpec((E, cap, w), lambda i: (0, i + first, 0))
+    part = lambda w: pl.BlockSpec((E, cap, w), lambda i: (0, i, 0))
     whole = lambda w: pl.BlockSpec((R, w), lambda i: (0, 0))
     return pl.pallas_call(
         functools.partial(merge_back_kernel, n, E, cap),
@@ -671,6 +686,10 @@
     local = w_gate.shape[0]
     cap = own_rows * TOPK // EXPERTS
 
+    own_weights = jnp.stack([w_gate, w_up, w_down.transpose(0, 2, 1)])
+    weights = lax.all_gather(own_weights, ("y", "x", "c"), axis=0, tiled=False)
+    weights = weights.reshape((groups, shards) + own_weights.shape)
+
     expert_ids = jnp.arange(EXPERTS, dtype=jnp.int32)
     member = jnp.sum((routes[:, :, None] == expert_ids[None, None, :]).astype(f32), 1)
     priority = fill_order[0]
@@ -684,9 +703,6 @@
     shift = z * groups * local + jnp.arange(groups * local, dtype=jnp.int32)
     shift_end = jnp.concatenate([shift, at_end.astype(jnp.int32)[None]])
 
-    own_weights = jnp.stack([w_gate, w_up, w_down.transpose(0, 2, 1)])
-    weights = lax.all_gather(own_weights, ("y", "x", "c"), axis=0, tiled=False)
-    weights = weights.reshape((groups, shards) + own_weights.shape)
 
     cos, sin = wide_tables(length)
     normed_one, query, key, value = project(tokens, gain_attn[None], w_query, w_key, w_value, cos, sin)
@@ -697,45 +713,59 @@
     attended, side_far = hold(attended, side_far)
     side_last = line_third(side_far)
 
-
     def out_block(place):
         rows = lax.dynamic_slice_in_dim(attended, place * own_rows, own_rows, 0)
         return jnp.dot(rows, w_out, preferred_element_type=f32)
 
     far_sum = out_block(rank ^ 2) + swap(out_block(rank ^ 3).astype(bf16), "c").astype(f32)
-    far_got = swap(far_sum.astype(bf16), "x").astype(f32)
-    near_got = swap(out_block(rank ^ 1).astype(bf16), "c").astype(f32)
+    far_got = swap(far_sum.astype(bf16), "x")
+    near_sum = out_block(rank) + swap(out_block(rank ^ 1).astype(bf16), "c").astype(f32)
+    near_sum, far_got, side_relay, side_last = hold(near_sum, far_got, side_relay, side_last)
     x_rows = lax.dynamic_slice_in_dim(tokens, rank * own_rows, own_rows, 0).astype(f32)
-    hidden_in = x_rows + out_block(rank) + near_got + far_got
+    hidden_in = x_rows + near_sum + far_got.astype(f32)
     rms_two = lax.rsqrt(jnp.mean(hidden_in * hidden_in, -1, keepdims=True) + EPSILON)
     gain_two = gain_moe.astype(f32)
     normed_two = (hidden_in * rms_two * gain_two).astype(bf16)
 
     near, across = line_first(normed_two)
-    near, across, side_last = hold(near, across, side_last)
+
+    def pick_of(rows, sides):
+        return pick(shift_end, rows, sides, router_wide, cap)
+
+    pick_own = pick_of((normed_two,), (side_own,))
+    near, across, *pick_own = hold(near, across, *pick_own)
     far, relay = line_second(near, across)
+    close = [pick_own, pick_of((near,), (side_near,))]
+    half_close = ffn(close, weights, (0,))
+    far, relay, *half_close = hold(far, relay, *half_close)
     last = line_third(far)
-    picked = [
-        pick(shift_end, rows, sides, router_wide, cap)
-        for rows, sides in (
-            ((normed_two,), (side_own,)),
-            ((near,), (side_near,)),
-            ((relay, far), (side_relay, side_far)),
-            ((last, across), (side_last, side_across)),
-        )
-    ]
+    done_close = ffn(close, weights, (1,), half_close)
+    apart = [pick_of((relay, far), (side_relay, side_far))]
+    last, *done_close = hold(last, *done_close)
+    apart.append(pick_of((last, across), (side_last, side_across)))
+    done_apart = ffn(apart, weights, (0, 1))
+    picked = close + apart
     gates = [p[3] for p in picked]
     codes = [p[4] for p in picked]
-    expert_out, rows_grad, gate_slots, act, hidden_grads = ffn(picked, weights)
-    far_back = merge_back(shift, codes[2:], 2, rows_grad, gate_slots, cap)
-    late_grad, *far_back = hold(rows_grad, *far_back)
-    back = [*merge_back(shift, codes[:2], 0, late_grad, gate_slots, cap), *far_back]
-    back_out = line_out(back)
-    late_act, *_ = hold(act, *back)
-    parts = wgrad(picked, late_act, hidden_grads, shards, groups)
-    back_far_out, parts = hold(back_out[0], parts)
-    back_out = (back_far_out, back_out[1])
-    back_own = line_sum(back, *back_out)
+    far_back = merge_back(shift, codes[2:], done_apart[1], done_apart[2], cap)
+    back = [*merge_back(shift, codes[:2], done_close[1], done_close[2], cap), *far_back]
+    back_end_far, back_end = line_out(back)
+    late_act, *_ = hold(done_apart[3], *back)
+    used = (done_close[3], late_act), (done_close[4], done_apart[4]), shards, groups
+    parts = wgrad(picked, *used, 0)
+    parts = wgrad(picked, *used, 1, (parts,))
+    back_end_far, parts = hold(back_end_far, parts)
+    across_far = line_over(back[2], back_end_far)
+    across = line_over(back[3], back_end)
+    late_close, late_apart, _ = hold(done_close[0], done_apart[0], across_far)
+    out_parts = [
+        *merge_out(shift, codes[:2], gates[:2], late_close, cap),
+        *merge_out(shift, codes[2:], gates[2:], late_apart, cap),
+    ]
+    got = line_in(back[1], across_far)
+    got, across, *out_parts = hold(got, across, *out_parts)
+    back_own = back[0].astype(f32) + across.astype(f32) + got.astype(f32)
+    out_end_far, out_end = line_out(out_parts)
     part_sum = lax.psum_scatter(
         parts.reshape((groups * shards,) + parts.shape[2:]), ("y", "x", "c"), scatter_dimension=0, tiled=False
     )
@@ -758,34 +788,29 @@
         - hidden_in * rms_two**3 * jnp.mean(scaled_two * hidden_in, -1, keepdims=True)
     ).astype(bf16)
     small = jnp.concatenate([router_part, gain_two_part[None], jnp.zeros((7, width), f32)], 0)
-    small = total_over(small.reshape(-1, width // 2).astype(bf16), ("c", "x"))
+    small = small.reshape(-1, width // 2).astype(bf16)
     hidden_over_x = swap(hidden_grad, "x")
-    late_out, *_ = hold(expert_out, hidden_grad)
-    out_parts = merge_out(shift, codes, gates, late_out, cap)
-    hidden_over_x, *out_parts = hold(hidden_over_x, *out_parts)
-    out_end_far, out_end = line_out(out_parts)
     rank_row = rank.astype(jnp.int32)[None]
     near_done = spread(rank_row, 0, [hidden_grad, swap(hidden_grad, "c")], attended, w_out)
-    hidden_over_x, *near_done = hold(hidden_over_x, *near_done)
+    *near_done, out_end_far, out_end = hold(*near_done, out_end_far, out_end)
+    out_two, out_three = add_low(out_parts[2], out_end_far), add_low(out_parts[3], out_end)
+    hidden_over_x, out_two, out_three, *near_done = hold(hidden_over_x, out_two, out_three, *near_done)
     hidden_all, attended_grad, out_grad = spread(
         rank_row, 2, [hidden_over_x, swap(hidden_over_x, "c")], attended, w_out, near_done
     )
-    attended_grad, small, out_low, out_end_far = hold(attended_grad, small, out_grad.astype(bf16), out_end_far)
-    out_far = line_over(out_parts[2], out_end_far)
+    attended_grad, small, out_low = hold(attended_grad, small, out_grad.astype(bf16))
+    out_far, out_across = (lax.ppermute(part, "z", MIDDLE) for part in (out_two, out_three))
     heads_back = attend_back(
         prefix, query, key, value, attended, attended_grad, log_total, cos, sin, BQ, BK_BACK
     )
     heads_in = jnp.concatenate([w_query, w_key, w_value], 1)
     heads_grad = jnp.einsum("id,ih->dh", normed_one, heads_back, preferred_element_type=f32)
     low = jnp.concatenate([heads_grad.astype(bf16), out_low.reshape(-1, heads_grad.shape[1]), small], 0)
-    heads_back, low, part_sum, out_far, out_end = hold(heads_back, low, part_sum, out_far, out_end)
-
-    low_all = lax.psum(low, ("z", "y"))
-
-    out_across = line_over(out_parts[3], out_end)
+    low = jnp.pad(low, ((0, -low.shape[0] % 1024), (0, 0)))
+    heads_back, low, part_sum, out_far, out_across = hold(heads_back, low, part_sum, out_far, out_across)
     out_got = line_in(out_parts[1], out_far)
-    moe_own = out_parts[0].astype(f32) + out_across.astype(f32) + out_got.astype(f32)
-    block_output = (hidden_in + moe_own).astype(bf16)
+
+    low_part = lax.psum_scatter(low, ("z", "y"), scatter_dimension=0, tiled=True)
 
     by_core = heads_back.reshape(shards // 2, 2, own_rows, -1)
 
@@ -795,8 +820,11 @@
 
     from_core = swap(rows_of(1 - c).astype(bf16), "c")
     core_sum = (rows_of(c) + from_core.astype(f32)).astype(bf16)
-    chip_sum = (core_sum.astype(f32) + swap(core_sum, "x").astype(f32)).astype(bf16)
-    chip_sum, low_all = hold(chip_sum, low_all)
+    core_got, low_part, out_got = hold(swap(core_sum, "x"), low_part, out_got)
+    moe_own = out_parts[0].astype(f32) + out_across.astype(f32) + out_got.astype(f32)
+    block_output = (hidden_in + moe_own).astype(bf16)
+    low_all = lax.all_gather(low_part, ("z", "y"), axis=0, tiled=True)
+    chip_sum = (core_sum.astype(f32) + core_got.astype(f32)).astype(bf16)
     other_sum = swap(chip_sum, "c")
     core = c.astype(jnp.int32)[None]
     gain_row = gain_attn[None]
@@ -805,27 +833,27 @@
     input_grad = finish(
         1 - core, other_sum.reshape(-1, width), tokens, hidden_all, gain_row, own_rows, (input_grad,)
     )
+    expert_grads = part_sum[0].astype(f32), part_sum[1].astype(f32), part_sum[2].astype(f32).transpose(0, 2, 1)
+    low_all, input_grad, block_output, *expert_grads = hold(low_all, input_grad, block_output, *expert_grads)
     low_all = low_all.astype(f32)
     split = width + out_grad.size // low.shape[1]
     heads_total = low_all[:width]
     out_total = low_all[width:split].reshape(out_grad.shape)
-    small_total = low_all[split:].reshape(-1, width)
     gain_one_part = jnp.sum(heads_total * heads_in.astype(f32), 1) / gain_attn.astype(f32)
-    gain_one_total = total_over(gain_one_part.reshape(8, -1), ("c", "x")).reshape(-1)
+    rest = jnp.concatenate([low_all[split : split + 2 * (EXPERTS + 8)].reshape(-1, width), gain_one_part[None], jnp.zeros((7, width), f32)], 0)
+    rest = total_over(rest.astype(bf16), ("c", "x")).astype(f32)
     cut = w_query.shape[1]
     return (
         block_output,
         input_grad,
-        gain_one_total,
+        rest[EXPERTS + 8],
         heads_total[:, :cut],
         heads_total[:, cut : cut + w_key.shape[1]],
         heads_total[:, cut + w_key.shape[1] :],
         out_total,
-        small_total[EXPERTS],
-        small_total[:EXPERTS].T,
-        part_sum[0].astype(f32),
-        part_sum[1].astype(f32),
-        part_sum[2].astype(f32).transpose(0, 2, 1),
+        rest[EXPERTS],
+        rest[:EXPERTS].T,
+        *expert_grads,
     )
 
 

time: 689 us -> 646 us (0.938)
  waiting for transfers between devices: 303 us -> 260 us
  starting transfers between devices: 58.9 us -> 46.6 us
    ppermute x13 -> x11, waiting for transfers between devices: 127 us -> 13.5 us  [swap(): return lax.ppermute(x, axis, [(i, i ^ bit) for i in range(count)])]
    psum x1 -> x0, waiting for transfers between devices: 58.1 us -> none  [per_device_fast(): low_all = lax.psum(low, ('z', 'y'))]
    all_gather x0 -> x1, waiting for transfers between devices: none -> 29.5 us  [per_device_fast(): low_all = lax.all_gather(low_part, ('z', 'y'), axis=0, tiled=True)]
    ppermute x2, waiting for transfers between devices: 22.6 us -> 49.4 us  [line_in(): return lax.ppermute(add_low(part, across_far), 'z', NEAR)]
    ppermute x2, waiting for transfers between devices: 20.5 us -> 42.3 us  [line_out(): lax.ppermute(parts[2], 'z', FROM_ENDS)]
    reduce_scatter x0 -> x1, waiting for transfers between devices: none -> 20.8 us  [per_device_fast(): lax.psum_scatter(low, ('z', 'y'), scatter_dimension=0, tiled=True)]
    ppermute x2, waiting for transfers between devices: 11.4 us -> 26.6 us  [line_third(): return lax.ppermute(across_far, 'z', TO_ENDS)]
    ppermute x2, waiting for transfers between devices: 6.28 us -> 18.5 us  [line_out(): lax.ppermute(parts[3], 'z', FROM_ENDS)]
  transfers between devices with their start and end apart: 36 -> 35, of which waited for: 15 -> 17; matrix products, arithmetic and copies ran while one was open for 7% -> 8% of each run, Pallas kernels for 24% -> 29%
where the time goes in v3:
time: 646 us; the launch traced here: 636 us
  waiting for transfers between devices  260 us (40%)
  Pallas kernels  219 us (34%)
  starting transfers between devices  46.6 us (7%)
  local copies, waits for them, and re-layouts  44.4 us (7%)
  other arithmetic  26.9 us (4%)
  matrix products  23.6 us (4%)
  between operations  16 us (2%)
    ppermute x2, waiting for transfers between devices, line_in(): return lax.ppermute(add_low(part, across_far), 'z', NEAR)  49.4 us
    pallas_call x3, Pallas kernels, ffn(): pl.pallas_call(functools.partial(ffn_kernel, n, blocks), grid=(len(groups...  48 us
    pallas_call x1, Pallas kernels, attend_back(): pl.pallas_call(functools.partial(attend_back_kernel, bq, bk), grid_spec=p...  43.4 us
    ppermute x2, waiting for transfers between devices, line_out(): lax.ppermute(parts[2], 'z', FROM_ENDS)  42.3 us
    ppermute x4, waiting for transfers between devices, line_second(): return (lax.ppermute(near, 'z', MIDDLE), lax.ppermute(across, 'z', TO_ENDS))  40.4 us
    unnamed x165, local copies, waits for them, and re-layouts  35.9 us
    all_gather x1, waiting for transfers between devices, per_device_fast(): low_all = lax.all_gather(low_part, ('z', 'y'), axis=0, tiled=True)  29.5 us
    pallas_call x2, Pallas kernels, attend(): pl.pallas_call(functools.partial(attend_kernel, bq, bk, kv), grid_spec=pl...  28.1 us
  transfers between devices with their start and end apart: 35, of which 17 were waited for; matrix products, arithmetic and copies ran while one was open for 8% of the time, Pallas kernels for 29%

profile of v3, /device:TPU:0, one launch (start us, length us, event | category | flops | bytes accessed | tf_op | source)
XLA Modules:
  0.0 636.2 jit_solution(5972887966991660488)
XLA Ops:
  23.2 8.7 %project.1 = (bf16[2048,1024]{1,0:T(8,128)(2,1)}, bf16[4,2048,128]{2,1,0:T(8,128)(2,1)}, bf16[2048,128]{1,0:T(8,128)(2,1)}, bf16[2048,256]{1,0:T(8,128)(2,1)}) custom-call(bf16[2048,1024]{1,0:T(8,128)(2,1)S(1)} %copy-done, bf16[1,1024]{1,0:T(2,128)(2,1)S(1)} %broadcast_in_dim.35.gain_ref, bf16[1024,256]{1,0:T(8,128)(2,1)S(1)} %copy-done.6, ...), custom_call_target="tpu_custom_call" | custom-call | flops 900000000 | tf_op jit(solution)/shard_map/project/pallas_call | solution.py:89
  35.8 14.1 %attend.2 = (bf16[2048,256]{1,0:T(8,128)(2,1)}, f32[2,8,4096]{2,1,0:T(8,128)}) custom-call(s32[1]{0:T(128)S(6)} %copy.78.prefix_ref, bf16[4,2048,128]{2,1,0:T(8,128)(2,1)S(1)} %copy-done.50, bf16[2048,128]{1,0:T(8,128)(2,1)S(1)} %copy-done.55, bf16[2048,256]{1,0:T(8,128)(2,1)S(1)} %copy-done.52), custom_call_target="tpu_custom_call" | custom-call | flops 1400000000 | tf_op jit(solution)/shard_map/attend/pallas_call | solution.py:155
  54.3 14.0 %attend.3 = (bf16[2048,256]{1,0:T(8,128)(2,1)}, f32[2,8,4096]{2,1,0:T(8,128)}) custom-call(s32[1]{0:T(128)S(6)} %copy.78.prefix_ref, bf16[4,2048,128]{2,1,0:T(8,128)(2,1)S(1)} %copy-done.51, bf16[2048,128]{1,0:T(8,128)(2,1)S(1)} %copy-done.55, bf16[2048,256]{1,0:T(8,128)(2,1)S(1)} %copy-done.53, ...), custom_call_target="tpu_custom_call", output_to_operand_aliasing={{0}: (4, {}), {1}: (5, {})} | custom-call | flops 1400000000 | tf_op jit(solution)/shard_map/attend/pallas_call | solution.py:155
  82.4 34.9 %collective-permute-done.6.refs_2_ = bf16[512,1152]{1,0:T(8,128)(2,1)} collective-permute-done((bf16[512,1152]{1,0:T(8,128)(2,1)S(1)}, bf16[512,1152]{1,0:T(8,128)(2,1)}, u32[]{:S(2)}, u32[]{:S(2)}) %collective-permute-start.6) | collective-permute-done | bytes 1179680 | tf_op jit(solution)/shard_map/ppermute | solution.py:627
  117.3 24.6 %collective-permute-done.7.refs_2_ = bf16[512,1152]{1,0:T(8,128)(2,1)} collective-permute-done((bf16[512,1152]{1,0:T(8,128)(2,1)}, bf16[512,1152]{1,0:T(8,128)(2,1)}, u32[]{:S(2)}, u32[]{:S(2)}) %collective-permute-start.7) | collective-permute-done | bytes 1179680 | tf_op jit(solution)/shard_map/ppermute | solution.py:631
  152.7 5.3 pick.4
  158.7 12.8 %collective-permute-done.8.refs_0_ = bf16[512,1024]{1,0:T(8,128)(2,1)} collective-permute-done((bf16[512,1024]{1,0:T(8,128)(2,1)S(1)}, bf16[512,1024]{1,0:T(8,128)(2,1)}, u32[]{:S(2)}, u32[]{:S(2)}) %collective-permute-start.8) | collective-permute-done | bytes 1048608 | tf_op jit(solution)/shard_map/ppermute | solution.py:623
  174.4 6.4 %pick.5 = (bf16[8,128,1024]{2,1,0:T(8,128)(2,1)}, bf16[8,128,1024]{2,1,0:T(8,128)(2,1)}, f32[8,128,128]{2,1,0:T(8,128)}, f32[512,128]{1,0:T(8,128)S(1)}, f32[512,128]{1,0:T(8,128)S(1)}) custom-call(s32[9]{0:T(128)S(1)} %pad_add_fusion.shift_ref, bf16[512,1024]{1,0:T(8,128)(2,1)} %collective-permute-done.8.refs_0_, ...), custom_call_target="tpu_custom_call" | custom-call | flops 400000000 | tf_op jit(solution)/shard_map/pick/pallas_call | solution.py:313
  182.3 12.7 %ffn.3 = (bf16[8,256,1024]{2,1,0:T(8,128)(2,1)}, bf16[8,256,1024]{2,1,0:T(8,128)(2,1)}, f32[8,256,128]{2,1,0:T(8,128)}, bf16[8,256,512]{2,1,0:T(8,128)(2,1)}, bf16[8,256,1024]{2,1,0:T(8,128)(2,1)}) custom-call(bf16[8,128,1024]{2,1,0:T(8,128)(2,1)} %get-tuple-element.163.refs_0_, bf16[8,128,1024]{2,1,0:T(8,128)(2,1)} %get-tuple-element.164.refs_1_, ...), custom_call_target="tpu_custom_call" | custom-call | flops 1200000000 | tf_op jit(solution)/shard_map/ffn/pallas_call | solution.py:379
  195.0 5.5 collective-permute-done.11.refs_0_
  202.1 7.1 %pick.6 = (bf16[8,128,1024]{2,1,0:T(8,128)(2,1)}, bf16[8,128,1024]{2,1,0:T(8,128)(2,1)}, f32[8,128,128]{2,1,0:T(8,128)}, f32[512,128]{1,0:T(8,128)S(1)}, f32[512,128]{1,0:T(8,128)S(1)}) custom-call(s32[9]{0:T(128)S(1)} %pad_add_fusion.shift_ref, bf16[512,1024]{1,0:T(8,128)(2,1)} %collective-permute-done.11.refs_0_, ...), custom_call_target="tpu_custom_call" | custom-call | flops 400000000 | tf_op jit(solution)/shard_map/pick/pallas_call | solution.py:313
  210.6 12.8 %ffn.4 = (bf16[8,256,1024]{2,1,0:T(8,128)(2,1)}, bf16[8,256,1024]{2,1,0:T(8,128)(2,1)}, f32[8,256,128]{2,1,0:T(8,128)}, bf16[8,256,512]{2,1,0:T(8,128)(2,1)}, bf16[8,256,1024]{2,1,0:T(8,128)(2,1)}) custom-call(bf16[8,128,1024]{2,1,0:T(8,128)(2,1)} %get-tuple-element.163.refs_0_, ...), custom_call_target="tpu_custom_call", output_to_operand_aliasing={{0}: (7, {}), {1}: (8, {}), {2}: (9, {}), {3}: (10, {}), {4... | custom-call | flops 1200000000 | tf_op jit(solution)/shard_map/ffn/pallas_call | solution.py:379
  227.5 6.5 %pick.7 = (bf16[8,128,1024]{2,1,0:T(8,128)(2,1)}, bf16[8,128,1024]{2,1,0:T(8,128)(2,1)}, f32[8,128,128]{2,1,0:T(8,128)}, f32[512,128]{1,0:T(8,128)S(1)}, f32[512,128]{1,0:T(8,128)S(1)}) custom-call(s32[9]{0:T(128)S(1)} %pad_add_fusion.shift_ref, bf16[512,1024]{1,0:T(8,128)(2,1)S(1)} %copy-done.27, bf16[512,1024]{1,0:T(8,128)(2,1)} %collective-permute-done.9.refs_1_, ...), custom_call_target="tpu_custom_call" | custom-call | flops 400000000 | tf_op jit(solution)/shard_map/pick/pallas_call | solution.py:313
  235.4 22.5 %ffn.5 = (bf16[8,256,1024]{2,1,0:T(8,128)(2,1)}, bf16[8,256,1024]{2,1,0:T(8,128)(2,1)}, f32[8,256,128]{2,1,0:T(8,128)}, bf16[8,256,512]{2,1,0:T(8,128)(2,1)}, bf16[8,256,1024]{2,1,0:T(8,128)(2,1)}) custom-call(bf16[8,128,1024]{2,1,0:T(8,128)(2,1)} %get-tuple-element.195.refs_0_.refs_2_, bf16[8,128,1024]{2,1,0:T(8,128)(2,1)} %get-tuple-element.196.refs_1_.refs_3_, ...), custom_call_target="tpu_custom_call" | custom-call | flops 2400000000 | tf_op jit(solution)/shard_map/ffn/pallas_call | solution.py:379
  260.2 5.0 merge_back.3
  276.3 13.9 %wgrad.2.refs_16_ = bf16[2,4,3,4,1024,128]{5,4,3,2,1,0:T(8,128)(2,1)} custom-call(bf16[8,128,1024]{2,1,0:T(8,128)(2,1)} %get-tuple-element.163.refs_0_, bf16[8,128,1024]{2,1,0:T(8,128)(2,1)} %get-tuple-element.164.refs_1_, bf16[8,128,1024]{2,1,0:T(8,128)(2,1)} %get-tuple-element.195.refs_0_.refs_2_, ...), custom_call_target="tpu_custom_call" | custom-call | flops 1300000000 | tf_op jit(solution)/shard_map/wgrad/pallas_call | solution.py:420
  290.2 13.6 %wgrad.3 = bf16[2,4,3,4,1024,128]{5,4,3,2,1,0:T(8,128)(2,1)} custom-call(bf16[8,128,1024]{2,1,0:T(8,128)(2,1)} %get-tuple-element.163.refs_0_, bf16[8,128,1024]{2,1,0:T(8,128)(2,1)} %get-tuple-element.164.refs_1_, bf16[8,128,1024]{2,1,0:T(8,128)(2,1)} %get-tuple-element.195.refs_0_.refs_2_, ...), custom_call_target="tpu_custom_call", output_to_operand_aliasing={{}: (16, {})} | custom-call | flops 1300000000 | tf_op jit(solution)/shard_map/wgrad/pallas_call | solution.py:420
  308.2 20.2 %collective-permute-done.16 = bf16[512,1152]{1,0:T(8,128)(2,1)S(1)} collective-permute-done((bf16[512,1152]{1,0:T(8,128)(2,1)}, bf16[512,1152]{1,0:T(8,128)(2,1)S(1)}, u32[]{:S(2)}, u32[]{:S(2)}) %collective-permute-start.16) | collective-permute-done | bytes 1179680 | tf_op jit(solution)/shard_map/ppermute | solution.py:639
  335.0 5.0 merge_out.3
  340.1 4.9 merge_out.2
  345.1 12.0 %collective-permute-done.15 = bf16[512,1152]{1,0:T(8,128)(2,1)S(1)} collective-permute-done((bf16[512,1152]{1,0:T(8,128)(2,1)S(1)}, bf16[512,1152]{1,0:T(8,128)(2,1)S(1)}, u32[]{:S(2)}, u32[]{:S(2)}) %collective-permute-start.15) | collective-permute-done | bytes 1179680 | tf_op jit(solution)/shard_map/ppermute | solution.py:651
  369.3 18.5 %collective-permute-done.20 = bf16[512,1024]{1,0:T(8,128)(2,1)S(1)} collective-permute-done((bf16[512,1024]{1,0:T(8,128)(2,1)S(1)}, bf16[512,1024]{1,0:T(8,128)(2,1)S(1)}, u32[]{:S(2)}, u32[]{:S(2)}) %collective-permute-start.20) | collective-permute-done | bytes 1048608 | tf_op jit(solution)/shard_map/ppermute | solution.py:639
  387.8 22.1 %collective-permute-done.21 = bf16[512,1024]{1,0:T(8,128)(2,1)S(1)} collective-permute-done((bf16[512,1024]{1,0:T(8,128)(2,1)S(1)}, bf16[512,1024]{1,0:T(8,128)(2,1)S(1)}, u32[]{:S(2)}, u32[]{:S(2)}) %collective-permute-start.21) | collective-permute-done | bytes 1048608 | tf_op jit(solution)/shard_map/ppermute | solution.py:639
  426.9 43.4 %attend_back.1 = bf16[2048,512]{1,0:T(8,128)(2,1)} custom-call(s32[1]{0:T(128)S(6)} %copy.78.prefix_ref, bf16[4,2048,128]{2,1,0:T(8,128)(2,1)} %get-tuple-element.140.q_ref, bf16[2048,128]{1,0:T(8,128)(2,1)S(1)} %copy-done.56, bf16[2048,256]{1,0:T(8,128)(2,1)S(1)} %copy-done.54, bf16[2048,256]{1,0:T(8,128)(2,1)S(1)} %copy-done.2, ...), custom_call_target="tpu_custom_call" | custom-call | flops 4600000000 | tf_op jit(solution)/shard_map/attend_back/pallas_call | solution.py:246
  470.5 5.2 convolution_convert_fusion.3
  477.2 5.7 reduce-scatter.3.cloned.1.call-done
  499.0 37.4 %collective-permute-done.27 = bf16[512,1024]{1,0:T(8,128)(2,1)S(1)} collective-permute-done((bf16[512,1024]{1,0:T(8,128)(2,1)S(1)}, bf16[512,1024]{1,0:T(8,128)(2,1)S(1)}, u32[]{:S(2)}, u32[]{:S(2)}) %collective-permute-start.27) | collective-permute-done | bytes 1048608 | tf_op jit(solution)/shard_map/ppermute | solution.py:651
  536.5 5.8 collective-permute-done.26
  542.3 20.8 %reduce-scatter.5.cloned.1.call-done = bf16[256,512]{1,0:T(8,128)(2,1)} async-done(((bf16[2048,512]{1,0:T(8,128)(2,1)}), bf16[256,512]{1,0:T(8,128)(2,1)}) %reduce-scatter.5.cloned.1.call-update) | async-done | bytes 262160 | tf_op jit(solution)/shard_map/reduce_scatter | solution.py:813
  569.4 5.9 finish.2.refs_0_
  578.3 5.5 finish.3
  583.9 29.5 %all-gather.4.cloned.1.call-done = bf16[2048,512]{1,0:T(8,128)(2,1)} async-done(((bf16[256,512]{1,0:T(8,128)(2,1)}), bf16[2048,512]{1,0:T(8,128)(2,1)}) %all-gather.4.cloned.1.call-update) | async-done | bytes 2097168 | tf_op jit(solution)/shard_map/all_gather | solution.py:826
  (288 shorter events, 157.8 us)
Async XLA Ops:
  7.2 175.1 %all-gather.6.cloned.1.call-start = ((), (), s32[]{:S(2)}) async-start(), calls=%async_computation.5 | async-start | bytes 28311552 | tf_op jit(solution)/shard_map/all_gather | solution.py:690
  12.3 470.5 %reduce-scatter.3.cloned.1.call-start = ((), (), s32[]{:S(2)}) async-start(), calls=%async_computation.2 | async-start | bytes 28311552 | tf_op jit(solution)/shard_map/reduce_scatter | solution.py:769
  13.7 36.1 %collective-permute-start = (bf16[512,1152]{1,0:T(8,128)(2,1)S(1)}, bf16[512,1152]{1,0:T(8,128)(2,1)}, u32[]{:S(2)}, u32[]{:S(2)}) collective-permute-start(bf16[512,1152]{1,0:T(8,128)(2,1)S(1)} %fusion.7.refs_1_), channel_id=1, source_target_pairs={{0,8},{8,0},{16,24},{24,16},{1,9},{9,1},{17,25},{25,17},{2,10},{10... | collective-permute-start | bytes 3538952 | tf_op jit(solution)/shard_map/ppermute | solution.py:623
  16.8 33.1 %collective-permute-start.1 = (bf16[512,1152]{1,0:T(8,128)(2,1)S(1)}, bf16[512,1152]{1,0:T(8,128)(2,1)S(1)}, u32[]{:S(2)}, u32[]{:S(2)}) collective-permute-start(bf16[512,1152]{1,0:T(8,128)(2,1)S(1)} %fusion.7.refs_1_), channel_id=1, source_target_pairs={{8,16},{16,8},{9,17},{17,9},{10,18},{18,10},{11,19},{19,11},{12,20... | collective-permute-start | bytes 3538952 | tf_op jit(solution)/shard_map/ppermute | solution.py:623
  49.8 18.6 %collective-permute-start.2 = (bf16[512,1152]{1,0:T(8,128)(2,1)}, bf16[512,1152]{1,0:T(8,128)(2,1)}, u32[]{:S(2)}, u32[]{:S(2)}) collective-permute-start(bf16[512,1152]{1,0:T(8,128)(2,1)} %collective-permute-done.refs_1_), channel_id=1, source_target_pairs={{8,16},{16,8},{9,17},{17,9},{10,18},{18,10},{11,19},{19,11},{12,20... | collective-permute-start | bytes 3538952 | tf_op jit(solution)/shard_map/ppermute | solution.py:627
  73.4 7.4 %collective-permute-start.3 = (bf16[512,1024]{1,0:T(8,128)(2,1)}, bf16[512,1024]{1,0:T(8,128)(2,1)}, u32[]{:S(2)}, u32[]{:S(2)}) collective-permute-start(bf16[512,1024]{1,0:T(8,128)(2,1)} %convolution_convert_fusion.2), channel_id=1, source_target_pairs={{0,1},{1,0},{2,3},{3,2},{4,5},{5,4},{6,7},{7,6},{8,9},{9,8},{10,11... | collective-permute-start | bytes 3145736 | tf_op jit(solution)/shard_map/ppermute | solution.py:594
  73.9 43.4 %collective-permute-start.6 = (bf16[512,1152]{1,0:T(8,128)(2,1)S(1)}, bf16[512,1152]{1,0:T(8,128)(2,1)}, u32[]{:S(2)}, u32[]{:S(2)}) collective-permute-start(bf16[512,1152]{1,0:T(8,128)(2,1)S(1)} %collective-permute-done.1.refs_3_), channel_id=1, source_target_pairs={{8,0},{16,24},{9,1},{17,25},{10,2},{18,26},{11,3},{19,27},{12,4},{... | collective-permute-start | bytes 3538952 | tf_op jit(solution)/shard_map/ppermute | solution.py:627
  75.2 66.8 %collective-permute-start.7 = (bf16[512,1152]{1,0:T(8,128)(2,1)}, bf16[512,1152]{1,0:T(8,128)(2,1)}, u32[]{:S(2)}, u32[]{:S(2)}) collective-permute-start(bf16[512,1152]{1,0:T(8,128)(2,1)} %collective-permute-done.2.refs_3_), channel_id=1, source_target_pairs={{8,0},{16,24},{9,1},{17,25},{10,2},{18,26},{11,3},{19,27},{12,4},{... | collective-permute-start | bytes 3538952 | tf_op jit(solution)/shard_map/ppermute | solution.py:631
  79.4 62.6 %collective-permute-start.5 = (bf16[512,1024]{1,0:T(8,128)(2,1)}, bf16[512,1024]{1,0:T(8,128)(2,1)}, u32[]{:S(2)}, u32[]{:S(2)}) collective-permute-start(bf16[512,1024]{1,0:T(8,128)(2,1)} %add_convert_fusion.9), channel_id=1, source_target_pairs={{0,2},{2,0},{1,3},{3,1},{4,6},{6,4},{5,7},{7,5},{8,10},{10,8},{9,1... | collective-permute-start | bytes 3145736 | tf_op jit(solution)/shard_map/ppermute | solution.py:594
  145.4 26.1 %collective-permute-start.8 = (bf16[512,1024]{1,0:T(8,128)(2,1)S(1)}, bf16[512,1024]{1,0:T(8,128)(2,1)}, u32[]{:S(2)}, u32[]{:S(2)}) collective-permute-start(bf16[512,1024]{1,0:T(8,128)(2,1)S(1)} %multiply_convert_fusion.refs_0_), channel_id=1, source_target_pairs={{0,8},{8,0},{16,24},{24,16},{1,9},{9,1},{17,25},{25,17},{2,10},{10... | collective-permute-start | bytes 3145736 | tf_op jit(solution)/shard_map/ppermute | solution.py:623
  148.8 22.7 %collective-permute-start.9 = (bf16[512,1024]{1,0:T(8,128)(2,1)S(1)}, bf16[512,1024]{1,0:T(8,128)(2,1)}, u32[]{:S(2)}, u32[]{:S(2)}) collective-permute-start(bf16[512,1024]{1,0:T(8,128)(2,1)S(1)} %multiply_convert_fusion.refs_0_), channel_id=1, source_target_pairs={{8,16},{16,8},{9,17},{17,9},{10,18},{18,10},{11,19},{19,11},{12,20... | collective-permute-start | bytes 3145736 | tf_op jit(solution)/shard_map/ppermute | solution.py:623
  171.5 23.5 %collective-permute-start.10 = (bf16[512,1024]{1,0:T(8,128)(2,1)}, bf16[512,1024]{1,0:T(8,128)(2,1)}, u32[]{:S(2)}, u32[]{:S(2)}) collective-permute-start(bf16[512,1024]{1,0:T(8,128)(2,1)} %collective-permute-done.8.refs_0_), channel_id=1, source_target_pairs={{8,16},{16,8},{9,17},{17,9},{10,18},{18,10},{11,19},{19,11},{12,20... | collective-permute-start | bytes 3145736 | tf_op jit(solution)/shard_map/ppermute | solution.py:627
  173.1 27.4 %collective-permute-start.11 = (bf16[512,1024]{1,0:T(8,128)(2,1)}, bf16[512,1024]{1,0:T(8,128)(2,1)}, u32[]{:S(2)}, u32[]{:S(2)}) collective-permute-start(bf16[512,1024]{1,0:T(8,128)(2,1)} %collective-permute-done.9.refs_1_), channel_id=1, source_target_pairs={{8,0},{16,24},{9,1},{17,25},{10,2},{18,26},{11,3},{19,27},{12,4},{... | collective-permute-start | bytes 3145736 | tf_op jit(solution)/shard_map/ppermute | solution.py:627
  200.5 24.8 %collective-permute-start.12 = (bf16[512,1024]{1,0:T(8,128)(2,1)}, bf16[512,1024]{1,0:T(8,128)(2,1)S(1)}, u32[]{:S(2)}, u32[]{:S(2)}) collective-permute-start(bf16[512,1024]{1,0:T(8,128)(2,1)} %collective-permute-done.10.refs_1_), channel_id=1, source_target_pairs={{8,0},{16,24},{9,1},{17,25},{10,2},{18,26},{11,3},{19,27},{12,4},{... | collective-permute-start | bytes 3145736 | tf_op jit(solution)/shard_map/ppermute | solution.py:631
  266.2 37.6 %collective-permute-start.13 = (bf16[512,1152]{1,0:T(8,128)(2,1)S(1)}, bf16[512,1152]{1,0:T(8,128)(2,1)}, u32[]{:S(2)}, u32[]{:S(2)}) collective-permute-start(bf16[512,1152]{1,0:T(8,128)(2,1)S(1)} %get-tuple-element.204), channel_id=1, source_target_pairs={{0,8},{24,16},{1,9},{25,17},{2,10},{26,18},{3,11},{27,19},{4,12},{... | collective-permute-start | bytes 3538952 | tf_op jit(solution)/shard_map/ppermute | solution.py:639
  303.8 259.2 %reduce-scatter.5.cloned.1.call-start = ((), (), s32[]{:S(2)}) async-start(), calls=%async_computation.3 | async-start | bytes 2359296 | tf_op jit(solution)/shard_map/reduce_scatter | solution.py:813
  303.9 24.5 %collective-permute-start.16 = (bf16[512,1152]{1,0:T(8,128)(2,1)}, bf16[512,1152]{1,0:T(8,128)(2,1)S(1)}, u32[]{:S(2)}, u32[]{:S(2)}) collective-permute-start(bf16[512,1152]{1,0:T(8,128)(2,1)} %copy-done.14), channel_id=1, source_target_pairs={{0,8},{24,16},{1,9},{25,17},{2,10},{26,18},{3,11},{27,19},{4,12},{... | collective-permute-start | bytes 3538952 | tf_op jit(solution)/shard_map/ppermute | solution.py:639
  307.3 22.5 %collective-permute-start.14 = (bf16[512,1152]{1,0:T(8,128)(2,1)S(1)}, bf16[512,1152]{1,0:T(8,128)(2,1)S(1)}, u32[]{:S(2)}, u32[]{:S(2)}) collective-permute-start(bf16[512,1152]{1,0:T(8,128)(2,1)S(1)} %add_convert_fusion.4), channel_id=1, source_target_pairs={{8,16},{16,8},{9,17},{17,9},{10,18},{18,10},{11,19},{19,11},{12,20... | collective-permute-start | bytes 3538952 | tf_op jit(solution)/shard_map/ppermute | solution.py:647
  328.7 16.3 %collective-permute-start.17 = (bf16[512,1152]{1,0:T(8,128)(2,1)S(1)}, bf16[512,1152]{1,0:T(8,128)(2,1)S(1)}, u32[]{:S(2)}, u32[]{:S(2)}) collective-permute-start(bf16[512,1152]{1,0:T(8,128)(2,1)S(1)} %add_convert_fusion.2), channel_id=1, source_target_pairs={{8,16},{16,8},{9,17},{17,9},{10,18},{18,10},{11,19},{19,11},{12,20... | collective-permute-start | bytes 3538952 | tf_op jit(solution)/shard_map/ppermute | solution.py:647
  330.1 26.9 %collective-permute-start.15 = (bf16[512,1152]{1,0:T(8,128)(2,1)S(1)}, bf16[512,1152]{1,0:T(8,128)(2,1)S(1)}, u32[]{:S(2)}, u32[]{:S(2)}) collective-permute-start(bf16[512,1152]{1,0:T(8,128)(2,1)S(1)} %add_convert_fusion.3), channel_id=1, source_target_pairs={{0,8},{8,0},{16,24},{24,16},{1,9},{9,1},{17,25},{25,17},{2,10},{10... | collective-permute-start | bytes 3538952 | tf_op jit(solution)/shard_map/ppermute | solution.py:651
  360.6 6.1 collective-permute-start.19
  360.7 27.2 %collective-permute-start.20 = (bf16[512,1024]{1,0:T(8,128)(2,1)S(1)}, bf16[512,1024]{1,0:T(8,128)(2,1)S(1)}, u32[]{:S(2)}, u32[]{:S(2)}) collective-permute-start(bf16[512,1024]{1,0:T(8,128)(2,1)S(1)} %get-tuple-element.229), channel_id=1, source_target_pairs={{0,8},{24,16},{1,9},{25,17},{2,10},{26,18},{3,11},{27,19},{4,12},{... | collective-permute-start | bytes 3145736 | tf_op jit(solution)/shard_map/ppermute | solution.py:639
  364.5 45.5 %collective-permute-start.21 = (bf16[512,1024]{1,0:T(8,128)(2,1)S(1)}, bf16[512,1024]{1,0:T(8,128)(2,1)S(1)}, u32[]{:S(2)}, u32[]{:S(2)}) collective-permute-start(bf16[512,1024]{1,0:T(8,128)(2,1)S(1)} %get-tuple-element.225), channel_id=1, source_target_pairs={{0,8},{24,16},{1,9},{25,17},{2,10},{26,18},{3,11},{27,19},{4,12},{... | collective-permute-start | bytes 3145736 | tf_op jit(solution)/shard_map/ppermute | solution.py:639
  365.8 48.4 %collective-permute-start.18 = (bf16[512,1024]{1,0:T(8,128)(2,1)S(1)}, bf16[512,1024]{1,0:T(8,128)(2,1)}, u32[]{:S(2)}, u32[]{:S(2)}) collective-permute-start(bf16[512,1024]{1,0:T(8,128)(2,1)S(1)} %subtract_convert_fusion.refs_0_), channel_id=1, source_target_pairs={{0,2},{2,0},{1,3},{3,1},{4,6},{6,4},{5,7},{7,5},{8,10},{10,8},{9,1... | collective-permute-start | bytes 3145736 | tf_op jit(solution)/shard_map/ppermute | solution.py:594
  414.2 5.9 collective-permute-start.22
  416.5 60.7 %collective-permute-start.23 = (bf16[512,1024]{1,0:T(8,128)(2,1)}, bf16[512,1024]{1,0:T(8,128)(2,1)}, u32[]{:S(2)}, u32[]{:S(2)}) collective-permute-start(bf16[512,1024]{1,0:T(8,128)(2,1)} %get-tuple-element.247), channel_id=1, source_target_pairs={{8,16},{16,8},{9,17},{17,9},{10,18},{18,10},{11,19},{19,11},{12,20... | collective-permute-start | bytes 3145736 | tf_op jit(solution)/shard_map/ppermute | solution.py:802
  418.2 59.0 %collective-permute-start.24 = (bf16[512,1024]{1,0:T(8,128)(2,1)}, bf16[512,1024]{1,0:T(8,128)(2,1)}, u32[]{:S(2)}, u32[]{:S(2)}) collective-permute-start(bf16[512,1024]{1,0:T(8,128)(2,1)} %get-tuple-element.248), channel_id=1, source_target_pairs={{8,16},{16,8},{9,17},{17,9},{10,18},{18,10},{11,19},{19,11},{12,20... | collective-permute-start | bytes 3145736 | tf_op jit(solution)/shard_map/ppermute | solution.py:802
  486.7 126.6 %all-gather.4.cloned.1.call-start = ((), (), s32[]{:S(2)}) async-start(), calls=%async_computation.4 | async-start | bytes 2359296 | tf_op jit(solution)/shard_map/all_gather | solution.py:826
  494.4 47.8 %collective-permute-start.26 = (bf16[2,512,1024]{2,1,0:T(8,128)(2,1)S(1)}, bf16[2,512,1024]{2,1,0:T(8,128)(2,1)}, u32[]{:S(2)}, u32[]{:S(2)}) collective-permute-start(bf16[2,512,1024]{2,1,0:T(8,128)(2,1)S(1)} %add_convert_fusion.1), channel_id=1, source_target_pairs={{0,2},{2,0},{1,3},{3,1},{4,6},{6,4},{5,7},{7,5},{8,10},{10,8},{9,1... | collective-permute-start | bytes 6291464 | tf_op jit(solution)/shard_map/ppermute | solution.py:594
  497.4 39.0 %collective-permute-start.27 = (bf16[512,1024]{1,0:T(8,128)(2,1)S(1)}, bf16[512,1024]{1,0:T(8,128)(2,1)S(1)}, u32[]{:S(2)}, u32[]{:S(2)}) collective-permute-start(bf16[512,1024]{1,0:T(8,128)(2,1)S(1)} %add_convert_fusion.6), channel_id=1, source_target_pairs={{0,8},{8,0},{16,24},{24,16},{1,9},{9,1},{17,25},{25,17},{2,10},{10... | collective-permute-start | bytes 3145736 | tf_op jit(solution)/shard_map/ppermute | solution.py:651
  566.5 11.8 %collective-permute-start.28 = (bf16[2,512,1024]{2,1,0:T(8,128)(2,1)S(1)}, bf16[2,512,1024]{2,1,0:T(8,128)(2,1)S(1)}, u32[]{:S(2)}, u32[]{:S(2)}) collective-permute-start(bf16[2,512,1024]{2,1,0:T(8,128)(2,1)S(1)} %add_convert_fusion), channel_id=1, source_target_pairs={{0,1},{1,0},{2,3},{3,2},{4,5},{5,4},{6,7},{7,6},{8,9},{9,8},{10,11... | collective-permute-start | bytes 6291464 | tf_op jit(solution)/shard_map/ppermute | solution.py:594
  617.9 10.0 %collective-permute-start.30 = (bf16[48,1024]{1,0:T(8,128)(2,1)S(1)}, bf16[48,1024]{1,0:T(8,128)(2,1)S(1)}, u32[]{:S(2)}, u32[]{:S(2)}) collective-permute-start(bf16[48,1024]{1,0:T(8,128)(2,1)S(1)} %fusion.34), channel_id=1, source_target_pairs={{0,2},{2,0},{1,3},{3,1},{4,6},{6,4},{5,7},{7,5},{8,10},{10,8},{9,1... | collective-permute-start | bytes 294920 | tf_op jit(solution)/shard_map/ppermute | solution.py:594
  (84 other events, 543.2 us)
Sparse Core Ops, SparseCore 0:
  12.4 149.3 all-gather.5
  304.0 178.8 reduce-scatter.2
  487.0 76.0 reduce-scatter.4
  565.1 48.2 all-gather.3

commit v4 on v3

--- a/solution.py
+++ b/solution.py
@@ -589,6 +589,27 @@
     )(rank, *operands)
 
 
+def grads_kernel(parts_ref, gate_ref, up_ref, down_ref):
+    gate_ref[0] = parts_ref[0, 0].astype(f32)
+    up_ref[0] = parts_ref[1, 0].astype(f32)
+    down_ref[0] = parts_ref[2, 0].astype(f32).T
+
+
+def expert_grads(parts):
+    _, E, D, F = parts.shape
+    one = lambda *s: pl.BlockSpec((1,) + s, lambda e: (e, 0, 0))
+    return pl.pallas_call(
+        grads_kernel,
+        grid=(E,),
+        in_specs=[pl.BlockSpec((3, 1, D, F), lambda e: (0, e, 0, 0))],
+        out_specs=[one(D, F), one(D, F), one(F, D)],
+        out_shape=[pltpu.HBM((E, D, F), f32), pltpu.HBM((E, D, F), f32), pltpu.HBM((E, F, D), f32)],
+        compiler_params=pltpu.CompilerParams(vmem_limit_bytes=32 << 20),
+        cost_estimate=busy(4),
+        name="expert_grads",
+    )(parts)
+
+
 def swap(x, axis, bit=1):
     count = lax.axis_size(axis)
     return lax.ppermute(x, axis, [(i, i ^ bit) for i in range(count)])
@@ -598,7 +619,8 @@
     for axis in axes:
         bit = 1
         while bit < lax.axis_size(axis):
-            x = x + swap(x, axis, bit)
+            low = x.astype(bf16)
+            x = low.astype(f32) + swap(low, axis, bit).astype(f32)
             bit *= 2
     return x
 
@@ -750,7 +772,7 @@
     far_back = merge_back(shift, codes[2:], done_apart[1], done_apart[2], cap)
     back = [*merge_back(shift, codes[:2], done_close[1], done_close[2], cap), *far_back]
     back_end_far, back_end = line_out(back)
-    late_act, *_ = hold(done_apart[3], *back)
+    late_act, *_ = hold(done_apart[3], *far_back)
     used = (done_close[3], late_act), (done_close[4], done_apart[4]), shards, groups
     parts = wgrad(picked, *used, 0)
     parts = wgrad(picked, *used, 1, (parts,))
@@ -788,7 +810,6 @@
         - hidden_in * rms_two**3 * jnp.mean(scaled_two * hidden_in, -1, keepdims=True)
     ).astype(bf16)
     small = jnp.concatenate([router_part, gain_two_part[None], jnp.zeros((7, width), f32)], 0)
-    small = small.reshape(-1, width // 2).astype(bf16)
     hidden_over_x = swap(hidden_grad, "x")
     rank_row = rank.astype(jnp.int32)[None]
     near_done = spread(rank_row, 0, [hidden_grad, swap(hidden_grad, "c")], attended, w_out)
@@ -805,8 +826,9 @@
     )
     heads_in = jnp.concatenate([w_query, w_key, w_value], 1)
     heads_grad = jnp.einsum("id,ih->dh", normed_one, heads_back, preferred_element_type=f32)
-    low = jnp.concatenate([heads_grad.astype(bf16), out_low.reshape(-1, heads_grad.shape[1]), small], 0)
-    low = jnp.pad(low, ((0, -low.shape[0] % 1024), (0, 0)))
+    low = jnp.concatenate([heads_grad.astype(bf16), out_low.reshape(-1, heads_grad.shape[1])], 0)
+    gain_one_part = jnp.sum(heads_grad * heads_in.astype(f32), 1) / gain_attn.astype(f32)
+    small = jnp.concatenate([small[: EXPERTS + 1], gain_one_part[None], small[EXPERTS + 2 :]], 0)
     heads_back, low, part_sum, out_far, out_across = hold(heads_back, low, part_sum, out_far, out_across)
     out_got = line_in(out_parts[1], out_far)
 
@@ -820,40 +842,37 @@
 
     from_core = swap(rows_of(1 - c).astype(bf16), "c")
     core_sum = (rows_of(c) + from_core.astype(f32)).astype(bf16)
-    core_got, low_part, out_got = hold(swap(core_sum, "x"), low_part, out_got)
+    core_got, low_part, out_got, small = hold(swap(core_sum, "x"), low_part, out_got, small)
+    rest = total_over(small, ("c", "x", "y", "z"))
     moe_own = out_parts[0].astype(f32) + out_across.astype(f32) + out_got.astype(f32)
     block_output = (hidden_in + moe_own).astype(bf16)
     low_all = lax.all_gather(low_part, ("z", "y"), axis=0, tiled=True)
+    summed_grads = expert_grads(part_sum)
     chip_sum = (core_sum.astype(f32) + core_got.astype(f32)).astype(bf16)
     other_sum = swap(chip_sum, "c")
     core = c.astype(jnp.int32)[None]
     gain_row = gain_attn[None]
     input_grad = finish(core, chip_sum.reshape(-1, width), tokens, hidden_all, gain_row, own_rows)
-    other_sum, input_grad = hold(other_sum, input_grad)
+    other_sum, input_grad, *summed_grads = hold(other_sum, input_grad, *summed_grads)
     input_grad = finish(
         1 - core, other_sum.reshape(-1, width), tokens, hidden_all, gain_row, own_rows, (input_grad,)
     )
-    expert_grads = part_sum[0].astype(f32), part_sum[1].astype(f32), part_sum[2].astype(f32).transpose(0, 2, 1)
-    low_all, input_grad, block_output, *expert_grads = hold(low_all, input_grad, block_output, *expert_grads)
+    low_all, input_grad, block_output, rest = hold(low_all, input_grad, block_output, rest)
     low_all = low_all.astype(f32)
-    split = width + out_grad.size // low.shape[1]
     heads_total = low_all[:width]
-    out_total = low_all[width:split].reshape(out_grad.shape)
-    gain_one_part = jnp.sum(heads_total * heads_in.astype(f32), 1) / gain_attn.astype(f32)
-    rest = jnp.concatenate([low_all[split : split + 2 * (EXPERTS + 8)].reshape(-1, width), gain_one_part[None], jnp.zeros((7, width), f32)], 0)
-    rest = total_over(rest.astype(bf16), ("c", "x")).astype(f32)
+    out_total = low_all[width:].reshape(out_grad.shape)
     cut = w_query.shape[1]
     return (
         block_output,
         input_grad,
-        rest[EXPERTS + 8],
+        rest[EXPERTS + 1],
         heads_total[:, :cut],
         heads_total[:, cut : cut + w_key.shape[1]],
         heads_total[:, cut + w_key.shape[1] :],
         out_total,
         rest[EXPERTS],
         rest[:EXPERTS].T,
-        *expert_grads,
+        *summed_grads,
     )
 
 

time: 646 us -> 613 us (0.949)
  waiting for transfers between devices: 260 us -> 231 us
  starting transfers between devices: 46.6 us -> 56.2 us
  other arithmetic: 26.9 us -> 18.9 us
  local copies, waits for them, and re-layouts: 44.4 us -> 37.8 us
    all_gather x1, waiting for transfers between devices: 29.5 us -> 7.42 us  [per_device_fast(): low_all = lax.all_gather(low_part, ('z', 'y'), axis=0, tiled=True)]
    ppermute x2, waiting for transfers between devices: 42.3 us -> 31.8 us  [line_out(): lax.ppermute(parts[2], 'z', FROM_ENDS)]
    unnamed x165 -> x152, local copies, waits for them, and re-layouts: 35.9 us -> 29.5 us
    ppermute x11 -> x14, waiting for transfers between devices: 13.5 us -> 17.7 us  [swap(): return lax.ppermute(x, axis, [(i, i ^ bit) for i in range(count)])]
  transfers between devices with their start and end apart: 35 -> 38, of which waited for: 17 -> 19; matrix products, arithmetic and copies ran while one was open for 8% -> 7% of each run, Pallas kernels for 29% -> 31%
where the time goes in v4:
time: 613 us; the launch traced here: 603 us
  waiting for transfers between devices  231 us (38%)
  Pallas kernels  219 us (36%)
  starting transfers between devices  56.2 us (9%)
  local copies, waits for them, and re-layouts  37.8 us (6%)
  matrix products  23.8 us (4%)
  other arithmetic  18.9 us (3%)
  between operations  15.9 us (3%)
    pallas_call x3, Pallas kernels, ffn(): pl.pallas_call(functools.partial(ffn_kernel, n, blocks), grid=(len(groups...  48 us
    ppermute x2, waiting for transfers between devices, line_in(): return lax.ppermute(add_low(part, across_far), 'z', NEAR)  43 us
    pallas_call x1, Pallas kernels, attend_back(): pl.pallas_call(functools.partial(attend_back_kernel, bq, bk), grid_spec=p...  40.4 us
    ppermute x4, waiting for transfers between devices, line_second(): return (lax.ppermute(near, 'z', MIDDLE), lax.ppermute(across, 'z', TO_ENDS))  34.9 us
    ppermute x2, waiting for transfers between devices, line_out(): lax.ppermute(parts[2], 'z', FROM_ENDS)  31.8 us
    unnamed x152, local copies, waits for them, and re-layouts  29.5 us
    pallas_call x2, Pallas kernels, attend(): pl.pallas_call(functools.partial(attend_kernel, bq, bk, kv), grid_spec=pl...  28.1 us
    pallas_call x2, Pallas kernels, wgrad(): pl.pallas_call(functools.partial(wgrad_kernel, n, len(acts), blocks), gri...  27.1 us
  transfers between devices with their start and end apart: 38, of which 19 were waited for; matrix products, arithmetic and copies ran while one was open for 7% of the time, Pallas kernels for 31%

profile of v4, /device:TPU:0, one launch (start us, length us, event | category | flops | bytes accessed | tf_op | source)
XLA Modules:
  0.0 603.4 jit_solution(12807448124637221666)
XLA Ops:
  14.9 5.8 collective-permute-start
  25.9 8.7 %project.1 = (bf16[2048,1024]{1,0:T(8,128)(2,1)}, bf16[4,2048,128]{2,1,0:T(8,128)(2,1)}, bf16[2048,128]{1,0:T(8,128)(2,1)}, bf16[2048,256]{1,0:T(8,128)(2,1)}) custom-call(bf16[2048,1024]{1,0:T(8,128)(2,1)S(1)} %copy-done, bf16[1,1024]{1,0:T(2,128)(2,1)S(1)} %broadcast_in_dim.36.gain_ref, bf16[1024,256]{1,0:T(8,128)(2,1)S(1)} %copy-done.7, ...), custom_call_target="tpu_custom_call" | custom-call | flops 900000000 | tf_op jit(solution)/shard_map/project/pallas_call | solution.py:89
  38.5 14.0 %attend.2 = (bf16[2048,256]{1,0:T(8,128)(2,1)}, f32[2,8,4096]{2,1,0:T(8,128)}) custom-call(s32[1]{0:T(128)S(6)} %copy.68.prefix_ref, bf16[4,2048,128]{2,1,0:T(8,128)(2,1)S(1)} %copy-done.46, bf16[2048,128]{1,0:T(8,128)(2,1)S(1)} %copy-done.51, bf16[2048,256]{1,0:T(8,128)(2,1)S(1)} %copy-done.48), custom_call_target="tpu_custom_call" | custom-call | flops 1400000000 | tf_op jit(solution)/shard_map/attend/pallas_call | solution.py:155
  56.9 14.1 %attend.3 = (bf16[2048,256]{1,0:T(8,128)(2,1)}, f32[2,8,4096]{2,1,0:T(8,128)}) custom-call(s32[1]{0:T(128)S(6)} %copy.68.prefix_ref, bf16[4,2048,128]{2,1,0:T(8,128)(2,1)S(1)} %copy-done.47, bf16[2048,128]{1,0:T(8,128)(2,1)S(1)} %copy-done.52, bf16[2048,256]{1,0:T(8,128)(2,1)S(1)} %copy-done.49, ...), custom_call_target="tpu_custom_call", output_to_operand_aliasing={{0}: (4, {}), {1}: (5, {})} | custom-call | flops 1400000000 | tf_op jit(solution)/shard_map/attend/pallas_call | solution.py:155
  85.0 30.5 %collective-permute-done.6.refs_2_ = bf16[512,1152]{1,0:T(8,128)(2,1)} collective-permute-done((bf16[512,1152]{1,0:T(8,128)(2,1)S(1)}, bf16[512,1152]{1,0:T(8,128)(2,1)}, u32[]{:S(2)}, u32[]{:S(2)}) %collective-permute-start.6) | collective-permute-done | bytes 1179680 | tf_op jit(solution)/shard_map/ppermute | solution.py:649
  115.5 24.6 %collective-permute-done.7.refs_2_ = bf16[512,1152]{1,0:T(8,128)(2,1)} collective-permute-done((bf16[512,1152]{1,0:T(8,128)(2,1)}, bf16[512,1152]{1,0:T(8,128)(2,1)}, u32[]{:S(2)}, u32[]{:S(2)}) %collective-permute-start.7) | collective-permute-done | bytes 1179680 | tf_op jit(solution)/shard_map/ppermute | solution.py:653
  151.2 5.4 pick.4
  157.3 14.0 %collective-permute-done.8.refs_0_ = bf16[512,1024]{1,0:T(8,128)(2,1)} collective-permute-done((bf16[512,1024]{1,0:T(8,128)(2,1)S(1)}, bf16[512,1024]{1,0:T(8,128)(2,1)}, u32[]{:S(2)}, u32[]{:S(2)}) %collective-permute-start.8) | collective-permute-done | bytes 1048608 | tf_op jit(solution)/shard_map/ppermute | solution.py:645
  174.2 6.4 %pick.5 = (bf16[8,128,1024]{2,1,0:T(8,128)(2,1)}, bf16[8,128,1024]{2,1,0:T(8,128)(2,1)}, f32[8,128,128]{2,1,0:T(8,128)}, f32[512,128]{1,0:T(8,128)S(1)}, f32[512,128]{1,0:T(8,128)S(1)}) custom-call(s32[9]{0:T(128)S(1)} %pad_add_fusion.shift_ref, bf16[512,1024]{1,0:T(8,128)(2,1)} %collective-permute-done.8.refs_0_, ...), custom_call_target="tpu_custom_call" | custom-call | flops 400000000 | tf_op jit(solution)/shard_map/pick/pallas_call | solution.py:313
  182.1 12.7 %ffn.3 = (bf16[8,256,1024]{2,1,0:T(8,128)(2,1)}, bf16[8,256,1024]{2,1,0:T(8,128)(2,1)}, f32[8,256,128]{2,1,0:T(8,128)}, bf16[8,256,512]{2,1,0:T(8,128)(2,1)}, bf16[8,256,1024]{2,1,0:T(8,128)(2,1)}) custom-call(bf16[8,128,1024]{2,1,0:T(8,128)(2,1)} %get-tuple-element.168.refs_0_, bf16[8,128,1024]{2,1,0:T(8,128)(2,1)} %get-tuple-element.169.refs_1_, ...), custom_call_target="tpu_custom_call" | custom-call | flops 1200000000 | tf_op jit(solution)/shard_map/ffn/pallas_call | solution.py:379
  200.8 7.1 %pick.6 = (bf16[8,128,1024]{2,1,0:T(8,128)(2,1)}, bf16[8,128,1024]{2,1,0:T(8,128)(2,1)}, f32[8,128,128]{2,1,0:T(8,128)}, f32[512,128]{1,0:T(8,128)S(1)}, f32[512,128]{1,0:T(8,128)S(1)}) custom-call(s32[9]{0:T(128)S(1)} %pad_add_fusion.shift_ref, bf16[512,1024]{1,0:T(8,128)(2,1)} %collective-permute-done.11.refs_0_, ...), custom_call_target="tpu_custom_call" | custom-call | flops 400000000 | tf_op jit(solution)/shard_map/pick/pallas_call | solution.py:313
  209.3 12.8 %ffn.4 = (bf16[8,256,1024]{2,1,0:T(8,128)(2,1)}, bf16[8,256,1024]{2,1,0:T(8,128)(2,1)}, f32[8,256,128]{2,1,0:T(8,128)}, bf16[8,256,512]{2,1,0:T(8,128)(2,1)}, bf16[8,256,1024]{2,1,0:T(8,128)(2,1)}) custom-call(bf16[8,128,1024]{2,1,0:T(8,128)(2,1)} %get-tuple-element.168.refs_0_, ...), custom_call_target="tpu_custom_call", output_to_operand_aliasing={{0}: (7, {}), {1}: (8, {}), {2}: (9, {}), {3}: (10, {}), {4... | custom-call | flops 1200000000 | tf_op jit(solution)/shard_map/ffn/pallas_call | solution.py:379
  225.6 6.5 %pick.7 = (bf16[8,128,1024]{2,1,0:T(8,128)(2,1)}, bf16[8,128,1024]{2,1,0:T(8,128)(2,1)}, f32[8,128,128]{2,1,0:T(8,128)}, f32[512,128]{1,0:T(8,128)S(1)}, f32[512,128]{1,0:T(8,128)S(1)}) custom-call(s32[9]{0:T(128)S(1)} %pad_add_fusion.shift_ref, bf16[512,1024]{1,0:T(8,128)(2,1)S(1)} %copy-done.24, bf16[512,1024]{1,0:T(8,128)(2,1)} %collective-permute-done.9.refs_1_, ...), custom_call_target="tpu_custom_call" | custom-call | flops 400000000 | tf_op jit(solution)/shard_map/pick/pallas_call | solution.py:313
  232.8 22.5 %ffn.5 = (bf16[8,256,1024]{2,1,0:T(8,128)(2,1)}, bf16[8,256,1024]{2,1,0:T(8,128)(2,1)}, f32[8,256,128]{2,1,0:T(8,128)}, bf16[8,256,512]{2,1,0:T(8,128)(2,1)}, bf16[8,256,1024]{2,1,0:T(8,128)(2,1)}) custom-call(bf16[8,128,1024]{2,1,0:T(8,128)(2,1)} %get-tuple-element.200.refs_0_.refs_2_, bf16[8,128,1024]{2,1,0:T(8,128)(2,1)} %get-tuple-element.201.refs_1_.refs_3_, ...), custom_call_target="tpu_custom_call" | custom-call | flops 2400000000 | tf_op jit(solution)/shard_map/ffn/pallas_call | solution.py:379
  256.7 4.9 merge_back.3
  265.4 13.5 %wgrad.2.refs_16_ = bf16[2,4,3,4,1024,128]{5,4,3,2,1,0:T(8,128)(2,1)} custom-call(bf16[8,128,1024]{2,1,0:T(8,128)(2,1)} %get-tuple-element.168.refs_0_, bf16[8,128,1024]{2,1,0:T(8,128)(2,1)} %get-tuple-element.169.refs_1_, bf16[8,128,1024]{2,1,0:T(8,128)(2,1)} %get-tuple-element.200.refs_0_.refs_2_, ...), custom_call_target="tpu_custom_call" | custom-call | flops 1300000000 | tf_op jit(solution)/shard_map/wgrad/pallas_call | solution.py:420
  278.9 13.5 %wgrad.3 = bf16[2,4,3,4,1024,128]{5,4,3,2,1,0:T(8,128)(2,1)} custom-call(bf16[8,128,1024]{2,1,0:T(8,128)(2,1)} %get-tuple-element.168.refs_0_, bf16[8,128,1024]{2,1,0:T(8,128)(2,1)} %get-tuple-element.169.refs_1_, bf16[8,128,1024]{2,1,0:T(8,128)(2,1)} %get-tuple-element.200.refs_0_.refs_2_, ...), custom_call_target="tpu_custom_call", output_to_operand_aliasing={{}: (16, {})} | custom-call | flops 1300000000 | tf_op jit(solution)/shard_map/wgrad/pallas_call | solution.py:420
  297.8 5.6 merge_back.2
  303.4 14.1 %collective-permute-done.16 = bf16[512,1152]{1,0:T(8,128)(2,1)S(1)} collective-permute-done((bf16[512,1152]{1,0:T(8,128)(2,1)}, bf16[512,1152]{1,0:T(8,128)(2,1)S(1)}, u32[]{:S(2)}, u32[]{:S(2)}) %collective-permute-start.16) | collective-permute-done | bytes 1179680 | tf_op jit(solution)/shard_map/ppermute | solution.py:661
  319.2 6.0 collective-permute-start.15
  325.2 5.0 merge_out.2
  337.1 8.9 %collective-permute-done.15 = bf16[512,1152]{1,0:T(8,128)(2,1)S(1)} collective-permute-done((bf16[512,1152]{1,0:T(8,128)(2,1)S(1)}, bf16[512,1152]{1,0:T(8,128)(2,1)S(1)}, u32[]{:S(2)}, u32[]{:S(2)}) %collective-permute-start.15) | collective-permute-done | bytes 1179680 | tf_op jit(solution)/shard_map/ppermute | solution.py:673
  359.3 17.7 %collective-permute-done.21 = bf16[512,1024]{1,0:T(8,128)(2,1)S(1)} collective-permute-done((bf16[512,1024]{1,0:T(8,128)(2,1)S(1)}, bf16[512,1024]{1,0:T(8,128)(2,1)S(1)}, u32[]{:S(2)}, u32[]{:S(2)}) %collective-permute-start.21) | collective-permute-done | bytes 1048608 | tf_op jit(solution)/shard_map/ppermute | solution.py:661
  377.0 22.1 %collective-permute-done.20 = bf16[512,1024]{1,0:T(8,128)(2,1)S(1)} collective-permute-done((bf16[512,1024]{1,0:T(8,128)(2,1)S(1)}, bf16[512,1024]{1,0:T(8,128)(2,1)S(1)}, u32[]{:S(2)}, u32[]{:S(2)}) %collective-permute-start.20) | collective-permute-done | bytes 1048608 | tf_op jit(solution)/shard_map/ppermute | solution.py:661
  413.9 40.4 %attend_back.1 = bf16[2048,512]{1,0:T(8,128)(2,1)} custom-call(s32[1]{0:T(128)S(6)} %copy.68.prefix_ref, bf16[4,2048,128]{2,1,0:T(8,128)(2,1)} %get-tuple-element.145.q_ref, bf16[2048,128]{1,0:T(8,128)(2,1)S(1)} %copy-done.53, bf16[2048,256]{1,0:T(8,128)(2,1)S(1)} %copy-done.50, bf16[2048,256]{1,0:T(8,128)(2,1)S(1)} %copy-done.2, ...), custom_call_target="tpu_custom_call" | custom-call | flops 4600000000 | tf_op jit(solution)/shard_map/attend_back/pallas_call | solution.py:246
  454.5 5.9 multiply_reduce_fusion
  461.7 10.7 %reduce-scatter.3.cloned.1.call-done = bf16[1,3,4,1024,128]{4,3,2,1,0:T(8,128)(2,1)} async-done(((bf16[8,3,4,1024,128]{4,3,2,1,0:T(8,128)(2,1)}), bf16[1,3,4,1024,128]{4,3,2,1,0:T(8,128)(2,1)}) %reduce-scatter.3.cloned.1.call-update) | async-done | bytes 3145744 | tf_op jit(solution)/shard_map/reduce_scatter | solution.py:791
  486.5 34.2 %collective-permute-done.27 = bf16[512,1024]{1,0:T(8,128)(2,1)S(1)} collective-permute-done((bf16[512,1024]{1,0:T(8,128)(2,1)S(1)}, bf16[512,1024]{1,0:T(8,128)(2,1)S(1)}, u32[]{:S(2)}, u32[]{:S(2)}) %collective-permute-start.27) | collective-permute-done | bytes 1048608 | tf_op jit(solution)/shard_map/ppermute | solution.py:673
  520.6 23.8 %reduce-scatter.5.cloned.1.call-done = bf16[192,512]{1,0:T(8,128)(2,1)} async-done(((bf16[1536,512]{1,0:T(8,128)(2,1)}), bf16[192,512]{1,0:T(8,128)(2,1)}) %reduce-scatter.5.cloned.1.call-update) | async-done | bytes 196624 | tf_op jit(solution)/shard_map/reduce_scatter | solution.py:835
  571.9 5.6 finish.2.refs_0_
  577.6 5.6 finish.3
  583.1 7.4 %all-gather.4.cloned.1.call-done = bf16[1536,512]{1,0:T(8,128)(2,1)} async-done(((bf16[192,512]{1,0:T(8,128)(2,1)}), bf16[1536,512]{1,0:T(8,128)(2,1)}) %all-gather.4.cloned.1.call-update) | async-done | bytes 1572880 | tf_op jit(solution)/shard_map/all_gather | solution.py:849
  (277 shorter events, 157.4 us)
Async XLA Ops:
  7.2 174.9 %all-gather.6.cloned.1.call-start = ((), (), s32[]{:S(2)}) async-start(), calls=%async_computation.5 | async-start | bytes 28311552 | tf_op jit(solution)/shard_map/all_gather | solution.py:712
  11.2 461.1 %reduce-scatter.3.cloned.1.call-start = ((), (), s32[]{:S(2)}) async-start(), calls=%async_computation.2 | async-start | bytes 28311552 | tf_op jit(solution)/shard_map/reduce_scatter | solution.py:791
  14.2 38.3 %collective-permute-start.1 = (bf16[512,1152]{1,0:T(8,128)(2,1)S(1)}, bf16[512,1152]{1,0:T(8,128)(2,1)S(1)}, u32[]{:S(2)}, u32[]{:S(2)}) collective-permute-start(bf16[512,1152]{1,0:T(8,128)(2,1)S(1)} %fusion.1.refs_1_), channel_id=1, source_target_pairs={{8,16},{16,8},{9,17},{17,9},{10,18},{18,10},{11,19},{19,11},{12,20... | collective-permute-start | bytes 3538952 | tf_op jit(solution)/shard_map/ppermute | solution.py:645
  14.9 37.6 %collective-permute-start = (bf16[512,1152]{1,0:T(8,128)(2,1)S(1)}, bf16[512,1152]{1,0:T(8,128)(2,1)}, u32[]{:S(2)}, u32[]{:S(2)}) collective-permute-start(bf16[512,1152]{1,0:T(8,128)(2,1)S(1)} %fusion.1.refs_1_), channel_id=1, source_target_pairs={{0,8},{8,0},{16,24},{24,16},{1,9},{9,1},{17,25},{25,17},{2,10},{10... | collective-permute-start | bytes 3538952 | tf_op jit(solution)/shard_map/ppermute | solution.py:645
  52.5 18.4 %collective-permute-start.2 = (bf16[512,1152]{1,0:T(8,128)(2,1)}, bf16[512,1152]{1,0:T(8,128)(2,1)}, u32[]{:S(2)}, u32[]{:S(2)}) collective-permute-start(bf16[512,1152]{1,0:T(8,128)(2,1)} %collective-permute-done.refs_1_), channel_id=1, source_target_pairs={{8,16},{16,8},{9,17},{17,9},{10,18},{18,10},{11,19},{19,11},{12,20... | collective-permute-start | bytes 3538952 | tf_op jit(solution)/shard_map/ppermute | solution.py:649
  75.8 7.5 %collective-permute-start.3 = (bf16[512,1024]{1,0:T(8,128)(2,1)}, bf16[512,1024]{1,0:T(8,128)(2,1)}, u32[]{:S(2)}, u32[]{:S(2)}) collective-permute-start(bf16[512,1024]{1,0:T(8,128)(2,1)} %convolution_convert_fusion.2), channel_id=1, source_target_pairs={{0,1},{1,0},{2,3},{3,2},{4,5},{5,4},{6,7},{7,6},{8,9},{9,8},{10,11... | collective-permute-start | bytes 3145736 | tf_op jit(solution)/shard_map/ppermute | solution.py:615
  76.3 39.2 %collective-permute-start.6 = (bf16[512,1152]{1,0:T(8,128)(2,1)S(1)}, bf16[512,1152]{1,0:T(8,128)(2,1)}, u32[]{:S(2)}, u32[]{:S(2)}) collective-permute-start(bf16[512,1152]{1,0:T(8,128)(2,1)S(1)} %collective-permute-done.1.refs_3_), channel_id=1, source_target_pairs={{8,0},{16,24},{9,1},{17,25},{10,2},{18,26},{11,3},{19,27},{12,4},{... | collective-permute-start | bytes 3538952 | tf_op jit(solution)/shard_map/ppermute | solution.py:649
  77.6 62.5 %collective-permute-start.7 = (bf16[512,1152]{1,0:T(8,128)(2,1)}, bf16[512,1152]{1,0:T(8,128)(2,1)}, u32[]{:S(2)}, u32[]{:S(2)}) collective-permute-start(bf16[512,1152]{1,0:T(8,128)(2,1)} %collective-permute-done.2.refs_3_), channel_id=1, source_target_pairs={{8,0},{16,24},{9,1},{17,25},{10,2},{18,26},{11,3},{19,27},{12,4},{... | collective-permute-start | bytes 3538952 | tf_op jit(solution)/shard_map/ppermute | solution.py:653
  81.7 58.4 %collective-permute-start.5 = (bf16[512,1024]{1,0:T(8,128)(2,1)}, bf16[512,1024]{1,0:T(8,128)(2,1)}, u32[]{:S(2)}, u32[]{:S(2)}) collective-permute-start(bf16[512,1024]{1,0:T(8,128)(2,1)} %add_convert_fusion.9), channel_id=1, source_target_pairs={{0,2},{2,0},{1,3},{3,1},{4,6},{6,4},{5,7},{7,5},{8,10},{10,8},{9,1... | collective-permute-start | bytes 3145736 | tf_op jit(solution)/shard_map/ppermute | solution.py:615
  143.5 13.7 %collective-permute-start.9 = (bf16[512,1024]{1,0:T(8,128)(2,1)S(1)}, bf16[512,1024]{1,0:T(8,128)(2,1)}, u32[]{:S(2)}, u32[]{:S(2)}) collective-permute-start(bf16[512,1024]{1,0:T(8,128)(2,1)S(1)} %multiply_convert_fusion.refs_0_), channel_id=1, source_target_pairs={{8,16},{16,8},{9,17},{17,9},{10,18},{18,10},{11,19},{19,11},{12,20... | collective-permute-start | bytes 3145736 | tf_op jit(solution)/shard_map/ppermute | solution.py:645
  145.2 26.1 %collective-permute-start.8 = (bf16[512,1024]{1,0:T(8,128)(2,1)S(1)}, bf16[512,1024]{1,0:T(8,128)(2,1)}, u32[]{:S(2)}, u32[]{:S(2)}) collective-permute-start(bf16[512,1024]{1,0:T(8,128)(2,1)S(1)} %multiply_convert_fusion.refs_0_), channel_id=1, source_target_pairs={{0,8},{8,0},{16,24},{24,16},{1,9},{9,1},{17,25},{25,17},{2,10},{10... | collective-permute-start | bytes 3145736 | tf_op jit(solution)/shard_map/ppermute | solution.py:645
  171.3 23.5 %collective-permute-start.10 = (bf16[512,1024]{1,0:T(8,128)(2,1)}, bf16[512,1024]{1,0:T(8,128)(2,1)}, u32[]{:S(2)}, u32[]{:S(2)}) collective-permute-start(bf16[512,1024]{1,0:T(8,128)(2,1)} %collective-permute-done.8.refs_0_), channel_id=1, source_target_pairs={{8,16},{16,8},{9,17},{17,9},{10,18},{18,10},{11,19},{19,11},{12,20... | collective-permute-start | bytes 3145736 | tf_op jit(solution)/shard_map/ppermute | solution.py:649
  172.9 26.3 %collective-permute-start.11 = (bf16[512,1024]{1,0:T(8,128)(2,1)}, bf16[512,1024]{1,0:T(8,128)(2,1)}, u32[]{:S(2)}, u32[]{:S(2)}) collective-permute-start(bf16[512,1024]{1,0:T(8,128)(2,1)} %collective-permute-done.9.refs_1_), channel_id=1, source_target_pairs={{8,0},{16,24},{9,1},{17,25},{10,2},{18,26},{11,3},{19,27},{12,4},{... | collective-permute-start | bytes 3145736 | tf_op jit(solution)/shard_map/ppermute | solution.py:649
  199.2 24.2 %collective-permute-start.12 = (bf16[512,1024]{1,0:T(8,128)(2,1)}, bf16[512,1024]{1,0:T(8,128)(2,1)S(1)}, u32[]{:S(2)}, u32[]{:S(2)}) collective-permute-start(bf16[512,1024]{1,0:T(8,128)(2,1)} %collective-permute-done.10.refs_1_), channel_id=1, source_target_pairs={{8,0},{16,24},{9,1},{17,25},{10,2},{18,26},{11,3},{19,27},{12,4},{... | collective-permute-start | bytes 3145736 | tf_op jit(solution)/shard_map/ppermute | solution.py:653
  261.5 30.9 %collective-permute-start.13 = (bf16[512,1152]{1,0:T(8,128)(2,1)S(1)}, bf16[512,1152]{1,0:T(8,128)(2,1)S(1)}, u32[]{:S(2)}, u32[]{:S(2)}) collective-permute-start(bf16[512,1152]{1,0:T(8,128)(2,1)S(1)} %get-tuple-element.209), channel_id=1, source_target_pairs={{0,8},{24,16},{1,9},{25,17},{2,10},{26,18},{3,11},{27,19},{4,12},{... | collective-permute-start | bytes 3538952 | tf_op jit(solution)/shard_map/ppermute | solution.py:661
  293.5 250.9 %reduce-scatter.5.cloned.1.call-start = ((), (), s32[]{:S(2)}) async-start(), calls=%async_computation.3 | async-start | bytes 1769472 | tf_op jit(solution)/shard_map/reduce_scatter | solution.py:835
  293.6 23.9 %collective-permute-start.16 = (bf16[512,1152]{1,0:T(8,128)(2,1)}, bf16[512,1152]{1,0:T(8,128)(2,1)S(1)}, u32[]{:S(2)}, u32[]{:S(2)}) collective-permute-start(bf16[512,1152]{1,0:T(8,128)(2,1)} %copy-done.13), channel_id=1, source_target_pairs={{0,8},{24,16},{1,9},{25,17},{2,10},{26,18},{3,11},{27,19},{4,12},{... | collective-permute-start | bytes 3538952 | tf_op jit(solution)/shard_map/ppermute | solution.py:661
  297.0 21.9 %collective-permute-start.14 = (bf16[512,1152]{1,0:T(8,128)(2,1)S(1)}, bf16[512,1152]{1,0:T(8,128)(2,1)S(1)}, u32[]{:S(2)}, u32[]{:S(2)}) collective-permute-start(bf16[512,1152]{1,0:T(8,128)(2,1)S(1)} %add_convert_fusion.4), channel_id=1, source_target_pairs={{8,16},{16,8},{9,17},{17,9},{10,18},{18,10},{11,19},{19,11},{12,20... | collective-permute-start | bytes 3538952 | tf_op jit(solution)/shard_map/ppermute | solution.py:669
  317.8 19.3 %collective-permute-start.17 = (bf16[512,1152]{1,0:T(8,128)(2,1)S(1)}, bf16[512,1152]{1,0:T(8,128)(2,1)S(1)}, u32[]{:S(2)}, u32[]{:S(2)}) collective-permute-start(bf16[512,1152]{1,0:T(8,128)(2,1)S(1)} %add_convert_fusion.2), channel_id=1, source_target_pairs={{8,16},{16,8},{9,17},{17,9},{10,18},{18,10},{11,19},{19,11},{12,20... | collective-permute-start | bytes 3538952 | tf_op jit(solution)/shard_map/ppermute | solution.py:669
  319.2 26.8 %collective-permute-start.15 = (bf16[512,1152]{1,0:T(8,128)(2,1)S(1)}, bf16[512,1152]{1,0:T(8,128)(2,1)S(1)}, u32[]{:S(2)}, u32[]{:S(2)}) collective-permute-start(bf16[512,1152]{1,0:T(8,128)(2,1)S(1)} %add_convert_fusion.3), channel_id=1, source_target_pairs={{0,8},{8,0},{16,24},{24,16},{1,9},{9,1},{17,25},{25,17},{2,10},{10... | collective-permute-start | bytes 3538952 | tf_op jit(solution)/shard_map/ppermute | solution.py:673
  349.6 7.1 %collective-permute-start.19 = (bf16[512,1024]{1,0:T(8,128)(2,1)S(1)}, bf16[512,1024]{1,0:T(8,128)(2,1)S(1)}, u32[]{:S(2)}, u32[]{:S(2)}) collective-permute-start(bf16[512,1024]{1,0:T(8,128)(2,1)S(1)} %subtract_convert_fusion.refs_0_), channel_id=1, source_target_pairs={{0,1},{1,0},{2,3},{3,2},{4,5},{5,4},{6,7},{7,6},{8,9},{9,8},{10,11... | collective-permute-start | bytes 3145736 | tf_op jit(solution)/shard_map/ppermute | solution.py:615
  349.7 27.3 %collective-permute-start.21 = (bf16[512,1024]{1,0:T(8,128)(2,1)S(1)}, bf16[512,1024]{1,0:T(8,128)(2,1)S(1)}, u32[]{:S(2)}, u32[]{:S(2)}) collective-permute-start(bf16[512,1024]{1,0:T(8,128)(2,1)S(1)} %get-tuple-element.230), channel_id=1, source_target_pairs={{0,8},{24,16},{1,9},{25,17},{2,10},{26,18},{3,11},{27,19},{4,12},{... | collective-permute-start | bytes 3145736 | tf_op jit(solution)/shard_map/ppermute | solution.py:661
  353.6 45.5 %collective-permute-start.20 = (bf16[512,1024]{1,0:T(8,128)(2,1)S(1)}, bf16[512,1024]{1,0:T(8,128)(2,1)S(1)}, u32[]{:S(2)}, u32[]{:S(2)}) collective-permute-start(bf16[512,1024]{1,0:T(8,128)(2,1)S(1)} %get-tuple-element.234), channel_id=1, source_target_pairs={{0,8},{24,16},{1,9},{25,17},{2,10},{26,18},{3,11},{27,19},{4,12},{... | collective-permute-start | bytes 3145736 | tf_op jit(solution)/shard_map/ppermute | solution.py:661
  355.0 48.4 %collective-permute-start.18 = (bf16[512,1024]{1,0:T(8,128)(2,1)S(1)}, bf16[512,1024]{1,0:T(8,128)(2,1)}, u32[]{:S(2)}, u32[]{:S(2)}) collective-permute-start(bf16[512,1024]{1,0:T(8,128)(2,1)S(1)} %subtract_convert_fusion.refs_0_), channel_id=1, source_target_pairs={{0,2},{2,0},{1,3},{3,1},{4,6},{6,4},{5,7},{7,5},{8,10},{10,8},{9,1... | collective-permute-start | bytes 3145736 | tf_op jit(solution)/shard_map/ppermute | solution.py:615
  405.4 56.3 %collective-permute-start.23 = (bf16[512,1024]{1,0:T(8,128)(2,1)}, bf16[512,1024]{1,0:T(8,128)(2,1)S(1)}, u32[]{:S(2)}, u32[]{:S(2)}) collective-permute-start(bf16[512,1024]{1,0:T(8,128)(2,1)} %get-tuple-element.251), channel_id=1, source_target_pairs={{8,16},{16,8},{9,17},{17,9},{10,18},{18,10},{11,19},{19,11},{12,20... | collective-permute-start | bytes 3145736 | tf_op jit(solution)/shard_map/ppermute | solution.py:823
  406.2 55.4 %collective-permute-start.24 = (bf16[512,1024]{1,0:T(8,128)(2,1)}, bf16[512,1024]{1,0:T(8,128)(2,1)}, u32[]{:S(2)}, u32[]{:S(2)}) collective-permute-start(bf16[512,1024]{1,0:T(8,128)(2,1)} %get-tuple-element.252), channel_id=1, source_target_pairs={{8,16},{16,8},{9,17},{17,9},{10,18},{18,10},{11,19},{19,11},{12,20... | collective-permute-start | bytes 3145736 | tf_op jit(solution)/shard_map/ppermute | solution.py:823
  475.3 115.3 %all-gather.4.cloned.1.call-start = ((), (), s32[]{:S(2)}) async-start(), calls=%async_computation.4 | async-start | bytes 1769472 | tf_op jit(solution)/shard_map/all_gather | solution.py:849
  483.1 61.4 %collective-permute-start.26 = (bf16[2,512,1024]{2,1,0:T(8,128)(2,1)S(1)}, bf16[2,512,1024]{2,1,0:T(8,128)(2,1)}, u32[]{:S(2)}, u32[]{:S(2)}) collective-permute-start(bf16[2,512,1024]{2,1,0:T(8,128)(2,1)S(1)} %add_convert_fusion.1), channel_id=1, source_target_pairs={{0,2},{2,0},{1,3},{3,1},{4,6},{6,4},{5,7},{7,5},{8,10},{10,8},{9,1... | collective-permute-start | bytes 6291464 | tf_op jit(solution)/shard_map/ppermute | solution.py:615
  484.9 35.8 %collective-permute-start.27 = (bf16[512,1024]{1,0:T(8,128)(2,1)S(1)}, bf16[512,1024]{1,0:T(8,128)(2,1)S(1)}, u32[]{:S(2)}, u32[]{:S(2)}) collective-permute-start(bf16[512,1024]{1,0:T(8,128)(2,1)S(1)} %add_convert_fusion.6), channel_id=1, source_target_pairs={{0,8},{8,0},{16,24},{24,16},{1,9},{9,1},{17,25},{25,17},{2,10},{10... | collective-permute-start | bytes 3145736 | tf_op jit(solution)/shard_map/ppermute | solution.py:673
  547.2 30.4 %collective-permute-start.28 = (bf16[2,512,1024]{2,1,0:T(8,128)(2,1)S(1)}, bf16[2,512,1024]{2,1,0:T(8,128)(2,1)S(1)}, u32[]{:S(2)}, u32[]{:S(2)}) collective-permute-start(bf16[2,512,1024]{2,1,0:T(8,128)(2,1)S(1)} %add_convert_fusion), channel_id=1, source_target_pairs={{0,1},{1,0},{2,3},{3,2},{4,5},{5,4},{6,7},{7,6},{8,9},{9,8},{10,11... | collective-permute-start | bytes 6291464 | tf_op jit(solution)/shard_map/ppermute | solution.py:615
  560.7 5.7 collective-permute-start.32
  566.4 11.1 %collective-permute-start.33 = (bf16[40,1024]{1,0:T(8,128)(2,1)S(1)}, bf16[40,1024]{1,0:T(8,128)(2,1)S(1)}, u32[]{:S(2)}, u32[]{:S(2)}) collective-permute-start(bf16[40,1024]{1,0:T(8,128)(2,1)S(1)} %add_convert_fusion.10), channel_id=1, source_target_pairs={{0,16},{8,24},{16,0},{24,8},{1,17},{9,25},{17,1},{25,9},{2,18},{10... | collective-permute-start | bytes 245768 | tf_op jit(solution)/shard_map/ppermute | solution.py:615
  (80 other events, 581.7 us)
Sparse Core Ops, SparseCore 0:
  11.3 149.3 all-gather.5
  293.6 178.6 reduce-scatter.2
  476.4 68.0 reduce-scatter.4
  546.7 43.8 all-gather.3

commit v5 on v4

--- a/solution.py
+++ b/solution.py
@@ -47,6 +47,10 @@
 BQ = 512
 BK = 1024
 BK_BACK = 512
+
+def from_hbm(*arrays):
+    return [pltpu.with_memory_space_constraint(a, pltpu.HBM) for a in arrays]
+
 
 def busy(us):
     return pl.CostEstimate(flops=int(us * 1e8), bytes_accessed=0, transcendentals=0)
@@ -94,7 +98,7 @@
         compiler_params=pltpu.CompilerParams(vmem_limit_bytes=40 << 20),
         cost_estimate=busy(9),
         name="project",
-    )(tokens, gain, wq, wk, wv, cos, sin)
+    )(*from_hbm(tokens), gain, wq, wk, wv, cos, sin)
 
 def attend_kernel(bq, bk, kv, prefix_ref, q_ref, k_ref, v_ref, *refs):
     o_ref, lse_ref, s_ref = refs[-3:]
@@ -168,7 +172,7 @@
         compiler_params=pltpu.CompilerParams(vmem_limit_bytes=48 << 20),
         cost_estimate=busy(14),
         name="attend",
-    )(prefix, q, k, v, *before)
+    )(prefix, *from_hbm(q, k, v), *before)
 
 
 def attend_back_kernel(bq, bk, prefix_ref, q_ref, k_ref, v_ref, o_ref, do_ref, lse_ref, cos_ref, sin_ref, cosa_ref, sina_ref,
@@ -610,6 +614,30 @@
     )(parts)
 
 
+def out_kernel(rank_ref, a_ref, b_ref, w_ref, keep_ref, send_ref):
+    keep_ref[...] = jnp.dot(a_ref[...], w_ref[...], preferred_element_type=f32)
+    send_ref[...] = jnp.dot(b_ref[...], w_ref[...], preferred_element_type=f32).astype(bf16)
+
+
+def out_pair(rank, bits, attended, w_out, rows):
+    H, D = w_out.shape
+    step = min(256, rows)
+    n = rows // step
+    block = lambda bit: pl.BlockSpec((step, H), lambda i, p: ((p[0] ^ bit) * n + i, 0))
+    out = pl.BlockSpec((step, D), lambda i, p: (i, 0))
+    return pl.pallas_call(
+        out_kernel,
+        grid_spec=pltpu.PrefetchScalarGridSpec(
+            num_scalar_prefetch=1, grid=(n,),
+            in_specs=[block(bits[0]), block(bits[1]), pl.BlockSpec((H, D), lambda i, p: (0, 0))],
+            out_specs=[out, out]),
+        out_shape=[jax.ShapeDtypeStruct((rows, D), f32), jax.ShapeDtypeStruct((rows, D), bf16)],
+        compiler_params=pltpu.CompilerParams(vmem_limit_bytes=32 << 20),
+        cost_estimate=busy(3),
+        name="out_pair",
+    )(rank, attended, attended, w_out)
+
+
 def swap(x, axis, bit=1):
     count = lax.axis_size(axis)
     return lax.ppermute(x, axis, [(i, i ^ bit) for i in range(count)])
@@ -708,10 +736,6 @@
     local = w_gate.shape[0]
     cap = own_rows * TOPK // EXPERTS
 
-    own_weights = jnp.stack([w_gate, w_up, w_down.transpose(0, 2, 1)])
-    weights = lax.all_gather(own_weights, ("y", "x", "c"), axis=0, tiled=False)
-    weights = weights.reshape((groups, shards) + own_weights.shape)
-
     expert_ids = jnp.arange(EXPERTS, dtype=jnp.int32)
     member = jnp.sum((routes[:, :, None] == expert_ids[None, None, :]).astype(f32), 1)
     priority = fill_order[0]
@@ -726,22 +750,24 @@
     shift_end = jnp.concatenate([shift, at_end.astype(jnp.int32)[None]])
 
 
+    own_weights = jnp.stack([w_gate, w_up, w_down.transpose(0, 2, 1)])
+    weights = lax.all_gather(own_weights, ("y", "x", "c"), axis=0, tiled=False)
+    weights = weights.reshape((groups, shards) + own_weights.shape)
+
     cos, sin = wide_tables(length)
     normed_one, query, key, value = project(tokens, gain_attn[None], w_query, w_key, w_value, cos, sin)
     first_half = attend(prefix, query, key, value, 0, BQ, BK)
     *first_half, side_near, side_across = hold(*first_half, side_near, side_across)
     side_far, side_relay = line_second(side_near, side_across)
     attended, log_total = attend(prefix, query, key, value, 1, BQ, BK, first_half)
-    attended, side_far = hold(attended, side_far)
+    rank_row = rank.astype(jnp.int32)[None]
+    far_keep, far_send = out_pair(rank_row, (2, 3), attended, w_out, own_rows)
+    far_keep, side_far = hold(far_keep, side_far)
     side_last = line_third(side_far)
-
-    def out_block(place):
-        rows = lax.dynamic_slice_in_dim(attended, place * own_rows, own_rows, 0)
-        return jnp.dot(rows, w_out, preferred_element_type=f32)
-
-    far_sum = out_block(rank ^ 2) + swap(out_block(rank ^ 3).astype(bf16), "c").astype(f32)
+    far_sum = far_keep + swap(far_send, "c").astype(f32)
     far_got = swap(far_sum.astype(bf16), "x")
-    near_sum = out_block(rank) + swap(out_block(rank ^ 1).astype(bf16), "c").astype(f32)
+    near_keep, near_send = out_pair(rank_row, (0, 1), attended, w_out, own_rows)
+    near_sum = near_keep + swap(near_send, "c").astype(f32)
     near_sum, far_got, side_relay, side_last = hold(near_sum, far_got, side_relay, side_last)
     x_rows = lax.dynamic_slice_in_dim(tokens, rank * own_rows, own_rows, 0).astype(f32)
     hidden_in = x_rows + near_sum + far_got.astype(f32)
@@ -811,7 +837,6 @@
     ).astype(bf16)
     small = jnp.concatenate([router_part, gain_two_part[None], jnp.zeros((7, width), f32)], 0)
     hidden_over_x = swap(hidden_grad, "x")
-    rank_row = rank.astype(jnp.int32)[None]
     near_done = spread(rank_row, 0, [hidden_grad, swap(hidden_grad, "c")], attended, w_out)
     *near_done, out_end_far, out_end = hold(*near_done, out_end_far, out_end)
     out_two, out_three = add_low(out_parts[2], out_end_far), add_low(out_parts[3], out_end)

time: 613 us -> 595 us (0.971)
  waiting for transfers between devices: 231 us -> 217 us
  local copies, waits for them, and re-layouts: 37.8 us -> 24.6 us
  Pallas kernels: 219 us -> 230 us
  matrix products: 23.8 us -> 13.1 us
    ppermute x14, waiting for transfers between devices: 17.7 us -> 39.2 us  [swap(): return lax.ppermute(x, axis, [(i, i ^ bit) for i in range(count)])]
    ppermute x2, waiting for transfers between devices: 26 us -> 4.75 us  [line_third(): return lax.ppermute(across_far, 'z', TO_ENDS)]
    unnamed x152 -> x128, local copies, waits for them, and re-layouts: 29.5 us -> 17.3 us
    dot_general x4 -> x0, matrix products: 9.14 us -> none  [out_block(): return jnp.dot(rows, w_out, preferred_element_type=f32)]
    ppermute x4, waiting for transfers between devices: 34.9 us -> 26.1 us  [line_second(): return (lax.ppermute(near, 'z', MIDDLE), lax.ppermute(across, 'z', TO_ENDS))]
  transfers between devices with their start and end apart: 38 -> 38, of which waited for: 19 -> 20; matrix products, arithmetic and copies ran while one was open for 7% -> 6% of each run, Pallas kernels for 31% -> 33%
where the time goes in v5:
time: 595 us; the launch traced here: 585 us
  Pallas kernels  230 us (39%)
  waiting for transfers between devices  217 us (36%)
  starting transfers between devices  60.7 us (10%)
  local copies, waits for them, and re-layouts  24.6 us (4%)
  other arithmetic  24.3 us (4%)
  between operations  15.9 us (3%)
  matrix products  13.1 us (2%)
    pallas_call x3, Pallas kernels, ffn(): pl.pallas_call(functools.partial(ffn_kernel, n, blocks), grid=(len(groups...  48.2 us
    pallas_call x1, Pallas kernels, attend_back(): pl.pallas_call(functools.partial(attend_back_kernel, bq, bk), grid_spec=p...  40.9 us
    ppermute x2, waiting for transfers between devices, line_in(): return lax.ppermute(add_low(part, across_far), 'z', NEAR)  39.7 us
    ppermute x14, waiting for transfers between devices, swap(): return lax.ppermute(x, axis, [(i, i ^ bit) for i in range(count)])  39.2 us
    pallas_call x2, Pallas kernels, attend(): pl.pallas_call(functools.partial(attend_kernel, bq, bk, kv), grid_spec=pl...  31.8 us
    ppermute x2, waiting for transfers between devices, line_out(): lax.ppermute(parts[2], 'z', FROM_ENDS)  30.7 us
    pallas_call x2, Pallas kernels, wgrad(): pl.pallas_call(functools.partial(wgrad_kernel, n, len(acts), blocks), gri...  27.1 us
    ppermute x4, waiting for transfers between devices, line_second(): return (lax.ppermute(near, 'z', MIDDLE), lax.ppermute(across, 'z', TO_ENDS))  26.1 us
  transfers between devices with their start and end apart: 38, of which 20 were waited for; matrix products, arithmetic and copies ran while one was open for 6% of the time, Pallas kernels for 33%

profile of v5, /device:TPU:0, one launch (start us, length us, event | category | flops | bytes accessed | tf_op | source)
XLA Modules:
  0.0 585.0 jit_solution(11284921631944205534)
XLA Ops:
  22.5 11.2 %project.1 = (bf16[2048,1024]{1,0:T(8,128)(2,1)}, bf16[4,2048,128]{2,1,0:T(8,128)(2,1)}, bf16[2048,128]{1,0:T(8,128)(2,1)}, bf16[2048,256]{1,0:T(8,128)(2,1)}) custom-call(bf16[2048,1024]{1,0:T(8,128)(2,1)} %x_ref.5, bf16[1,1024]{1,0:T(2,128)(2,1)S(1)} %broadcast_in_dim.36.gain_ref, bf16[1024,256]{1,0:T(8,128)(2,1)S(1)} %copy-done.7, ...), custom_call_target="tpu_custom_call" | custom-call | flops 900000000 | tf_op jit(solution)/shard_map/project/pallas_call | solution.py:93
  33.7 15.9 %attend.2 = (bf16[2048,256]{1,0:T(8,128)(2,1)}, f32[2,8,4096]{2,1,0:T(8,128)}) custom-call(s32[1]{0:T(128)S(6)} %copy.68.prefix_ref, bf16[4,2048,128]{2,1,0:T(8,128)(2,1)} %get-tuple-element.149.q_ref, bf16[2048,128]{1,0:T(8,128)(2,1)} %get-tuple-element.150.k_ref, bf16[2048,256]{1,0:T(8,128)(2,1)} %get-tuple-element.151.v_ref), custom_call_target="tpu_custom_call" | custom-call | flops 1400000000 | tf_op jit(solution)/shard_map/attend/pallas_call | solution.py:159
  51.5 15.9 %attend.3 = (bf16[2048,256]{1,0:T(8,128)(2,1)}, f32[2,8,4096]{2,1,0:T(8,128)}) custom-call(s32[1]{0:T(128)S(6)} %copy.68.prefix_ref, bf16[4,2048,128]{2,1,0:T(8,128)(2,1)} %get-tuple-element.149.q_ref, bf16[2048,128]{1,0:T(8,128)(2,1)} %get-tuple-element.150.k_ref, ...), custom_call_target="tpu_custom_call", output_to_operand_aliasing={{0}: (4, {}), {1}: (5, {})} | custom-call | flops 1400000000 | tf_op jit(solution)/shard_map/attend/pallas_call | solution.py:159
  79.2 23.9 %collective-permute-done.6.refs_2_ = bf16[512,1152]{1,0:T(8,128)(2,1)} collective-permute-done((bf16[512,1152]{1,0:T(8,128)(2,1)}, bf16[512,1152]{1,0:T(8,128)(2,1)}, u32[]{:S(2)}, u32[]{:S(2)}) %collective-permute-start.6) | collective-permute-done | bytes 1179680 | tf_op jit(solution)/shard_map/ppermute | solution.py:677
  103.1 21.5 %collective-permute-done.5 = bf16[512,1024]{1,0:T(8,128)(2,1)} collective-permute-done((bf16[512,1024]{1,0:T(8,128)(2,1)}, bf16[512,1024]{1,0:T(8,128)(2,1)}, u32[]{:S(2)}, u32[]{:S(2)}) %collective-permute-start.5) | collective-permute-done | bytes 1048608 | tf_op jit(solution)/shard_map/ppermute | solution.py:643
  132.7 5.3 collective-permute-start.8
  140.2 5.4 pick.4
  146.3 12.6 %collective-permute-done.8.refs_0_ = bf16[512,1024]{1,0:T(8,128)(2,1)} collective-permute-done((bf16[512,1024]{1,0:T(8,128)(2,1)S(1)}, bf16[512,1024]{1,0:T(8,128)(2,1)}, u32[]{:S(2)}, u32[]{:S(2)}) %collective-permute-start.8) | collective-permute-done | bytes 1048608 | tf_op jit(solution)/shard_map/ppermute | solution.py:673
  161.9 6.5 %pick.5 = (bf16[8,128,1024]{2,1,0:T(8,128)(2,1)}, bf16[8,128,1024]{2,1,0:T(8,128)(2,1)}, f32[8,128,128]{2,1,0:T(8,128)}, f32[512,128]{1,0:T(8,128)S(1)}, f32[512,128]{1,0:T(8,128)S(1)}) custom-call(s32[9]{0:T(128)S(1)} %pad_add_fusion.shift_ref, bf16[512,1024]{1,0:T(8,128)(2,1)} %collective-permute-done.8.refs_0_, ...), custom_call_target="tpu_custom_call" | custom-call | flops 400000000 | tf_op jit(solution)/shard_map/pick/pallas_call | solution.py:317
  169.8 12.7 %ffn.3 = (bf16[8,256,1024]{2,1,0:T(8,128)(2,1)}, bf16[8,256,1024]{2,1,0:T(8,128)(2,1)}, f32[8,256,128]{2,1,0:T(8,128)}, bf16[8,256,512]{2,1,0:T(8,128)(2,1)}, bf16[8,256,1024]{2,1,0:T(8,128)(2,1)}) custom-call(bf16[8,128,1024]{2,1,0:T(8,128)(2,1)} %get-tuple-element.176.refs_0_, bf16[8,128,1024]{2,1,0:T(8,128)(2,1)} %get-tuple-element.177.refs_1_, ...), custom_call_target="tpu_custom_call" | custom-call | flops 1200000000 | tf_op jit(solution)/shard_map/ffn/pallas_call | solution.py:383
  186.0 7.1 %pick.6 = (bf16[8,128,1024]{2,1,0:T(8,128)(2,1)}, bf16[8,128,1024]{2,1,0:T(8,128)(2,1)}, f32[8,128,128]{2,1,0:T(8,128)}, f32[512,128]{1,0:T(8,128)S(1)}, f32[512,128]{1,0:T(8,128)S(1)}) custom-call(s32[9]{0:T(128)S(1)} %pad_add_fusion.shift_ref, bf16[512,1024]{1,0:T(8,128)(2,1)} %collective-permute-done.11.refs_0_, ...), custom_call_target="tpu_custom_call" | custom-call | flops 400000000 | tf_op jit(solution)/shard_map/pick/pallas_call | solution.py:317
  193.1 12.8 %ffn.4 = (bf16[8,256,1024]{2,1,0:T(8,128)(2,1)}, bf16[8,256,1024]{2,1,0:T(8,128)(2,1)}, f32[8,256,128]{2,1,0:T(8,128)}, bf16[8,256,512]{2,1,0:T(8,128)(2,1)}, bf16[8,256,1024]{2,1,0:T(8,128)(2,1)}) custom-call(bf16[8,128,1024]{2,1,0:T(8,128)(2,1)} %get-tuple-element.176.refs_0_, ...), custom_call_target="tpu_custom_call", output_to_operand_aliasing={{0}: (7, {}), {1}: (8, {}), {2}: (9, {}), {3}: (10, {}), {4... | custom-call | flops 1200000000 | tf_op jit(solution)/shard_map/ffn/pallas_call | solution.py:383
  207.9 6.9 %pick.7 = (bf16[8,128,1024]{2,1,0:T(8,128)(2,1)}, bf16[8,128,1024]{2,1,0:T(8,128)(2,1)}, f32[8,128,128]{2,1,0:T(8,128)}, f32[512,128]{1,0:T(8,128)S(1)}, f32[512,128]{1,0:T(8,128)S(1)}) custom-call(s32[9]{0:T(128)S(1)} %pad_add_fusion.shift_ref, bf16[512,1024]{1,0:T(8,128)(2,1)S(1)} %collective-permute-done.12.refs_0_, ...), custom_call_target="tpu_custom_call" | custom-call | flops 400000000 | tf_op jit(solution)/shard_map/pick/pallas_call | solution.py:317
  214.8 22.6 %ffn.5 = (bf16[8,256,1024]{2,1,0:T(8,128)(2,1)}, bf16[8,256,1024]{2,1,0:T(8,128)(2,1)}, f32[8,256,128]{2,1,0:T(8,128)}, bf16[8,256,512]{2,1,0:T(8,128)(2,1)}, bf16[8,256,1024]{2,1,0:T(8,128)(2,1)}) custom-call(bf16[8,128,1024]{2,1,0:T(8,128)(2,1)} %get-tuple-element.208.refs_0_.refs_2_, bf16[8,128,1024]{2,1,0:T(8,128)(2,1)} %get-tuple-element.209.refs_1_.refs_3_, ...), custom_call_target="tpu_custom_call" | custom-call | flops 2400000000 | tf_op jit(solution)/shard_map/ffn/pallas_call | solution.py:383
  246.8 13.5 %wgrad.2.refs_16_ = bf16[2,4,3,4,1024,128]{5,4,3,2,1,0:T(8,128)(2,1)} custom-call(bf16[8,128,1024]{2,1,0:T(8,128)(2,1)} %get-tuple-element.176.refs_0_, bf16[8,128,1024]{2,1,0:T(8,128)(2,1)} %get-tuple-element.177.refs_1_, bf16[8,128,1024]{2,1,0:T(8,128)(2,1)} %get-tuple-element.208.refs_0_.refs_2_, ...), custom_call_target="tpu_custom_call" | custom-call | flops 1300000000 | tf_op jit(solution)/shard_map/wgrad/pallas_call | solution.py:424
  260.4 13.5 %wgrad.3 = bf16[2,4,3,4,1024,128]{5,4,3,2,1,0:T(8,128)(2,1)} custom-call(bf16[8,128,1024]{2,1,0:T(8,128)(2,1)} %get-tuple-element.176.refs_0_, bf16[8,128,1024]{2,1,0:T(8,128)(2,1)} %get-tuple-element.177.refs_1_, bf16[8,128,1024]{2,1,0:T(8,128)(2,1)} %get-tuple-element.208.refs_0_.refs_2_, ...), custom_call_target="tpu_custom_call", output_to_operand_aliasing={{}: (16, {})} | custom-call | flops 1300000000 | tf_op jit(solution)/shard_map/wgrad/pallas_call | solution.py:424
  279.3 5.6 merge_back.2
  284.9 13.0 %collective-permute-done.16 = bf16[512,1152]{1,0:T(8,128)(2,1)S(1)} collective-permute-done((bf16[512,1152]{1,0:T(8,128)(2,1)}, bf16[512,1152]{1,0:T(8,128)(2,1)S(1)}, u32[]{:S(2)}, u32[]{:S(2)}) %collective-permute-start.16) | collective-permute-done | bytes 1179680 | tf_op jit(solution)/shard_map/ppermute | solution.py:689
  299.5 7.2 %collective-permute-start.15 = (bf16[512,1152]{1,0:T(8,128)(2,1)S(1)}, bf16[512,1152]{1,0:T(8,128)(2,1)S(1)}, u32[]{:S(2)}, u32[]{:S(2)}) collective-permute-start(bf16[512,1152]{1,0:T(8,128)(2,1)S(1)} %add_convert_fusion.3), channel_id=1, source_target_pairs={{0,8},{8,0},{16,24},{24,16},{1,9},{9,1},{17,25},{25,17},{2,10},{10... | collective-permute-start | bytes 3538952 | tf_op jit(solution)/shard_map/ppermute | solution.py:701
  306.7 5.1 merge_out.2
  318.6 5.8 collective-permute-done.15
  328.1 5.8 collective-permute-start.21
  339.6 17.7 %collective-permute-done.21 = bf16[512,1024]{1,0:T(8,128)(2,1)S(1)} collective-permute-done((bf16[512,1024]{1,0:T(8,128)(2,1)S(1)}, bf16[512,1024]{1,0:T(8,128)(2,1)S(1)}, u32[]{:S(2)}, u32[]{:S(2)}) %collective-permute-start.21) | collective-permute-done | bytes 1048608 | tf_op jit(solution)/shard_map/ppermute | solution.py:689
  357.3 22.1 %collective-permute-done.20 = bf16[512,1024]{1,0:T(8,128)(2,1)S(1)} collective-permute-done((bf16[512,1024]{1,0:T(8,128)(2,1)S(1)}, bf16[512,1024]{1,0:T(8,128)(2,1)S(1)}, u32[]{:S(2)}, u32[]{:S(2)}) %collective-permute-start.20) | collective-permute-done | bytes 1048608 | tf_op jit(solution)/shard_map/ppermute | solution.py:689
  395.3 40.9 %attend_back.1 = bf16[2048,512]{1,0:T(8,128)(2,1)} custom-call(s32[1]{0:T(128)S(6)} %copy.68.prefix_ref, bf16[4,2048,128]{2,1,0:T(8,128)(2,1)} %get-tuple-element.149.q_ref, bf16[2048,128]{1,0:T(8,128)(2,1)S(1)} %copy-done.41, bf16[2048,256]{1,0:T(8,128)(2,1)S(1)} %copy-done.40, bf16[2048,256]{1,0:T(8,128)(2,1)S(1)} %copy-done.1, ...), custom_call_target="tpu_custom_call" | custom-call | flops 4600000000 | tf_op jit(solution)/shard_map/attend_back/pallas_call | solution.py:250
  436.4 5.9 %multiply_reduce_fusion = (f32[1024]{0:T(1024)S(1)}, bf16[1024,512]{1,0:T(8,128)(2,1)S(1)}) fusion(bf16[1024,512]{1,0:T(8,128)(2,1)} %copy-done.53, bf16[2048,1024]{1,0:T(8,128)(2,1)} %get-tuple-element.256, bf16[2048,512]{1,0:T(8,128)(2,1)} %attend_back.1), kind=kOutput, calls=%fused_computation.11 | convolution fusion | flops 2149579776 | bytes 8392704 | tf_op jit(solution)/shard_map/id,ih->dh/dot_general | solution.py:853
  443.6 10.5 %reduce-scatter.3.cloned.1.call-done = bf16[1,3,4,1024,128]{4,3,2,1,0:T(8,128)(2,1)} async-done(((bf16[8,3,4,1024,128]{4,3,2,1,0:T(8,128)(2,1)}), bf16[1,3,4,1024,128]{4,3,2,1,0:T(8,128)(2,1)}) %reduce-scatter.3.cloned.1.call-update) | async-done | bytes 3145744 | tf_op jit(solution)/shard_map/reduce_scatter | solution.py:817
  468.7 33.9 %collective-permute-done.27 = bf16[512,1024]{1,0:T(8,128)(2,1)S(1)} collective-permute-done((bf16[512,1024]{1,0:T(8,128)(2,1)S(1)}, bf16[512,1024]{1,0:T(8,128)(2,1)S(1)}, u32[]{:S(2)}, u32[]{:S(2)}) %collective-permute-start.27) | collective-permute-done | bytes 1048608 | tf_op jit(solution)/shard_map/ppermute | solution.py:701
  502.6 23.4 %reduce-scatter.5.cloned.1.call-done = bf16[192,512]{1,0:T(8,128)(2,1)} async-done(((bf16[1536,512]{1,0:T(8,128)(2,1)}), bf16[192,512]{1,0:T(8,128)(2,1)}) %reduce-scatter.5.cloned.1.call-update) | async-done | bytes 196624 | tf_op jit(solution)/shard_map/reduce_scatter | solution.py:860
  553.4 5.7 finish.2.refs_0_
  559.2 5.6 finish.3
  564.8 7.4 %all-gather.4.cloned.1.call-done = bf16[1536,512]{1,0:T(8,128)(2,1)} async-done(((bf16[192,512]{1,0:T(8,128)(2,1)}), bf16[1536,512]{1,0:T(8,128)(2,1)}) %all-gather.4.cloned.1.call-update) | async-done | bytes 1572880 | tf_op jit(solution)/shard_map/all_gather | solution.py:874
  (253 shorter events, 146.1 us)
Async XLA Ops:
  7.2 162.6 %all-gather.6.cloned.1.call-start = ((), (), s32[]{:S(2)}) async-start(), calls=%async_computation.5 | async-start | bytes 28311552 | tf_op jit(solution)/shard_map/all_gather | solution.py:754
  11.2 442.9 %reduce-scatter.3.cloned.1.call-start = ((), (), s32[]{:S(2)}) async-start(), calls=%async_computation.2 | async-start | bytes 28311552 | tf_op jit(solution)/shard_map/reduce_scatter | solution.py:817
  13.7 35.9 %collective-permute-start.1 = (bf16[512,1152]{1,0:T(8,128)(2,1)S(1)}, bf16[512,1152]{1,0:T(8,128)(2,1)}, u32[]{:S(2)}, u32[]{:S(2)}) collective-permute-start(bf16[512,1152]{1,0:T(8,128)(2,1)S(1)} %fusion.1.refs_1_), channel_id=1, source_target_pairs={{8,16},{16,8},{9,17},{17,9},{10,18},{18,10},{11,19},{19,11},{12,20... | collective-permute-start | bytes 3538952 | tf_op jit(solution)/shard_map/ppermute | solution.py:673
  15.4 34.2 %collective-permute-start = (bf16[512,1152]{1,0:T(8,128)(2,1)S(1)}, bf16[512,1152]{1,0:T(8,128)(2,1)}, u32[]{:S(2)}, u32[]{:S(2)}) collective-permute-start(bf16[512,1152]{1,0:T(8,128)(2,1)S(1)} %fusion.1.refs_1_), channel_id=1, source_target_pairs={{0,8},{8,0},{16,24},{24,16},{1,9},{9,1},{17,25},{25,17},{2,10},{10... | collective-permute-start | bytes 3538952 | tf_op jit(solution)/shard_map/ppermute | solution.py:673
  49.6 23.7 %collective-permute-start.3 = (bf16[512,1152]{1,0:T(8,128)(2,1)}, bf16[512,1152]{1,0:T(8,128)(2,1)}, u32[]{:S(2)}, u32[]{:S(2)}) collective-permute-start(bf16[512,1152]{1,0:T(8,128)(2,1)} %collective-permute-done.refs_1_), channel_id=1, source_target_pairs={{8,16},{16,8},{9,17},{17,9},{10,18},{18,10},{11,19},{19,11},{12,20... | collective-permute-start | bytes 3538952 | tf_op jit(solution)/shard_map/ppermute | solution.py:677
  71.6 6.0 %collective-permute-start.2 = (bf16[512,1024]{1,0:T(8,128)(2,1)}, bf16[512,1024]{1,0:T(8,128)(2,1)}, u32[]{:S(2)}, u32[]{:S(2)}) collective-permute-start(bf16[512,1024]{1,0:T(8,128)(2,1)} %get-tuple-element.158), channel_id=1, source_target_pairs={{0,1},{1,0},{2,3},{3,2},{4,5},{5,4},{6,7},{7,6},{8,9},{9,8},{10,11... | collective-permute-start | bytes 3145736 | tf_op jit(solution)/shard_map/ppermute | solution.py:643
  72.0 31.0 %collective-permute-start.6 = (bf16[512,1152]{1,0:T(8,128)(2,1)}, bf16[512,1152]{1,0:T(8,128)(2,1)}, u32[]{:S(2)}, u32[]{:S(2)}) collective-permute-start(bf16[512,1152]{1,0:T(8,128)(2,1)} %collective-permute-done.1.refs_3_), channel_id=1, source_target_pairs={{8,0},{16,24},{9,1},{17,25},{10,2},{18,26},{11,3},{19,27},{12,4},{... | collective-permute-start | bytes 3538952 | tf_op jit(solution)/shard_map/ppermute | solution.py:677
  73.3 54.1 %collective-permute-start.7 = (bf16[512,1152]{1,0:T(8,128)(2,1)}, bf16[512,1152]{1,0:T(8,128)(2,1)}, u32[]{:S(2)}, u32[]{:S(2)}) collective-permute-start(bf16[512,1152]{1,0:T(8,128)(2,1)} %collective-permute-done.3.refs_3_), channel_id=1, source_target_pairs={{8,0},{16,24},{9,1},{17,25},{10,2},{18,26},{11,3},{19,27},{12,4},{... | collective-permute-start | bytes 3538952 | tf_op jit(solution)/shard_map/ppermute | solution.py:681
  76.0 48.5 %collective-permute-start.5 = (bf16[512,1024]{1,0:T(8,128)(2,1)}, bf16[512,1024]{1,0:T(8,128)(2,1)}, u32[]{:S(2)}, u32[]{:S(2)}) collective-permute-start(bf16[512,1024]{1,0:T(8,128)(2,1)} %add_convert_fusion.9), channel_id=1, source_target_pairs={{0,2},{2,0},{1,3},{3,1},{4,6},{6,4},{5,7},{7,5},{8,10},{10,8},{9,1... | collective-permute-start | bytes 3145736 | tf_op jit(solution)/shard_map/ppermute | solution.py:643
  130.8 15.4 %collective-permute-start.9 = (bf16[512,1024]{1,0:T(8,128)(2,1)S(1)}, bf16[512,1024]{1,0:T(8,128)(2,1)}, u32[]{:S(2)}, u32[]{:S(2)}) collective-permute-start(bf16[512,1024]{1,0:T(8,128)(2,1)S(1)} %multiply_convert_fusion.refs_0_), channel_id=1, source_target_pairs={{8,16},{16,8},{9,17},{17,9},{10,18},{18,10},{11,19},{19,11},{12,20... | collective-permute-start | bytes 3145736 | tf_op jit(solution)/shard_map/ppermute | solution.py:673
  132.7 26.2 %collective-permute-start.8 = (bf16[512,1024]{1,0:T(8,128)(2,1)S(1)}, bf16[512,1024]{1,0:T(8,128)(2,1)}, u32[]{:S(2)}, u32[]{:S(2)}) collective-permute-start(bf16[512,1024]{1,0:T(8,128)(2,1)S(1)} %multiply_convert_fusion.refs_0_), channel_id=1, source_target_pairs={{0,8},{8,0},{16,24},{24,16},{1,9},{9,1},{17,25},{25,17},{2,10},{10... | collective-permute-start | bytes 3145736 | tf_op jit(solution)/shard_map/ppermute | solution.py:673
  158.9 23.6 %collective-permute-start.10 = (bf16[512,1024]{1,0:T(8,128)(2,1)}, bf16[512,1024]{1,0:T(8,128)(2,1)}, u32[]{:S(2)}, u32[]{:S(2)}) collective-permute-start(bf16[512,1024]{1,0:T(8,128)(2,1)} %collective-permute-done.8.refs_0_), channel_id=1, source_target_pairs={{8,16},{16,8},{9,17},{17,9},{10,18},{18,10},{11,19},{19,11},{12,20... | collective-permute-start | bytes 3145736 | tf_op jit(solution)/shard_map/ppermute | solution.py:677
  160.6 24.2 %collective-permute-start.11 = (bf16[512,1024]{1,0:T(8,128)(2,1)}, bf16[512,1024]{1,0:T(8,128)(2,1)}, u32[]{:S(2)}, u32[]{:S(2)}) collective-permute-start(bf16[512,1024]{1,0:T(8,128)(2,1)} %collective-permute-done.9.refs_1_), channel_id=1, source_target_pairs={{8,0},{16,24},{9,1},{17,25},{10,2},{18,26},{11,3},{19,27},{12,4},{... | collective-permute-start | bytes 3145736 | tf_op jit(solution)/shard_map/ppermute | solution.py:677
  184.7 23.1 %collective-permute-start.12 = (bf16[512,1024]{1,0:T(8,128)(2,1)}, bf16[512,1024]{1,0:T(8,128)(2,1)S(1)}, u32[]{:S(2)}, u32[]{:S(2)}) collective-permute-start(bf16[512,1024]{1,0:T(8,128)(2,1)} %collective-permute-done.10.refs_1_), channel_id=1, source_target_pairs={{8,0},{16,24},{9,1},{17,25},{10,2},{18,26},{11,3},{19,27},{12,4},{... | collective-permute-start | bytes 3145736 | tf_op jit(solution)/shard_map/ppermute | solution.py:681
  243.5 30.4 %collective-permute-start.13 = (bf16[512,1152]{1,0:T(8,128)(2,1)S(1)}, bf16[512,1152]{1,0:T(8,128)(2,1)S(1)}, u32[]{:S(2)}, u32[]{:S(2)}) collective-permute-start(bf16[512,1152]{1,0:T(8,128)(2,1)S(1)} %get-tuple-element.217), channel_id=1, source_target_pairs={{0,8},{24,16},{1,9},{25,17},{2,10},{26,18},{3,11},{27,19},{4,12},{... | collective-permute-start | bytes 3538952 | tf_op jit(solution)/shard_map/ppermute | solution.py:689
  275.0 251.0 %reduce-scatter.5.cloned.1.call-start = ((), (), s32[]{:S(2)}) async-start(), calls=%async_computation.3 | async-start | bytes 1769472 | tf_op jit(solution)/shard_map/reduce_scatter | solution.py:860
  275.1 22.8 %collective-permute-start.16 = (bf16[512,1152]{1,0:T(8,128)(2,1)}, bf16[512,1152]{1,0:T(8,128)(2,1)S(1)}, u32[]{:S(2)}, u32[]{:S(2)}) collective-permute-start(bf16[512,1152]{1,0:T(8,128)(2,1)} %copy-done.10), channel_id=1, source_target_pairs={{0,8},{24,16},{1,9},{25,17},{2,10},{26,18},{3,11},{27,19},{4,12},{... | collective-permute-start | bytes 3538952 | tf_op jit(solution)/shard_map/ppermute | solution.py:689
  278.5 20.8 %collective-permute-start.14 = (bf16[512,1152]{1,0:T(8,128)(2,1)S(1)}, bf16[512,1152]{1,0:T(8,128)(2,1)S(1)}, u32[]{:S(2)}, u32[]{:S(2)}) collective-permute-start(bf16[512,1152]{1,0:T(8,128)(2,1)S(1)} %add_convert_fusion.4), channel_id=1, source_target_pairs={{8,16},{16,8},{9,17},{17,9},{10,18},{18,10},{11,19},{19,11},{12,20... | collective-permute-start | bytes 3538952 | tf_op jit(solution)/shard_map/ppermute | solution.py:697
  298.2 20.5 %collective-permute-start.17 = (bf16[512,1152]{1,0:T(8,128)(2,1)S(1)}, bf16[512,1152]{1,0:T(8,128)(2,1)S(1)}, u32[]{:S(2)}, u32[]{:S(2)}) collective-permute-start(bf16[512,1152]{1,0:T(8,128)(2,1)S(1)} %add_convert_fusion.2), channel_id=1, source_target_pairs={{8,16},{16,8},{9,17},{17,9},{10,18},{18,10},{11,19},{19,11},{12,20... | collective-permute-start | bytes 3538952 | tf_op jit(solution)/shard_map/ppermute | solution.py:697
  299.5 24.9 %collective-permute-start.15 = (bf16[512,1152]{1,0:T(8,128)(2,1)S(1)}, bf16[512,1152]{1,0:T(8,128)(2,1)S(1)}, u32[]{:S(2)}, u32[]{:S(2)}) collective-permute-start(bf16[512,1152]{1,0:T(8,128)(2,1)S(1)} %add_convert_fusion.3), channel_id=1, source_target_pairs={{0,8},{8,0},{16,24},{24,16},{1,9},{9,1},{17,25},{25,17},{2,10},{10... | collective-permute-start | bytes 3538952 | tf_op jit(solution)/shard_map/ppermute | solution.py:701
  328.0 8.9 %collective-permute-start.19 = (bf16[512,1024]{1,0:T(8,128)(2,1)S(1)}, bf16[512,1024]{1,0:T(8,128)(2,1)S(1)}, u32[]{:S(2)}, u32[]{:S(2)}) collective-permute-start(bf16[512,1024]{1,0:T(8,128)(2,1)S(1)} %subtract_convert_fusion.refs_0_), channel_id=1, source_target_pairs={{0,1},{1,0},{2,3},{3,2},{4,5},{5,4},{6,7},{7,6},{8,9},{9,8},{10,11... | collective-permute-start | bytes 3145736 | tf_op jit(solution)/shard_map/ppermute | solution.py:643
  328.1 29.2 %collective-permute-start.21 = (bf16[512,1024]{1,0:T(8,128)(2,1)S(1)}, bf16[512,1024]{1,0:T(8,128)(2,1)S(1)}, u32[]{:S(2)}, u32[]{:S(2)}) collective-permute-start(bf16[512,1024]{1,0:T(8,128)(2,1)S(1)} %get-tuple-element.238), channel_id=1, source_target_pairs={{0,8},{24,16},{1,9},{25,17},{2,10},{26,18},{3,11},{27,19},{4,12},{... | collective-permute-start | bytes 3145736 | tf_op jit(solution)/shard_map/ppermute | solution.py:689
  333.9 45.5 %collective-permute-start.20 = (bf16[512,1024]{1,0:T(8,128)(2,1)S(1)}, bf16[512,1024]{1,0:T(8,128)(2,1)S(1)}, u32[]{:S(2)}, u32[]{:S(2)}) collective-permute-start(bf16[512,1024]{1,0:T(8,128)(2,1)S(1)} %get-tuple-element.242), channel_id=1, source_target_pairs={{0,8},{24,16},{1,9},{25,17},{2,10},{26,18},{3,11},{27,19},{4,12},{... | collective-permute-start | bytes 3145736 | tf_op jit(solution)/shard_map/ppermute | solution.py:689
  335.3 48.4 %collective-permute-start.18 = (bf16[512,1024]{1,0:T(8,128)(2,1)S(1)}, bf16[512,1024]{1,0:T(8,128)(2,1)}, u32[]{:S(2)}, u32[]{:S(2)}) collective-permute-start(bf16[512,1024]{1,0:T(8,128)(2,1)S(1)} %subtract_convert_fusion.refs_0_), channel_id=1, source_target_pairs={{0,2},{2,0},{1,3},{3,1},{4,6},{6,4},{5,7},{7,5},{8,10},{10,8},{9,1... | collective-permute-start | bytes 3145736 | tf_op jit(solution)/shard_map/ppermute | solution.py:643
  385.5 58.1 %collective-permute-start.23 = (bf16[512,1024]{1,0:T(8,128)(2,1)}, bf16[512,1024]{1,0:T(8,128)(2,1)}, u32[]{:S(2)}, u32[]{:S(2)}) collective-permute-start(bf16[512,1024]{1,0:T(8,128)(2,1)} %get-tuple-element.259), channel_id=1, source_target_pairs={{8,16},{16,8},{9,17},{17,9},{10,18},{18,10},{11,19},{19,11},{12,20... | collective-permute-start | bytes 3145736 | tf_op jit(solution)/shard_map/ppermute | solution.py:848
  387.3 56.3 %collective-permute-start.24 = (bf16[512,1024]{1,0:T(8,128)(2,1)}, bf16[512,1024]{1,0:T(8,128)(2,1)}, u32[]{:S(2)}, u32[]{:S(2)}) collective-permute-start(bf16[512,1024]{1,0:T(8,128)(2,1)} %get-tuple-element.260), channel_id=1, source_target_pairs={{8,16},{16,8},{9,17},{17,9},{10,18},{18,10},{11,19},{19,11},{12,20... | collective-permute-start | bytes 3145736 | tf_op jit(solution)/shard_map/ppermute | solution.py:848
  456.7 115.5 %all-gather.4.cloned.1.call-start = ((), (), s32[]{:S(2)}) async-start(), calls=%async_computation.4 | async-start | bytes 1769472 | tf_op jit(solution)/shard_map/all_gather | solution.py:874
  464.2 61.9 %collective-permute-start.26 = (bf16[2,512,1024]{2,1,0:T(8,128)(2,1)S(1)}, bf16[2,512,1024]{2,1,0:T(8,128)(2,1)}, u32[]{:S(2)}, u32[]{:S(2)}) collective-permute-start(bf16[2,512,1024]{2,1,0:T(8,128)(2,1)S(1)} %add_convert_fusion.1), channel_id=1, source_target_pairs={{0,2},{2,0},{1,3},{3,1},{4,6},{6,4},{5,7},{7,5},{8,10},{10,8},{9,1... | collective-permute-start | bytes 6291464 | tf_op jit(solution)/shard_map/ppermute | solution.py:643
  467.1 35.5 %collective-permute-start.27 = (bf16[512,1024]{1,0:T(8,128)(2,1)S(1)}, bf16[512,1024]{1,0:T(8,128)(2,1)S(1)}, u32[]{:S(2)}, u32[]{:S(2)}) collective-permute-start(bf16[512,1024]{1,0:T(8,128)(2,1)S(1)} %add_convert_fusion.6), channel_id=1, source_target_pairs={{0,8},{8,0},{16,24},{24,16},{1,9},{9,1},{17,25},{25,17},{2,10},{10... | collective-permute-start | bytes 3145736 | tf_op jit(solution)/shard_map/ppermute | solution.py:701
  528.8 30.3 %collective-permute-start.28 = (bf16[2,512,1024]{2,1,0:T(8,128)(2,1)S(1)}, bf16[2,512,1024]{2,1,0:T(8,128)(2,1)S(1)}, u32[]{:S(2)}, u32[]{:S(2)}) collective-permute-start(bf16[2,512,1024]{2,1,0:T(8,128)(2,1)S(1)} %add_convert_fusion), channel_id=1, source_target_pairs={{0,1},{1,0},{2,3},{3,2},{4,5},{5,4},{6,7},{7,6},{8,9},{9,8},{10,11... | collective-permute-start | bytes 6291464 | tf_op jit(solution)/shard_map/ppermute | solution.py:643
  542.3 5.6 collective-permute-start.32
  548.0 11.2 %collective-permute-start.33 = (bf16[40,1024]{1,0:T(8,128)(2,1)S(1)}, bf16[40,1024]{1,0:T(8,128)(2,1)S(1)}, u32[]{:S(2)}, u32[]{:S(2)}) collective-permute-start(bf16[40,1024]{1,0:T(8,128)(2,1)S(1)} %add_convert_fusion.10), channel_id=1, source_target_pairs={{0,16},{8,24},{16,0},{24,8},{1,17},{9,25},{17,1},{25,9},{2,18},{10... | collective-permute-start | bytes 245768 | tf_op jit(solution)/shard_map/ppermute | solution.py:643
  (68 other events, 554.3 us)
Sparse Core Ops, SparseCore 0:
  11.2 149.3 all-gather.5
  275.1 178.9 reduce-scatter.2
  458.1 67.9 reduce-scatter.4
  528.3 43.8 all-gather.3

commit v6 on v5

--- a/solution.py
+++ b/solution.py
@@ -309,7 +309,7 @@
     R, D = rows[0].shape
     E = shift.shape[0] - 1
     W = router.shape[1]
-    per = 2
+    per = 4
     operands = [*rows, *sides, router]
     whole = lambda a: pl.BlockSpec(a.shape, lambda e: (0, 0))
     some = lambda w: pl.BlockSpec((per, cap, w), lambda e: (e, 0, 0))
@@ -339,28 +339,25 @@
     gs = jnp.concatenate([r[0] for r in gs_refs], 0)
     dout = (dy.astype(f32) * gs[:, :1]).astype(bf16)
     F = w_ref.shape[-1]
-    eout = jnp.zeros((M, D), f32)
-    drows = jnp.zeros((M, D), f32)
-    for pair in range(0, blocks, 2):
-        acts = []
-        wd2 = jnp.concatenate([w_ref[0, pair, 2, 0], w_ref[0, pair + 1, 2, 0]], 1)
-        dact2 = jnp.dot(dout, wd2, preferred_element_type=f32)
-        for b in (pair, pair + 1):
-            w = jnp.concatenate([w_ref[0, b, 0, 0], w_ref[0, b, 1, 0]], 1)
-            gu = jnp.dot(rows, w, preferred_element_type=f32)
-            g, u = gu[:, :F], gu[:, F:]
-            sg = 1.0 / (1.0 + jnp.exp(-g))
-            gsg = g * sg
-            acts.append((gsg * u).astype(bf16))
-            dact = dact2[:, (b - pair) * F : (b - pair + 1) * F]
-            dg = dact * u * (sg + gsg * (1.0 - sg))
-            du = dact * gsg
-            dgu = jnp.concatenate([dg, du], 1).astype(bf16)
-            dgu_ref[0, :, b * 2 * F : (b + 1) * 2 * F] = dgu
-            drows = drows + lax.dot_general(dgu, w, NT, preferred_element_type=f32)
-        act = jnp.concatenate(acts, 1)
-        act_ref[0, :, pair * F : (pair + 2) * F] = act
-        eout = eout + lax.dot_general(act, wd2, NT, preferred_element_type=f32)
+    w = jnp.concatenate([w_ref[0, b, part, 0] for b in range(blocks) for part in (0, 1)], 1)
+    wd = jnp.concatenate([w_ref[0, b, 2, 0] for b in range(blocks)], 1)
+    gu = jnp.dot(rows, w, preferred_element_type=f32)
+    dacts = jnp.dot(dout, wd, preferred_element_type=f32)
+    acts, dgus = [], []
+    for b in range(blocks):
+        g, u = gu[:, 2 * b * F : (2 * b + 1) * F], gu[:, (2 * b + 1) * F : (2 * b + 2) * F]
+        dact = dacts[:, b * F : (b + 1) * F]
+        sg = 1.0 / (1.0 + jnp.exp(-g))
+        gsg = g * sg
+        acts.append((gsg * u).astype(bf16))
+        dgus.append((dact * u * (sg + gsg * (1.0 - sg))).astype(bf16))
+        dgus.append((dact * gsg).astype(bf16))
+    act = jnp.concatenate(acts, 1)
+    dgu = jnp.concatenate(dgus, 1)
+    act_ref[0] = act
+    dgu_ref[0] = dgu
+    drows = lax.dot_general(dgu, w, NT, preferred_element_type=f32)
+    eout = lax.dot_general(act, wd, NT, preferred_element_type=f32)
     eout = eout.astype(bf16)
     eout_ref[0] = eout
     drows_ref[0] = drows.astype(bf16)
@@ -636,6 +633,34 @@
         cost_estimate=busy(3),
         name="out_pair",
     )(rank, attended, attended, w_out)
+
+
+def parted_kernel(cuts, low_ref, left_ref, right_ref, *outs):
+    at = 0
+    for out, cut in zip(outs[:-1], cuts):
+        out[...] = low_ref[:, at : at + cut].astype(f32)
+        at += cut
+    half = left_ref.shape[1]
+    outs[-1][:, :half] = left_ref[...].astype(f32)
+    outs[-1][:, half:] = right_ref[...].astype(f32)
+
+
+def parted(low, cuts):
+    total, half = low.shape
+    rows = 2 * half
+    part = (total - rows) // 2
+    n = 4
+    block = lambda r, w, at: pl.BlockSpec((r // n, w), lambda i: (at * n // r + i, 0))
+    return pl.pallas_call(
+        functools.partial(parted_kernel, cuts),
+        grid=(n,),
+        in_specs=[block(rows, half, 0), block(part, half, rows), block(part, half, rows + part)],
+        out_specs=[block(rows, cut, 0) for cut in cuts] + [block(part, 2 * half, 0)],
+        out_shape=[pltpu.HBM((rows, cut), f32) for cut in cuts] + [pltpu.HBM((part, 2 * half), f32)],
+        compiler_params=pltpu.CompilerParams(vmem_limit_bytes=32 << 20),
+        cost_estimate=busy(3),
+        name="parted",
+    )(*from_hbm(low, low, low))
 
 
 def swap(x, axis, bit=1):
@@ -851,7 +876,7 @@
     )
     heads_in = jnp.concatenate([w_query, w_key, w_value], 1)
     heads_grad = jnp.einsum("id,ih->dh", normed_one, heads_back, preferred_element_type=f32)
-    low = jnp.concatenate([heads_grad.astype(bf16), out_low.reshape(-1, heads_grad.shape[1])], 0)
+    low = jnp.concatenate([heads_grad.astype(bf16), out_low[:, : width // 2], out_low[:, width // 2 :]], 0)
     gain_one_part = jnp.sum(heads_grad * heads_in.astype(f32), 1) / gain_attn.astype(f32)
     small = jnp.concatenate([small[: EXPERTS + 1], gain_one_part[None], small[EXPERTS + 2 :]], 0)
     heads_back, low, part_sum, out_far, out_across = hold(heads_back, low, part_sum, out_far, out_across)
@@ -882,21 +907,16 @@
     input_grad = finish(
         1 - core, other_sum.reshape(-1, width), tokens, hidden_all, gain_row, own_rows, (input_grad,)
     )
-    low_all, input_grad, block_output, rest = hold(low_all, input_grad, block_output, rest)
-    low_all = low_all.astype(f32)
-    heads_total = low_all[:width]
-    out_total = low_all[width:].reshape(out_grad.shape)
-    cut = w_query.shape[1]
+    smalls = rest[EXPERTS + 1], rest[EXPERTS], rest[:EXPERTS].T
+    low_all, input_grad, block_output, *smalls = hold(low_all, input_grad, block_output, *smalls)
+    heads = parted(low_all, (w_query.shape[1], w_key.shape[1], w_value.shape[1]))
     return (
         block_output,
         input_grad,
-        rest[EXPERTS + 1],
-        heads_total[:, :cut],
-        heads_total[:, cut : cut + w_key.shape[1]],
-        heads_total[:, cut + w_key.shape[1] :],
-        out_total,
-        rest[EXPERTS],
-        rest[:EXPERTS].T,
+        smalls[0],
+        *heads,
+        smalls[1],
+        smalls[2],
         *summed_grads,
     )
 

time: 595 us -> 592 us (level)
    unnamed x128 -> x134, local copies, waits for them, and re-layouts: 17.3 us -> 17.1 us
  transfers between devices with their start and end apart: 38 -> 38, of which waited for: 20 -> 19; matrix products, arithmetic and copies ran while one was open for 6% -> 6% of each run, Pallas kernels for 33% -> 34%
where the time goes in v6:
time: 592 us; the launch traced here: 581 us
  Pallas kernels  233 us (39%)
  waiting for transfers between devices  221 us (37%)
  starting transfers between devices  55.7 us (9%)
  other arithmetic  23.6 us (4%)
  local copies, waits for them, and re-layouts  19.8 us (3%)
  between operations  16 us (3%)
  matrix products  12.9 us (2%)
    pallas_call x3, Pallas kernels, ffn(): pl.pallas_call(functools.partial(ffn_kernel, n, blocks), grid=(len(groups...  45.8 us
    pallas_call x1, Pallas kernels, attend_back(): pl.pallas_call(functools.partial(attend_back_kernel, bq, bk), grid_spec=p...  44.2 us
    ppermute x2, waiting for transfers between devices, line_in(): return lax.ppermute(add_low(part, across_far), 'z', NEAR)  39.7 us
    ppermute x14, waiting for transfers between devices, swap(): return lax.ppermute(x, axis, [(i, i ^ bit) for i in range(count)])  38.3 us
    pallas_call x2, Pallas kernels, attend(): pl.pallas_call(functools.partial(attend_kernel, bq, bk, kv), grid_spec=pl...  31.8 us
    ppermute x2, waiting for transfers between devices, line_out(): lax.ppermute(parts[2], 'z', FROM_ENDS)  30.8 us
    pallas_call x2, Pallas kernels, wgrad(): pl.pallas_call(functools.partial(wgrad_kernel, n, len(acts), blocks), gri...  27 us
    ppermute x4, waiting for transfers between devices, line_second(): return (lax.ppermute(near, 'z', MIDDLE), lax.ppermute(across, 'z', TO_ENDS))  27 us
  transfers between devices with their start and end apart: 38, of which 19 were waited for; matrix products, arithmetic and copies ran while one was open for 6% of the time, Pallas kernels for 34%

profile of v6, /device:TPU:0, one launch (start us, length us, event | category | flops | bytes accessed | tf_op | source)
XLA Modules:
  0.0 581.3 jit_solution(7537960494944826829)
XLA Ops:
  15.4 4.9 collective-permute-start
  22.5 11.2 %project.1 = (bf16[2048,1024]{1,0:T(8,128)(2,1)}, bf16[4,2048,128]{2,1,0:T(8,128)(2,1)}, bf16[2048,128]{1,0:T(8,128)(2,1)}, bf16[2048,256]{1,0:T(8,128)(2,1)}) custom-call(bf16[2048,1024]{1,0:T(8,128)(2,1)} %x_ref.5, bf16[1,1024]{1,0:T(2,128)(2,1)S(1)} %broadcast_in_dim.36.gain_ref, bf16[1024,256]{1,0:T(8,128)(2,1)S(1)} %copy-done.7, ...), custom_call_target="tpu_custom_call" | custom-call | flops 900000000 | tf_op jit(solution)/shard_map/project/pallas_call | solution.py:93
  33.7 15.9 %attend.2 = (bf16[2048,256]{1,0:T(8,128)(2,1)}, f32[2,8,4096]{2,1,0:T(8,128)}) custom-call(s32[1]{0:T(128)S(6)} %copy.68.prefix_ref, bf16[4,2048,128]{2,1,0:T(8,128)(2,1)} %get-tuple-element.155.q_ref, bf16[2048,128]{1,0:T(8,128)(2,1)} %get-tuple-element.156.k_ref, bf16[2048,256]{1,0:T(8,128)(2,1)} %get-tuple-element.157.v_ref), custom_call_target="tpu_custom_call" | custom-call | flops 1400000000 | tf_op jit(solution)/shard_map/attend/pallas_call | solution.py:159
  51.5 15.9 %attend.3 = (bf16[2048,256]{1,0:T(8,128)(2,1)}, f32[2,8,4096]{2,1,0:T(8,128)}) custom-call(s32[1]{0:T(128)S(6)} %copy.68.prefix_ref, bf16[4,2048,128]{2,1,0:T(8,128)(2,1)} %get-tuple-element.155.q_ref, bf16[2048,128]{1,0:T(8,128)(2,1)} %get-tuple-element.156.k_ref, ...), custom_call_target="tpu_custom_call", output_to_operand_aliasing={{0}: (4, {}), {1}: (5, {})} | custom-call | flops 1400000000 | tf_op jit(solution)/shard_map/attend/pallas_call | solution.py:159
  79.2 23.9 %collective-permute-done.6.refs_2_ = bf16[512,1152]{1,0:T(8,128)(2,1)} collective-permute-done((bf16[512,1152]{1,0:T(8,128)(2,1)}, bf16[512,1152]{1,0:T(8,128)(2,1)}, u32[]{:S(2)}, u32[]{:S(2)}) %collective-permute-start.6) | collective-permute-done | bytes 1179680 | tf_op jit(solution)/shard_map/ppermute | solution.py:702
  103.1 21.5 %collective-permute-done.5 = bf16[512,1024]{1,0:T(8,128)(2,1)} collective-permute-done((bf16[512,1024]{1,0:T(8,128)(2,1)}, bf16[512,1024]{1,0:T(8,128)(2,1)}, u32[]{:S(2)}, u32[]{:S(2)}) %collective-permute-start.5) | collective-permute-done | bytes 1048608 | tf_op jit(solution)/shard_map/ppermute | solution.py:668
  132.7 5.3 collective-permute-start.8
  140.3 5.0 pick.4
  146.0 13.0 %collective-permute-done.8.refs_0_ = bf16[512,1024]{1,0:T(8,128)(2,1)} collective-permute-done((bf16[512,1024]{1,0:T(8,128)(2,1)S(1)}, bf16[512,1024]{1,0:T(8,128)(2,1)}, u32[]{:S(2)}, u32[]{:S(2)}) %collective-permute-start.8) | collective-permute-done | bytes 1048608 | tf_op jit(solution)/shard_map/ppermute | solution.py:698
  161.9 6.2 %pick.5 = (bf16[8,128,1024]{2,1,0:T(8,128)(2,1)}, bf16[8,128,1024]{2,1,0:T(8,128)(2,1)}, f32[8,128,128]{2,1,0:T(8,128)}, f32[512,128]{1,0:T(8,128)S(1)}, f32[512,128]{1,0:T(8,128)S(1)}) custom-call(s32[9]{0:T(128)S(1)} %pad_add_fusion.shift_ref, bf16[512,1024]{1,0:T(8,128)(2,1)} %collective-permute-done.8.refs_0_, ...), custom_call_target="tpu_custom_call" | custom-call | flops 400000000 | tf_op jit(solution)/shard_map/pick/pallas_call | solution.py:317
  169.6 12.1 %ffn.3 = (bf16[8,256,1024]{2,1,0:T(8,128)(2,1)}, bf16[8,256,1024]{2,1,0:T(8,128)(2,1)}, f32[8,256,128]{2,1,0:T(8,128)}, bf16[8,256,512]{2,1,0:T(8,128)(2,1)}, bf16[8,256,1024]{2,1,0:T(8,128)(2,1)}) custom-call(bf16[8,128,1024]{2,1,0:T(8,128)(2,1)} %get-tuple-element.182.refs_0_, bf16[8,128,1024]{2,1,0:T(8,128)(2,1)} %get-tuple-element.183.refs_1_, ...), custom_call_target="tpu_custom_call" | custom-call | flops 1200000000 | tf_op jit(solution)/shard_map/ffn/pallas_call | solution.py:380
  186.1 6.9 %pick.6 = (bf16[8,128,1024]{2,1,0:T(8,128)(2,1)}, bf16[8,128,1024]{2,1,0:T(8,128)(2,1)}, f32[8,128,128]{2,1,0:T(8,128)}, f32[512,128]{1,0:T(8,128)S(1)}, f32[512,128]{1,0:T(8,128)S(1)}) custom-call(s32[9]{0:T(128)S(1)} %pad_add_fusion.shift_ref, bf16[512,1024]{1,0:T(8,128)(2,1)} %collective-permute-done.11.refs_0_, ...), custom_call_target="tpu_custom_call" | custom-call | flops 400000000 | tf_op jit(solution)/shard_map/pick/pallas_call | solution.py:317
  193.0 12.2 %ffn.4 = (bf16[8,256,1024]{2,1,0:T(8,128)(2,1)}, bf16[8,256,1024]{2,1,0:T(8,128)(2,1)}, f32[8,256,128]{2,1,0:T(8,128)}, bf16[8,256,512]{2,1,0:T(8,128)(2,1)}, bf16[8,256,1024]{2,1,0:T(8,128)(2,1)}) custom-call(bf16[8,128,1024]{2,1,0:T(8,128)(2,1)} %get-tuple-element.182.refs_0_, ...), custom_call_target="tpu_custom_call", output_to_operand_aliasing={{0}: (7, {}), {1}: (8, {}), {2}: (9, {}), {3}: (10, {}), {4... | custom-call | flops 1200000000 | tf_op jit(solution)/shard_map/ffn/pallas_call | solution.py:380
  207.9 6.6 %pick.7 = (bf16[8,128,1024]{2,1,0:T(8,128)(2,1)}, bf16[8,128,1024]{2,1,0:T(8,128)(2,1)}, f32[8,128,128]{2,1,0:T(8,128)}, f32[512,128]{1,0:T(8,128)S(1)}, f32[512,128]{1,0:T(8,128)S(1)}) custom-call(s32[9]{0:T(128)S(1)} %pad_add_fusion.shift_ref, bf16[512,1024]{1,0:T(8,128)(2,1)S(1)} %collective-permute-done.12.refs_0_, ...), custom_call_target="tpu_custom_call" | custom-call | flops 400000000 | tf_op jit(solution)/shard_map/pick/pallas_call | solution.py:317
  214.5 21.6 %ffn.5 = (bf16[8,256,1024]{2,1,0:T(8,128)(2,1)}, bf16[8,256,1024]{2,1,0:T(8,128)(2,1)}, f32[8,256,128]{2,1,0:T(8,128)}, bf16[8,256,512]{2,1,0:T(8,128)(2,1)}, bf16[8,256,1024]{2,1,0:T(8,128)(2,1)}) custom-call(bf16[8,128,1024]{2,1,0:T(8,128)(2,1)} %get-tuple-element.214.refs_0_.refs_2_, bf16[8,128,1024]{2,1,0:T(8,128)(2,1)} %get-tuple-element.215.refs_1_.refs_3_, ...), custom_call_target="tpu_custom_call" | custom-call | flops 2400000000 | tf_op jit(solution)/shard_map/ffn/pallas_call | solution.py:380
  244.6 13.5 %wgrad.2.refs_16_ = bf16[2,4,3,4,1024,128]{5,4,3,2,1,0:T(8,128)(2,1)} custom-call(bf16[8,128,1024]{2,1,0:T(8,128)(2,1)} %get-tuple-element.182.refs_0_, bf16[8,128,1024]{2,1,0:T(8,128)(2,1)} %get-tuple-element.183.refs_1_, bf16[8,128,1024]{2,1,0:T(8,128)(2,1)} %get-tuple-element.214.refs_0_.refs_2_, ...), custom_call_target="tpu_custom_call" | custom-call | flops 1300000000 | tf_op jit(solution)/shard_map/wgrad/pallas_call | solution.py:421
  258.2 13.5 %wgrad.3 = bf16[2,4,3,4,1024,128]{5,4,3,2,1,0:T(8,128)(2,1)} custom-call(bf16[8,128,1024]{2,1,0:T(8,128)(2,1)} %get-tuple-element.182.refs_0_, bf16[8,128,1024]{2,1,0:T(8,128)(2,1)} %get-tuple-element.183.refs_1_, bf16[8,128,1024]{2,1,0:T(8,128)(2,1)} %get-tuple-element.214.refs_0_.refs_2_, ...), custom_call_target="tpu_custom_call", output_to_operand_aliasing={{}: (16, {})} | custom-call | flops 1300000000 | tf_op jit(solution)/shard_map/wgrad/pallas_call | solution.py:421
  277.0 5.6 merge_back.2
  282.6 13.0 %collective-permute-done.16 = bf16[512,1152]{1,0:T(8,128)(2,1)S(1)} collective-permute-done((bf16[512,1152]{1,0:T(8,128)(2,1)}, bf16[512,1152]{1,0:T(8,128)(2,1)S(1)}, u32[]{:S(2)}, u32[]{:S(2)}) %collective-permute-start.16) | collective-permute-done | bytes 1179680 | tf_op jit(solution)/shard_map/ppermute | solution.py:714
  297.3 7.1 %collective-permute-start.15 = (bf16[512,1152]{1,0:T(8,128)(2,1)S(1)}, bf16[512,1152]{1,0:T(8,128)(2,1)S(1)}, u32[]{:S(2)}, u32[]{:S(2)}) collective-permute-start(bf16[512,1152]{1,0:T(8,128)(2,1)S(1)} %add_convert_fusion.3), channel_id=1, source_target_pairs={{0,8},{8,0},{16,24},{24,16},{1,9},{9,1},{17,25},{25,17},{2,10},{10... | collective-permute-start | bytes 3538952 | tf_op jit(solution)/shard_map/ppermute | solution.py:726
  304.5 5.1 merge_out.2
  316.4 5.8 collective-permute-done.15
  325.9 5.8 collective-permute-start.21
  337.3 17.8 %collective-permute-done.21 = bf16[512,1024]{1,0:T(8,128)(2,1)S(1)} collective-permute-done((bf16[512,1024]{1,0:T(8,128)(2,1)S(1)}, bf16[512,1024]{1,0:T(8,128)(2,1)S(1)}, u32[]{:S(2)}, u32[]{:S(2)}) %collective-permute-start.21) | collective-permute-done | bytes 1048608 | tf_op jit(solution)/shard_map/ppermute | solution.py:714
  355.1 22.1 %collective-permute-done.20 = bf16[512,1024]{1,0:T(8,128)(2,1)S(1)} collective-permute-done((bf16[512,1024]{1,0:T(8,128)(2,1)S(1)}, bf16[512,1024]{1,0:T(8,128)(2,1)S(1)}, u32[]{:S(2)}, u32[]{:S(2)}) %collective-permute-start.20) | collective-permute-done | bytes 1048608 | tf_op jit(solution)/shard_map/ppermute | solution.py:714
  391.7 44.2 %attend_back.1 = bf16[2048,512]{1,0:T(8,128)(2,1)} custom-call(s32[1]{0:T(128)S(6)} %copy.68.prefix_ref, bf16[4,2048,128]{2,1,0:T(8,128)(2,1)} %get-tuple-element.155.q_ref, bf16[2048,128]{1,0:T(8,128)(2,1)S(1)} %copy-done.41, bf16[2048,256]{1,0:T(8,128)(2,1)S(1)} %copy-done.40, bf16[2048,256]{1,0:T(8,128)(2,1)S(1)} %copy-done.1, ...), custom_call_target="tpu_custom_call" | custom-call | flops 4600000000 | tf_op jit(solution)/shard_map/attend_back/pallas_call | solution.py:250
  441.2 10.6 %reduce-scatter.3.cloned.1.call-done = bf16[1,3,4,1024,128]{4,3,2,1,0:T(8,128)(2,1)} async-done(((bf16[8,3,4,1024,128]{4,3,2,1,0:T(8,128)(2,1)}), bf16[1,3,4,1024,128]{4,3,2,1,0:T(8,128)(2,1)}) %reduce-scatter.3.cloned.1.call-update) | async-done | bytes 3145744 | tf_op jit(solution)/shard_map/reduce_scatter | solution.py:842
  467.1 33.9 %collective-permute-done.27 = bf16[512,1024]{1,0:T(8,128)(2,1)S(1)} collective-permute-done((bf16[512,1024]{1,0:T(8,128)(2,1)S(1)}, bf16[512,1024]{1,0:T(8,128)(2,1)S(1)}, u32[]{:S(2)}, u32[]{:S(2)}) %collective-permute-start.27) | collective-permute-done | bytes 1048608 | tf_op jit(solution)/shard_map/ppermute | solution.py:726
  501.0 23.1 %reduce-scatter.5.cloned.1.call-done = bf16[192,512]{1,0:T(8,128)(2,1)} async-done(((bf16[1536,512]{1,0:T(8,128)(2,1)}), bf16[192,512]{1,0:T(8,128)(2,1)}) %reduce-scatter.5.cloned.1.call-update) | async-done | bytes 196624 | tf_op jit(solution)/shard_map/reduce_scatter | solution.py:885
  547.7 5.6 finish.2.refs_0_
  554.6 5.6 finish.3
  560.2 10.3 %all-gather.4.cloned.1.call-done.low_ref.left_ref.right_ref = bf16[1536,512]{1,0:T(8,128)(2,1)} async-done(((bf16[192,512]{1,0:T(8,128)(2,1)}), bf16[1536,512]{1,0:T(8,128)(2,1)}) %all-gather.4.cloned.1.call-update) | async-done | bytes 1572880 | tf_op jit(solution)/shard_map/all_gather | solution.py:899
  (256 shorter events, 140.8 us)
Async XLA Ops:
  7.2 162.4 %all-gather.6.cloned.1.call-start = ((), (), s32[]{:S(2)}) async-start(), calls=%async_computation.5 | async-start | bytes 28311552 | tf_op jit(solution)/shard_map/all_gather | solution.py:779
  11.2 440.6 %reduce-scatter.3.cloned.1.call-start = ((), (), s32[]{:S(2)}) async-start(), calls=%async_computation.2 | async-start | bytes 28311552 | tf_op jit(solution)/shard_map/reduce_scatter | solution.py:842
  13.7 35.9 %collective-permute-start.1 = (bf16[512,1152]{1,0:T(8,128)(2,1)S(1)}, bf16[512,1152]{1,0:T(8,128)(2,1)}, u32[]{:S(2)}, u32[]{:S(2)}) collective-permute-start(bf16[512,1152]{1,0:T(8,128)(2,1)S(1)} %fusion.1.refs_1_), channel_id=1, source_target_pairs={{8,16},{16,8},{9,17},{17,9},{10,18},{18,10},{11,19},{19,11},{12,20... | collective-permute-start | bytes 3538952 | tf_op jit(solution)/shard_map/ppermute | solution.py:698
  15.4 34.2 %collective-permute-start = (bf16[512,1152]{1,0:T(8,128)(2,1)S(1)}, bf16[512,1152]{1,0:T(8,128)(2,1)}, u32[]{:S(2)}, u32[]{:S(2)}) collective-permute-start(bf16[512,1152]{1,0:T(8,128)(2,1)S(1)} %fusion.1.refs_1_), channel_id=1, source_target_pairs={{0,8},{8,0},{16,24},{24,16},{1,9},{9,1},{17,25},{25,17},{2,10},{10... | collective-permute-start | bytes 3538952 | tf_op jit(solution)/shard_map/ppermute | solution.py:698
  49.7 23.7 %collective-permute-start.3 = (bf16[512,1152]{1,0:T(8,128)(2,1)}, bf16[512,1152]{1,0:T(8,128)(2,1)}, u32[]{:S(2)}, u32[]{:S(2)}) collective-permute-start(bf16[512,1152]{1,0:T(8,128)(2,1)} %collective-permute-done.refs_1_), channel_id=1, source_target_pairs={{8,16},{16,8},{9,17},{17,9},{10,18},{18,10},{11,19},{19,11},{12,20... | collective-permute-start | bytes 3538952 | tf_op jit(solution)/shard_map/ppermute | solution.py:702
  71.6 6.0 %collective-permute-start.2 = (bf16[512,1024]{1,0:T(8,128)(2,1)}, bf16[512,1024]{1,0:T(8,128)(2,1)}, u32[]{:S(2)}, u32[]{:S(2)}) collective-permute-start(bf16[512,1024]{1,0:T(8,128)(2,1)} %get-tuple-element.164), channel_id=1, source_target_pairs={{0,1},{1,0},{2,3},{3,2},{4,5},{5,4},{6,7},{7,6},{8,9},{9,8},{10,11... | collective-permute-start | bytes 3145736 | tf_op jit(solution)/shard_map/ppermute | solution.py:668
  72.0 31.0 %collective-permute-start.6 = (bf16[512,1152]{1,0:T(8,128)(2,1)}, bf16[512,1152]{1,0:T(8,128)(2,1)}, u32[]{:S(2)}, u32[]{:S(2)}) collective-permute-start(bf16[512,1152]{1,0:T(8,128)(2,1)} %collective-permute-done.1.refs_3_), channel_id=1, source_target_pairs={{8,0},{16,24},{9,1},{17,25},{10,2},{18,26},{11,3},{19,27},{12,4},{... | collective-permute-start | bytes 3538952 | tf_op jit(solution)/shard_map/ppermute | solution.py:702
  73.4 54.1 %collective-permute-start.7 = (bf16[512,1152]{1,0:T(8,128)(2,1)}, bf16[512,1152]{1,0:T(8,128)(2,1)}, u32[]{:S(2)}, u32[]{:S(2)}) collective-permute-start(bf16[512,1152]{1,0:T(8,128)(2,1)} %collective-permute-done.3.refs_3_), channel_id=1, source_target_pairs={{8,0},{16,24},{9,1},{17,25},{10,2},{18,26},{11,3},{19,27},{12,4},{... | collective-permute-start | bytes 3538952 | tf_op jit(solution)/shard_map/ppermute | solution.py:706
  76.0 48.5 %collective-permute-start.5 = (bf16[512,1024]{1,0:T(8,128)(2,1)}, bf16[512,1024]{1,0:T(8,128)(2,1)}, u32[]{:S(2)}, u32[]{:S(2)}) collective-permute-start(bf16[512,1024]{1,0:T(8,128)(2,1)} %add_convert_fusion.9), channel_id=1, source_target_pairs={{0,2},{2,0},{1,3},{3,1},{4,6},{6,4},{5,7},{7,5},{8,10},{10,8},{9,1... | collective-permute-start | bytes 3145736 | tf_op jit(solution)/shard_map/ppermute | solution.py:668
  130.8 15.2 %collective-permute-start.9 = (bf16[512,1024]{1,0:T(8,128)(2,1)S(1)}, bf16[512,1024]{1,0:T(8,128)(2,1)}, u32[]{:S(2)}, u32[]{:S(2)}) collective-permute-start(bf16[512,1024]{1,0:T(8,128)(2,1)S(1)} %multiply_convert_fusion.refs_0_), channel_id=1, source_target_pairs={{8,16},{16,8},{9,17},{17,9},{10,18},{18,10},{11,19},{19,11},{12,20... | collective-permute-start | bytes 3145736 | tf_op jit(solution)/shard_map/ppermute | solution.py:698
  132.7 26.3 %collective-permute-start.8 = (bf16[512,1024]{1,0:T(8,128)(2,1)S(1)}, bf16[512,1024]{1,0:T(8,128)(2,1)}, u32[]{:S(2)}, u32[]{:S(2)}) collective-permute-start(bf16[512,1024]{1,0:T(8,128)(2,1)S(1)} %multiply_convert_fusion.refs_0_), channel_id=1, source_target_pairs={{0,8},{8,0},{16,24},{24,16},{1,9},{9,1},{17,25},{25,17},{2,10},{10... | collective-permute-start | bytes 3145736 | tf_op jit(solution)/shard_map/ppermute | solution.py:698
  159.0 22.7 %collective-permute-start.10 = (bf16[512,1024]{1,0:T(8,128)(2,1)}, bf16[512,1024]{1,0:T(8,128)(2,1)}, u32[]{:S(2)}, u32[]{:S(2)}) collective-permute-start(bf16[512,1024]{1,0:T(8,128)(2,1)} %collective-permute-done.8.refs_0_), channel_id=1, source_target_pairs={{8,16},{16,8},{9,17},{17,9},{10,18},{18,10},{11,19},{19,11},{12,20... | collective-permute-start | bytes 3145736 | tf_op jit(solution)/shard_map/ppermute | solution.py:702
  160.6 24.1 %collective-permute-start.11 = (bf16[512,1024]{1,0:T(8,128)(2,1)}, bf16[512,1024]{1,0:T(8,128)(2,1)}, u32[]{:S(2)}, u32[]{:S(2)}) collective-permute-start(bf16[512,1024]{1,0:T(8,128)(2,1)} %collective-permute-done.9.refs_1_), channel_id=1, source_target_pairs={{8,0},{16,24},{9,1},{17,25},{10,2},{18,26},{11,3},{19,27},{12,4},{... | collective-permute-start | bytes 3145736 | tf_op jit(solution)/shard_map/ppermute | solution.py:702
  184.8 23.1 %collective-permute-start.12 = (bf16[512,1024]{1,0:T(8,128)(2,1)}, bf16[512,1024]{1,0:T(8,128)(2,1)S(1)}, u32[]{:S(2)}, u32[]{:S(2)}) collective-permute-start(bf16[512,1024]{1,0:T(8,128)(2,1)} %collective-permute-done.10.refs_1_), channel_id=1, source_target_pairs={{8,0},{16,24},{9,1},{17,25},{10,2},{18,26},{11,3},{19,27},{12,4},{... | collective-permute-start | bytes 3145736 | tf_op jit(solution)/shard_map/ppermute | solution.py:706
  242.2 29.5 %collective-permute-start.13 = (bf16[512,1152]{1,0:T(8,128)(2,1)S(1)}, bf16[512,1152]{1,0:T(8,128)(2,1)S(1)}, u32[]{:S(2)}, u32[]{:S(2)}) collective-permute-start(bf16[512,1152]{1,0:T(8,128)(2,1)S(1)} %get-tuple-element.223), channel_id=1, source_target_pairs={{0,8},{24,16},{1,9},{25,17},{2,10},{26,18},{3,11},{27,19},{4,12},{... | collective-permute-start | bytes 3538952 | tf_op jit(solution)/shard_map/ppermute | solution.py:714
  272.8 251.3 %reduce-scatter.5.cloned.1.call-start = ((), (), s32[]{:S(2)}) async-start(), calls=%async_computation.3 | async-start | bytes 1769472 | tf_op jit(solution)/shard_map/reduce_scatter | solution.py:885
  272.8 22.8 %collective-permute-start.16 = (bf16[512,1152]{1,0:T(8,128)(2,1)}, bf16[512,1152]{1,0:T(8,128)(2,1)S(1)}, u32[]{:S(2)}, u32[]{:S(2)}) collective-permute-start(bf16[512,1152]{1,0:T(8,128)(2,1)} %copy-done.10), channel_id=1, source_target_pairs={{0,8},{24,16},{1,9},{25,17},{2,10},{26,18},{3,11},{27,19},{4,12},{... | collective-permute-start | bytes 3538952 | tf_op jit(solution)/shard_map/ppermute | solution.py:714
  276.3 20.8 %collective-permute-start.14 = (bf16[512,1152]{1,0:T(8,128)(2,1)S(1)}, bf16[512,1152]{1,0:T(8,128)(2,1)S(1)}, u32[]{:S(2)}, u32[]{:S(2)}) collective-permute-start(bf16[512,1152]{1,0:T(8,128)(2,1)S(1)} %add_convert_fusion.4), channel_id=1, source_target_pairs={{8,16},{16,8},{9,17},{17,9},{10,18},{18,10},{11,19},{19,11},{12,20... | collective-permute-start | bytes 3538952 | tf_op jit(solution)/shard_map/ppermute | solution.py:722
  296.0 20.4 %collective-permute-start.17 = (bf16[512,1152]{1,0:T(8,128)(2,1)S(1)}, bf16[512,1152]{1,0:T(8,128)(2,1)S(1)}, u32[]{:S(2)}, u32[]{:S(2)}) collective-permute-start(bf16[512,1152]{1,0:T(8,128)(2,1)S(1)} %add_convert_fusion.2), channel_id=1, source_target_pairs={{8,16},{16,8},{9,17},{17,9},{10,18},{18,10},{11,19},{19,11},{12,20... | collective-permute-start | bytes 3538952 | tf_op jit(solution)/shard_map/ppermute | solution.py:722
  297.3 24.9 %collective-permute-start.15 = (bf16[512,1152]{1,0:T(8,128)(2,1)S(1)}, bf16[512,1152]{1,0:T(8,128)(2,1)S(1)}, u32[]{:S(2)}, u32[]{:S(2)}) collective-permute-start(bf16[512,1152]{1,0:T(8,128)(2,1)S(1)} %add_convert_fusion.3), channel_id=1, source_target_pairs={{0,8},{8,0},{16,24},{24,16},{1,9},{9,1},{17,25},{25,17},{2,10},{10... | collective-permute-start | bytes 3538952 | tf_op jit(solution)/shard_map/ppermute | solution.py:726
  325.8 8.9 %collective-permute-start.19 = (bf16[512,1024]{1,0:T(8,128)(2,1)S(1)}, bf16[512,1024]{1,0:T(8,128)(2,1)S(1)}, u32[]{:S(2)}, u32[]{:S(2)}) collective-permute-start(bf16[512,1024]{1,0:T(8,128)(2,1)S(1)} %subtract_convert_fusion.refs_0_), channel_id=1, source_target_pairs={{0,1},{1,0},{2,3},{3,2},{4,5},{5,4},{6,7},{7,6},{8,9},{9,8},{10,11... | collective-permute-start | bytes 3145736 | tf_op jit(solution)/shard_map/ppermute | solution.py:668
  325.9 29.2 %collective-permute-start.21 = (bf16[512,1024]{1,0:T(8,128)(2,1)S(1)}, bf16[512,1024]{1,0:T(8,128)(2,1)S(1)}, u32[]{:S(2)}, u32[]{:S(2)}) collective-permute-start(bf16[512,1024]{1,0:T(8,128)(2,1)S(1)} %get-tuple-element.244), channel_id=1, source_target_pairs={{0,8},{24,16},{1,9},{25,17},{2,10},{26,18},{3,11},{27,19},{4,12},{... | collective-permute-start | bytes 3145736 | tf_op jit(solution)/shard_map/ppermute | solution.py:714
  331.7 45.5 %collective-permute-start.20 = (bf16[512,1024]{1,0:T(8,128)(2,1)S(1)}, bf16[512,1024]{1,0:T(8,128)(2,1)S(1)}, u32[]{:S(2)}, u32[]{:S(2)}) collective-permute-start(bf16[512,1024]{1,0:T(8,128)(2,1)S(1)} %get-tuple-element.248), channel_id=1, source_target_pairs={{0,8},{24,16},{1,9},{25,17},{2,10},{26,18},{3,11},{27,19},{4,12},{... | collective-permute-start | bytes 3145736 | tf_op jit(solution)/shard_map/ppermute | solution.py:714
  333.1 48.4 %collective-permute-start.18 = (bf16[512,1024]{1,0:T(8,128)(2,1)S(1)}, bf16[512,1024]{1,0:T(8,128)(2,1)}, u32[]{:S(2)}, u32[]{:S(2)}) collective-permute-start(bf16[512,1024]{1,0:T(8,128)(2,1)S(1)} %subtract_convert_fusion.refs_0_), channel_id=1, source_target_pairs={{0,2},{2,0},{1,3},{3,1},{4,6},{6,4},{5,7},{7,5},{8,10},{10,8},{9,1... | collective-permute-start | bytes 3145736 | tf_op jit(solution)/shard_map/ppermute | solution.py:668
  383.3 58.0 %collective-permute-start.23 = (bf16[512,1024]{1,0:T(8,128)(2,1)}, bf16[512,1024]{1,0:T(8,128)(2,1)S(1)}, u32[]{:S(2)}, u32[]{:S(2)}) collective-permute-start(bf16[512,1024]{1,0:T(8,128)(2,1)} %get-tuple-element.265), channel_id=1, source_target_pairs={{8,16},{16,8},{9,17},{17,9},{10,18},{18,10},{11,19},{19,11},{12,20... | collective-permute-start | bytes 3145736 | tf_op jit(solution)/shard_map/ppermute | solution.py:873
  384.1 57.1 %collective-permute-start.24 = (bf16[512,1024]{1,0:T(8,128)(2,1)}, bf16[512,1024]{1,0:T(8,128)(2,1)}, u32[]{:S(2)}, u32[]{:S(2)}) collective-permute-start(bf16[512,1024]{1,0:T(8,128)(2,1)} %get-tuple-element.266), channel_id=1, source_target_pairs={{8,16},{16,8},{9,17},{17,9},{10,18},{18,10},{11,19},{19,11},{12,20... | collective-permute-start | bytes 3145736 | tf_op jit(solution)/shard_map/ppermute | solution.py:873
  455.7 114.7 %all-gather.4.cloned.1.call-start = ((), (), s32[]{:S(2)}) async-start(), calls=%async_computation.4 | async-start | bytes 1769472 | tf_op jit(solution)/shard_map/all_gather | solution.py:899
  463.7 60.4 %collective-permute-start.26 = (bf16[2,512,1024]{2,1,0:T(8,128)(2,1)S(1)}, bf16[2,512,1024]{2,1,0:T(8,128)(2,1)}, u32[]{:S(2)}, u32[]{:S(2)}) collective-permute-start(bf16[2,512,1024]{2,1,0:T(8,128)(2,1)S(1)} %add_convert_fusion.1), channel_id=1, source_target_pairs={{0,2},{2,0},{1,3},{3,1},{4,6},{6,4},{5,7},{7,5},{8,10},{10,8},{9,1... | collective-permute-start | bytes 6291464 | tf_op jit(solution)/shard_map/ppermute | solution.py:668
  465.5 35.5 %collective-permute-start.27 = (bf16[512,1024]{1,0:T(8,128)(2,1)S(1)}, bf16[512,1024]{1,0:T(8,128)(2,1)S(1)}, u32[]{:S(2)}, u32[]{:S(2)}) collective-permute-start(bf16[512,1024]{1,0:T(8,128)(2,1)S(1)} %add_convert_fusion.6), channel_id=1, source_target_pairs={{0,8},{8,0},{16,24},{24,16},{1,9},{9,1},{17,25},{25,17},{2,10},{10... | collective-permute-start | bytes 3145736 | tf_op jit(solution)/shard_map/ppermute | solution.py:726
  527.0 27.6 %collective-permute-start.28 = (bf16[2,512,1024]{2,1,0:T(8,128)(2,1)S(1)}, bf16[2,512,1024]{2,1,0:T(8,128)(2,1)S(1)}, u32[]{:S(2)}, u32[]{:S(2)}) collective-permute-start(bf16[2,512,1024]{2,1,0:T(8,128)(2,1)S(1)} %add_convert_fusion), channel_id=1, source_target_pairs={{0,1},{1,0},{2,3},{3,2},{4,5},{5,4},{6,7},{7,6},{8,9},{9,8},{10,11... | collective-permute-start | bytes 6291464 | tf_op jit(solution)/shard_map/ppermute | solution.py:668
  537.6 6.7 %collective-permute-start.32 = (bf16[40,1024]{1,0:T(8,128)(2,1)S(1)}, bf16[40,1024]{1,0:T(8,128)(2,1)S(1)}, u32[]{:S(2)}, u32[]{:S(2)}) collective-permute-start(bf16[40,1024]{1,0:T(8,128)(2,1)S(1)} %add_convert_fusion.11), channel_id=1, source_target_pairs={{0,8},{8,0},{16,24},{24,16},{1,9},{9,1},{17,25},{25,17},{2,10},{10... | collective-permute-start | bytes 245768 | tf_op jit(solution)/shard_map/ppermute | solution.py:668
  544.3 9.0 %collective-permute-start.33 = (bf16[40,1024]{1,0:T(8,128)(2,1)S(1)}, bf16[40,1024]{1,0:T(8,128)(2,1)S(1)}, u32[]{:S(2)}, u32[]{:S(2)}) collective-permute-start(bf16[40,1024]{1,0:T(8,128)(2,1)S(1)} %add_convert_fusion.10), channel_id=1, source_target_pairs={{0,16},{8,24},{16,0},{24,8},{1,17},{9,25},{17,1},{25,9},{2,18},{10... | collective-permute-start | bytes 245768 | tf_op jit(solution)/shard_map/ppermute | solution.py:668
  (71 other events, 665.4 us)
Sparse Core Ops, SparseCore 0:
  11.3 149.3 all-gather.5
  272.9 178.9 reduce-scatter.2
  455.9 68.1 reduce-scatter.4
  526.4 44.0 all-gather.3

commit v7 on v6

--- a/solution.py
+++ b/solution.py
@@ -409,27 +409,25 @@
         out_ref[0, pair + 1, 2, 0] = gd[:, F:]
 
 
-def wgrad(picked, acts, dgus, blocks, groups, group, before=()):
+def wgrad(picked, acts, dgus, blocks, groups):
     n = len(picked)
     total, cap, D = picked[0][0].shape
     H = acts[0].shape[2]
     F = H // blocks
     E = total // groups
-    spec = lambda w: pl.BlockSpec((1, cap, w), lambda e: (e + group * E, 0, 0))
-    wide = lambda a: pl.BlockSpec((1,) + a.shape[1:], lambda e: (e + group * E, 0, 0))
+    spec = lambda w: pl.BlockSpec((1, cap, w), lambda e: (e, 0, 0))
+    wide = lambda a: pl.BlockSpec((1,) + a.shape[1:], lambda e: (e, 0, 0))
     operands = [*[p[i] for i in range(3) for p in picked], *acts, *dgus]
     return pl.pallas_call(
         functools.partial(wgrad_kernel, n, len(acts), blocks),
-        grid=(E,),
-        in_specs=[spec(D)] * (2 * n) + [spec(128)] * n + [wide(a) for a in (*acts, *dgus)]
-        + [pl.BlockSpec(memory_space=pl.ANY)] * len(before),
-        out_specs=pl.BlockSpec((1, blocks, 3, 1, D, F), lambda e: (group, 0, 0, e, 0, 0)),
+        grid=(total,),
+        in_specs=[spec(D)] * (2 * n) + [spec(128)] * n + [wide(a) for a in (*acts, *dgus)],
+        out_specs=pl.BlockSpec((1, blocks, 3, 1, D, F), lambda e: (e // E, 0, 0, e % E, 0, 0)),
         out_shape=pltpu.HBM((groups, blocks, 3, E, D, F), bf16),
-        input_output_aliases={len(operands) + i: i for i in range(len(before))},
         compiler_params=pltpu.CompilerParams(vmem_limit_bytes=56 << 20),
-        cost_estimate=busy(13),
+        cost_estimate=busy(26),
         name="wgrad",
-    )(*operands, *before)
+    )(*operands)
 
 
 def hot_columns(code, shift, cap):
@@ -825,8 +823,7 @@
     back_end_far, back_end = line_out(back)
     late_act, *_ = hold(done_apart[3], *far_back)
     used = (done_close[3], late_act), (done_close[4], done_apart[4]), shards, groups
-    parts = wgrad(picked, *used, 0)
-    parts = wgrad(picked, *used, 1, (parts,))
+    parts = wgrad(picked, *used)
     back_end_far, parts = hold(back_end_far, parts)
     across_far = line_over(back[2], back_end_far)
     across = line_over(back[3], back_end)

time: 592 us -> 593 us (level)
  starting transfers between devices: 55.7 us -> 70.2 us
  waiting for transfers between devices: 221 us -> 208 us
    reduce_scatter x1, starting transfers between devices: 0.04 us -> 11.2 us  [per_device_fast(): lax.psum_scatter(low, ('z', 'y'), scatter_dimension=0, tiled=True)]
    reduce_scatter x1, waiting for transfers between devices: 10.6 us -> 0.02 us  [per_device_fast(): lax.psum_scatter(parts.reshape((groups * shards,) + parts.shape[2:]), ('y...]
    pallas_call x2 -> x1, Pallas kernels: 27 us -> 25.6 us  [wgrad(): pl.pallas_call(functools.partial(wgrad_kernel, n, len(acts), blocks), gri...]
  transfers between devices with their start and end apart: 38 -> 38, of which waited for: 19 -> 18; matrix products, arithmetic and copies ran while one was open for 6% -> 6% of each run, Pallas kernels for 34% -> 33%
where the time goes in v7:
time: 593 us; the launch traced here: 583 us
  Pallas kernels  231 us (39%)
  waiting for transfers between devices  208 us (35%)
  starting transfers between devices  70.2 us (12%)
  other arithmetic  24.1 us (4%)
  local copies, waits for them, and re-layouts  20.1 us (3%)
  between operations  16 us (3%)
  matrix products  12.9 us (2%)
    pallas_call x3, Pallas kernels, ffn(): pl.pallas_call(functools.partial(ffn_kernel, n, blocks), grid=(len(groups...  45.8 us
    pallas_call x1, Pallas kernels, attend_back(): pl.pallas_call(functools.partial(attend_back_kernel, bq, bk), grid_spec=p...  44.1 us
    ppermute x2, waiting for transfers between devices, line_in(): return lax.ppermute(add_low(part, across_far), 'z', NEAR)  38.7 us
    ppermute x14, waiting for transfers between devices, swap(): return lax.ppermute(x, axis, [(i, i ^ bit) for i in range(count)])  38 us
    pallas_call x2, Pallas kernels, attend(): pl.pallas_call(functools.partial(attend_kernel, bq, bk, kv), grid_spec=pl...  31.8 us
    ppermute x2, waiting for transfers between devices, line_out(): lax.ppermute(parts[2], 'z', FROM_ENDS)  30.3 us
    ppermute x4, waiting for transfers between devices, line_second(): return (lax.ppermute(near, 'z', MIDDLE), lax.ppermute(across, 'z', TO_ENDS))  27 us
    pallas_call x1, Pallas kernels, wgrad(): pl.pallas_call(functools.partial(wgrad_kernel, n, len(acts), blocks), gri...  25.6 us
  transfers between devices with their start and end apart: 38, of which 18 were waited for; matrix products, arithmetic and copies ran while one was open for 6% of the time, Pallas kernels for 33%

profile of v7, /device:TPU:0, one launch (start us, length us, event | category | flops | bytes accessed | tf_op | source)
XLA Modules:
  0.0 583.0 jit_solution(3112214956124865254)
XLA Ops:
  15.4 4.9 collective-permute-start
  22.5 11.2 %project.1 = (bf16[2048,1024]{1,0:T(8,128)(2,1)}, bf16[4,2048,128]{2,1,0:T(8,128)(2,1)}, bf16[2048,128]{1,0:T(8,128)(2,1)}, bf16[2048,256]{1,0:T(8,128)(2,1)}) custom-call(bf16[2048,1024]{1,0:T(8,128)(2,1)} %x_ref.5, bf16[1,1024]{1,0:T(2,128)(2,1)S(1)} %broadcast_in_dim.36.gain_ref, bf16[1024,256]{1,0:T(8,128)(2,1)S(1)} %copy-done.7, ...), custom_call_target="tpu_custom_call" | custom-call | flops 900000000 | tf_op jit(solution)/shard_map/project/pallas_call | solution.py:93
  33.7 15.9 %attend.2 = (bf16[2048,256]{1,0:T(8,128)(2,1)}, f32[2,8,4096]{2,1,0:T(8,128)}) custom-call(s32[1]{0:T(128)S(6)} %copy.66.prefix_ref, bf16[4,2048,128]{2,1,0:T(8,128)(2,1)} %get-tuple-element.155.q_ref, bf16[2048,128]{1,0:T(8,128)(2,1)} %get-tuple-element.156.k_ref, bf16[2048,256]{1,0:T(8,128)(2,1)} %get-tuple-element.157.v_ref), custom_call_target="tpu_custom_call" | custom-call | flops 1400000000 | tf_op jit(solution)/shard_map/attend/pallas_call | solution.py:159
  51.5 15.9 %attend.3 = (bf16[2048,256]{1,0:T(8,128)(2,1)}, f32[2,8,4096]{2,1,0:T(8,128)}) custom-call(s32[1]{0:T(128)S(6)} %copy.66.prefix_ref, bf16[4,2048,128]{2,1,0:T(8,128)(2,1)} %get-tuple-element.155.q_ref, bf16[2048,128]{1,0:T(8,128)(2,1)} %get-tuple-element.156.k_ref, ...), custom_call_target="tpu_custom_call", output_to_operand_aliasing={{0}: (4, {}), {1}: (5, {})} | custom-call | flops 1400000000 | tf_op jit(solution)/shard_map/attend/pallas_call | solution.py:159
  79.2 23.9 %collective-permute-done.6.refs_2_ = bf16[512,1152]{1,0:T(8,128)(2,1)} collective-permute-done((bf16[512,1152]{1,0:T(8,128)(2,1)}, bf16[512,1152]{1,0:T(8,128)(2,1)}, u32[]{:S(2)}, u32[]{:S(2)}) %collective-permute-start.6) | collective-permute-done | bytes 1179680 | tf_op jit(solution)/shard_map/ppermute | solution.py:700
  103.1 21.5 %collective-permute-done.5 = bf16[512,1024]{1,0:T(8,128)(2,1)} collective-permute-done((bf16[512,1024]{1,0:T(8,128)(2,1)}, bf16[512,1024]{1,0:T(8,128)(2,1)}, u32[]{:S(2)}, u32[]{:S(2)}) %collective-permute-start.5) | collective-permute-done | bytes 1048608 | tf_op jit(solution)/shard_map/ppermute | solution.py:666
  132.7 5.3 collective-permute-start.8
  140.3 5.0 pick.4
  146.1 13.0 %collective-permute-done.8.refs_0_ = bf16[512,1024]{1,0:T(8,128)(2,1)} collective-permute-done((bf16[512,1024]{1,0:T(8,128)(2,1)S(1)}, bf16[512,1024]{1,0:T(8,128)(2,1)}, u32[]{:S(2)}, u32[]{:S(2)}) %collective-permute-start.8) | collective-permute-done | bytes 1048608 | tf_op jit(solution)/shard_map/ppermute | solution.py:696
  162.0 6.2 %pick.5 = (bf16[8,128,1024]{2,1,0:T(8,128)(2,1)}, bf16[8,128,1024]{2,1,0:T(8,128)(2,1)}, f32[8,128,128]{2,1,0:T(8,128)}, f32[512,128]{1,0:T(8,128)S(1)}, f32[512,128]{1,0:T(8,128)S(1)}) custom-call(s32[9]{0:T(128)S(1)} %pad_add_fusion.shift_ref, bf16[512,1024]{1,0:T(8,128)(2,1)} %collective-permute-done.8.refs_0_, ...), custom_call_target="tpu_custom_call" | custom-call | flops 400000000 | tf_op jit(solution)/shard_map/pick/pallas_call | solution.py:317
  169.6 12.1 %ffn.3 = (bf16[8,256,1024]{2,1,0:T(8,128)(2,1)}, bf16[8,256,1024]{2,1,0:T(8,128)(2,1)}, f32[8,256,128]{2,1,0:T(8,128)}, bf16[8,256,512]{2,1,0:T(8,128)(2,1)}, bf16[8,256,1024]{2,1,0:T(8,128)(2,1)}) custom-call(bf16[8,128,1024]{2,1,0:T(8,128)(2,1)} %get-tuple-element.182.refs_0_, bf16[8,128,1024]{2,1,0:T(8,128)(2,1)} %get-tuple-element.183.refs_1_, ...), custom_call_target="tpu_custom_call" | custom-call | flops 1200000000 | tf_op jit(solution)/shard_map/ffn/pallas_call | solution.py:380
  186.1 6.9 %pick.6 = (bf16[8,128,1024]{2,1,0:T(8,128)(2,1)}, bf16[8,128,1024]{2,1,0:T(8,128)(2,1)}, f32[8,128,128]{2,1,0:T(8,128)}, f32[512,128]{1,0:T(8,128)S(1)}, f32[512,128]{1,0:T(8,128)S(1)}) custom-call(s32[9]{0:T(128)S(1)} %pad_add_fusion.shift_ref, bf16[512,1024]{1,0:T(8,128)(2,1)} %collective-permute-done.11.refs_0_, ...), custom_call_target="tpu_custom_call" | custom-call | flops 400000000 | tf_op jit(solution)/shard_map/pick/pallas_call | solution.py:317
  193.0 12.2 %ffn.4 = (bf16[8,256,1024]{2,1,0:T(8,128)(2,1)}, bf16[8,256,1024]{2,1,0:T(8,128)(2,1)}, f32[8,256,128]{2,1,0:T(8,128)}, bf16[8,256,512]{2,1,0:T(8,128)(2,1)}, bf16[8,256,1024]{2,1,0:T(8,128)(2,1)}) custom-call(bf16[8,128,1024]{2,1,0:T(8,128)(2,1)} %get-tuple-element.182.refs_0_, ...), custom_call_target="tpu_custom_call", output_to_operand_aliasing={{0}: (7, {}), {1}: (8, {}), {2}: (9, {}), {3}: (10, {}), {4... | custom-call | flops 1200000000 | tf_op jit(solution)/shard_map/ffn/pallas_call | solution.py:380
  207.9 6.6 %pick.7 = (bf16[8,128,1024]{2,1,0:T(8,128)(2,1)}, bf16[8,128,1024]{2,1,0:T(8,128)(2,1)}, f32[8,128,128]{2,1,0:T(8,128)}, f32[512,128]{1,0:T(8,128)S(1)}, f32[512,128]{1,0:T(8,128)S(1)}) custom-call(s32[9]{0:T(128)S(1)} %pad_add_fusion.shift_ref, bf16[512,1024]{1,0:T(8,128)(2,1)S(1)} %collective-permute-done.12.refs_0_, ...), custom_call_target="tpu_custom_call" | custom-call | flops 400000000 | tf_op jit(solution)/shard_map/pick/pallas_call | solution.py:317
  214.6 21.6 %ffn.5 = (bf16[8,256,1024]{2,1,0:T(8,128)(2,1)}, bf16[8,256,1024]{2,1,0:T(8,128)(2,1)}, f32[8,256,128]{2,1,0:T(8,128)}, bf16[8,256,512]{2,1,0:T(8,128)(2,1)}, bf16[8,256,1024]{2,1,0:T(8,128)(2,1)}) custom-call(bf16[8,128,1024]{2,1,0:T(8,128)(2,1)} %get-tuple-element.214.refs_0_.refs_2_, bf16[8,128,1024]{2,1,0:T(8,128)(2,1)} %get-tuple-element.215.refs_1_.refs_3_, ...), custom_call_target="tpu_custom_call" | custom-call | flops 2400000000 | tf_op jit(solution)/shard_map/ffn/pallas_call | solution.py:380
  244.3 25.6 %wgrad.1 = bf16[2,4,3,4,1024,128]{5,4,3,2,1,0:T(8,128)(2,1)} custom-call(bf16[8,128,1024]{2,1,0:T(8,128)(2,1)} %get-tuple-element.182.refs_0_, bf16[8,128,1024]{2,1,0:T(8,128)(2,1)} %get-tuple-element.183.refs_1_, bf16[8,128,1024]{2,1,0:T(8,128)(2,1)} %get-tuple-element.214.refs_0_.refs_2_, bf16[8,128,1024]{2,1,0:T(8,128)(2,1)} %get-tuple-element.215.refs_1_.refs_3_, ...), custom_call_target="tpu_custom_call" | custom-call | flops 2600000000 | tf_op jit(solution)/shard_map/wgrad/pallas_call | solution.py:421
  271.0 11.2 %reduce-scatter.5.cloned.1.call-start = ((), (), s32[]{:S(2)}) async-start(), calls=%async_computation.3 | async-start | bytes 1769472 | tf_op jit(solution)/shard_map/reduce_scatter | solution.py:882
  286.9 5.6 merge_back.2
  292.5 12.5 %collective-permute-done.16 = bf16[512,1152]{1,0:T(8,128)(2,1)S(1)} collective-permute-done((bf16[512,1152]{1,0:T(8,128)(2,1)}, bf16[512,1152]{1,0:T(8,128)(2,1)S(1)}, u32[]{:S(2)}, u32[]{:S(2)}) %collective-permute-start.16) | collective-permute-done | bytes 1179680 | tf_op jit(solution)/shard_map/ppermute | solution.py:712
  306.5 7.6 %collective-permute-start.15 = (bf16[512,1152]{1,0:T(8,128)(2,1)S(1)}, bf16[512,1152]{1,0:T(8,128)(2,1)S(1)}, u32[]{:S(2)}, u32[]{:S(2)}) collective-permute-start(bf16[512,1152]{1,0:T(8,128)(2,1)S(1)} %add_convert_fusion.3), channel_id=1, source_target_pairs={{0,8},{8,0},{16,24},{24,16},{1,9},{9,1},{17,25},{25,17},{2,10},{10... | collective-permute-start | bytes 3538952 | tf_op jit(solution)/shard_map/ppermute | solution.py:724
  314.0 5.0 merge_out.2
  321.1 5.2 merge_out.3
  326.2 5.1 collective-permute-done.15
  334.8 6.4 %collective-permute-start.21 = (bf16[512,1024]{1,0:T(8,128)(2,1)S(1)}, bf16[512,1024]{1,0:T(8,128)(2,1)S(1)}, u32[]{:S(2)}, u32[]{:S(2)}) collective-permute-start(bf16[512,1024]{1,0:T(8,128)(2,1)S(1)} %get-tuple-element.244), channel_id=1, source_target_pairs={{0,8},{24,16},{1,9},{25,17},{2,10},{26,18},{3,11},{27,19},{4,12},{... | collective-permute-start | bytes 3145736 | tf_op jit(solution)/shard_map/ppermute | solution.py:712
  346.8 17.9 %collective-permute-done.21 = bf16[512,1024]{1,0:T(8,128)(2,1)S(1)} collective-permute-done((bf16[512,1024]{1,0:T(8,128)(2,1)S(1)}, bf16[512,1024]{1,0:T(8,128)(2,1)S(1)}, u32[]{:S(2)}, u32[]{:S(2)}) %collective-permute-start.21) | collective-permute-done | bytes 1048608 | tf_op jit(solution)/shard_map/ppermute | solution.py:712
  364.6 22.1 %collective-permute-done.20 = bf16[512,1024]{1,0:T(8,128)(2,1)S(1)} collective-permute-done((bf16[512,1024]{1,0:T(8,128)(2,1)S(1)}, bf16[512,1024]{1,0:T(8,128)(2,1)S(1)}, u32[]{:S(2)}, u32[]{:S(2)}) %collective-permute-start.20) | collective-permute-done | bytes 1048608 | tf_op jit(solution)/shard_map/ppermute | solution.py:712
  401.2 44.1 %attend_back.1 = bf16[2048,512]{1,0:T(8,128)(2,1)} custom-call(s32[1]{0:T(128)S(6)} %copy.66.prefix_ref, bf16[4,2048,128]{2,1,0:T(8,128)(2,1)} %get-tuple-element.155.q_ref, bf16[2048,128]{1,0:T(8,128)(2,1)S(1)} %copy-done.41, bf16[2048,256]{1,0:T(8,128)(2,1)S(1)} %copy-done.40, bf16[2048,256]{1,0:T(8,128)(2,1)S(1)} %copy-done.1, ...), custom_call_target="tpu_custom_call" | custom-call | flops 4600000000 | tf_op jit(solution)/shard_map/attend_back/pallas_call | solution.py:250
  469.1 33.7 %collective-permute-done.27 = bf16[512,1024]{1,0:T(8,128)(2,1)S(1)} collective-permute-done((bf16[512,1024]{1,0:T(8,128)(2,1)S(1)}, bf16[512,1024]{1,0:T(8,128)(2,1)S(1)}, u32[]{:S(2)}, u32[]{:S(2)}) %collective-permute-start.27) | collective-permute-done | bytes 1048608 | tf_op jit(solution)/shard_map/ppermute | solution.py:724
  502.7 22.6 %reduce-scatter.5.cloned.1.call-done = bf16[192,512]{1,0:T(8,128)(2,1)} async-done(((bf16[1536,512]{1,0:T(8,128)(2,1)}), bf16[192,512]{1,0:T(8,128)(2,1)}) %reduce-scatter.5.cloned.1.call-update) | async-done | bytes 196624 | tf_op jit(solution)/shard_map/reduce_scatter | solution.py:882
  549.0 5.6 finish.2.refs_0_
  555.9 5.6 finish.3
  561.4 10.7 %all-gather.4.cloned.1.call-done.low_ref.left_ref.right_ref = bf16[1536,512]{1,0:T(8,128)(2,1)} async-done(((bf16[192,512]{1,0:T(8,128)(2,1)}), bf16[1536,512]{1,0:T(8,128)(2,1)}) %all-gather.4.cloned.1.call-update) | async-done | bytes 1572880 | tf_op jit(solution)/shard_map/all_gather | solution.py:896
  (255 shorter events, 138.7 us)
Async XLA Ops:
  7.2 162.4 %all-gather.6.cloned.1.call-start = ((), (), s32[]{:S(2)}) async-start(), calls=%async_computation.5 | async-start | bytes 28311552 | tf_op jit(solution)/shard_map/all_gather | solution.py:777
  11.2 439.5 %reduce-scatter.3.cloned.1.call-start = ((), (), s32[]{:S(2)}) async-start(), calls=%async_computation.2 | async-start | bytes 28311552 | tf_op jit(solution)/shard_map/reduce_scatter | solution.py:839
  13.7 35.9 %collective-permute-start.1 = (bf16[512,1152]{1,0:T(8,128)(2,1)S(1)}, bf16[512,1152]{1,0:T(8,128)(2,1)}, u32[]{:S(2)}, u32[]{:S(2)}) collective-permute-start(bf16[512,1152]{1,0:T(8,128)(2,1)S(1)} %fusion.1.refs_1_), channel_id=1, source_target_pairs={{8,16},{16,8},{9,17},{17,9},{10,18},{18,10},{11,19},{19,11},{12,20... | collective-permute-start | bytes 3538952 | tf_op jit(solution)/shard_map/ppermute | solution.py:696
  15.4 34.2 %collective-permute-start = (bf16[512,1152]{1,0:T(8,128)(2,1)S(1)}, bf16[512,1152]{1,0:T(8,128)(2,1)}, u32[]{:S(2)}, u32[]{:S(2)}) collective-permute-start(bf16[512,1152]{1,0:T(8,128)(2,1)S(1)} %fusion.1.refs_1_), channel_id=1, source_target_pairs={{0,8},{8,0},{16,24},{24,16},{1,9},{9,1},{17,25},{25,17},{2,10},{10... | collective-permute-start | bytes 3538952 | tf_op jit(solution)/shard_map/ppermute | solution.py:696
  49.7 23.7 %collective-permute-start.3 = (bf16[512,1152]{1,0:T(8,128)(2,1)}, bf16[512,1152]{1,0:T(8,128)(2,1)}, u32[]{:S(2)}, u32[]{:S(2)}) collective-permute-start(bf16[512,1152]{1,0:T(8,128)(2,1)} %collective-permute-done.refs_1_), channel_id=1, source_target_pairs={{8,16},{16,8},{9,17},{17,9},{10,18},{18,10},{11,19},{19,11},{12,20... | collective-permute-start | bytes 3538952 | tf_op jit(solution)/shard_map/ppermute | solution.py:700
  71.6 6.0 %collective-permute-start.2 = (bf16[512,1024]{1,0:T(8,128)(2,1)}, bf16[512,1024]{1,0:T(8,128)(2,1)}, u32[]{:S(2)}, u32[]{:S(2)}) collective-permute-start(bf16[512,1024]{1,0:T(8,128)(2,1)} %get-tuple-element.164), channel_id=1, source_target_pairs={{0,1},{1,0},{2,3},{3,2},{4,5},{5,4},{6,7},{7,6},{8,9},{9,8},{10,11... | collective-permute-start | bytes 3145736 | tf_op jit(solution)/shard_map/ppermute | solution.py:666
  72.0 31.0 %collective-permute-start.6 = (bf16[512,1152]{1,0:T(8,128)(2,1)}, bf16[512,1152]{1,0:T(8,128)(2,1)}, u32[]{:S(2)}, u32[]{:S(2)}) collective-permute-start(bf16[512,1152]{1,0:T(8,128)(2,1)} %collective-permute-done.1.refs_3_), channel_id=1, source_target_pairs={{8,0},{16,24},{9,1},{17,25},{10,2},{18,26},{11,3},{19,27},{12,4},{... | collective-permute-start | bytes 3538952 | tf_op jit(solution)/shard_map/ppermute | solution.py:700
  73.4 54.1 %collective-permute-start.7 = (bf16[512,1152]{1,0:T(8,128)(2,1)}, bf16[512,1152]{1,0:T(8,128)(2,1)}, u32[]{:S(2)}, u32[]{:S(2)}) collective-permute-start(bf16[512,1152]{1,0:T(8,128)(2,1)} %collective-permute-done.3.refs_3_), channel_id=1, source_target_pairs={{8,0},{16,24},{9,1},{17,25},{10,2},{18,26},{11,3},{19,27},{12,4},{... | collective-permute-start | bytes 3538952 | tf_op jit(solution)/shard_map/ppermute | solution.py:704
  76.0 48.5 %collective-permute-start.5 = (bf16[512,1024]{1,0:T(8,128)(2,1)}, bf16[512,1024]{1,0:T(8,128)(2,1)}, u32[]{:S(2)}, u32[]{:S(2)}) collective-permute-start(bf16[512,1024]{1,0:T(8,128)(2,1)} %add_convert_fusion.9), channel_id=1, source_target_pairs={{0,2},{2,0},{1,3},{3,1},{4,6},{6,4},{5,7},{7,5},{8,10},{10,8},{9,1... | collective-permute-start | bytes 3145736 | tf_op jit(solution)/shard_map/ppermute | solution.py:666
  130.8 15.2 %collective-permute-start.9 = (bf16[512,1024]{1,0:T(8,128)(2,1)S(1)}, bf16[512,1024]{1,0:T(8,128)(2,1)}, u32[]{:S(2)}, u32[]{:S(2)}) collective-permute-start(bf16[512,1024]{1,0:T(8,128)(2,1)S(1)} %multiply_convert_fusion.refs_0_), channel_id=1, source_target_pairs={{8,16},{16,8},{9,17},{17,9},{10,18},{18,10},{11,19},{19,11},{12,20... | collective-permute-start | bytes 3145736 | tf_op jit(solution)/shard_map/ppermute | solution.py:696
  132.7 26.3 %collective-permute-start.8 = (bf16[512,1024]{1,0:T(8,128)(2,1)S(1)}, bf16[512,1024]{1,0:T(8,128)(2,1)}, u32[]{:S(2)}, u32[]{:S(2)}) collective-permute-start(bf16[512,1024]{1,0:T(8,128)(2,1)S(1)} %multiply_convert_fusion.refs_0_), channel_id=1, source_target_pairs={{0,8},{8,0},{16,24},{24,16},{1,9},{9,1},{17,25},{25,17},{2,10},{10... | collective-permute-start | bytes 3145736 | tf_op jit(solution)/shard_map/ppermute | solution.py:696
  159.0 22.7 %collective-permute-start.10 = (bf16[512,1024]{1,0:T(8,128)(2,1)}, bf16[512,1024]{1,0:T(8,128)(2,1)}, u32[]{:S(2)}, u32[]{:S(2)}) collective-permute-start(bf16[512,1024]{1,0:T(8,128)(2,1)} %collective-permute-done.8.refs_0_), channel_id=1, source_target_pairs={{8,16},{16,8},{9,17},{17,9},{10,18},{18,10},{11,19},{19,11},{12,20... | collective-permute-start | bytes 3145736 | tf_op jit(solution)/shard_map/ppermute | solution.py:700
  160.7 24.1 %collective-permute-start.11 = (bf16[512,1024]{1,0:T(8,128)(2,1)}, bf16[512,1024]{1,0:T(8,128)(2,1)}, u32[]{:S(2)}, u32[]{:S(2)}) collective-permute-start(bf16[512,1024]{1,0:T(8,128)(2,1)} %collective-permute-done.9.refs_1_), channel_id=1, source_target_pairs={{8,0},{16,24},{9,1},{17,25},{10,2},{18,26},{11,3},{19,27},{12,4},{... | collective-permute-start | bytes 3145736 | tf_op jit(solution)/shard_map/ppermute | solution.py:700
  184.8 23.1 %collective-permute-start.12 = (bf16[512,1024]{1,0:T(8,128)(2,1)}, bf16[512,1024]{1,0:T(8,128)(2,1)S(1)}, u32[]{:S(2)}, u32[]{:S(2)}) collective-permute-start(bf16[512,1024]{1,0:T(8,128)(2,1)} %collective-permute-done.10.refs_1_), channel_id=1, source_target_pairs={{8,0},{16,24},{9,1},{17,25},{10,2},{18,26},{11,3},{19,27},{12,4},{... | collective-permute-start | bytes 3145736 | tf_op jit(solution)/shard_map/ppermute | solution.py:704
  242.3 27.7 %collective-permute-start.13 = (bf16[512,1152]{1,0:T(8,128)(2,1)S(1)}, bf16[512,1152]{1,0:T(8,128)(2,1)S(1)}, u32[]{:S(2)}, u32[]{:S(2)}) collective-permute-start(bf16[512,1152]{1,0:T(8,128)(2,1)S(1)} %get-tuple-element.223), channel_id=1, source_target_pairs={{0,8},{24,16},{1,9},{25,17},{2,10},{26,18},{3,11},{27,19},{4,12},{... | collective-permute-start | bytes 3538952 | tf_op jit(solution)/shard_map/ppermute | solution.py:712
  271.0 254.4 %reduce-scatter.5.cloned.1.call-start = ((), (), s32[]{:S(2)}) async-start(), calls=%async_computation.3 | async-start | bytes 1769472 | tf_op jit(solution)/shard_map/reduce_scatter | solution.py:882
  282.2 22.8 %collective-permute-start.16 = (bf16[512,1152]{1,0:T(8,128)(2,1)}, bf16[512,1152]{1,0:T(8,128)(2,1)S(1)}, u32[]{:S(2)}, u32[]{:S(2)}) collective-permute-start(bf16[512,1152]{1,0:T(8,128)(2,1)} %copy-done.10), channel_id=1, source_target_pairs={{0,8},{24,16},{1,9},{25,17},{2,10},{26,18},{3,11},{27,19},{4,12},{... | collective-permute-start | bytes 3538952 | tf_op jit(solution)/shard_map/ppermute | solution.py:712
  286.1 20.0 %collective-permute-start.14 = (bf16[512,1152]{1,0:T(8,128)(2,1)S(1)}, bf16[512,1152]{1,0:T(8,128)(2,1)S(1)}, u32[]{:S(2)}, u32[]{:S(2)}) collective-permute-start(bf16[512,1152]{1,0:T(8,128)(2,1)S(1)} %add_convert_fusion.4), channel_id=1, source_target_pairs={{8,16},{16,8},{9,17},{17,9},{10,18},{18,10},{11,19},{19,11},{12,20... | collective-permute-start | bytes 3538952 | tf_op jit(solution)/shard_map/ppermute | solution.py:720
  305.3 20.9 %collective-permute-start.17 = (bf16[512,1152]{1,0:T(8,128)(2,1)S(1)}, bf16[512,1152]{1,0:T(8,128)(2,1)S(1)}, u32[]{:S(2)}, u32[]{:S(2)}) collective-permute-start(bf16[512,1152]{1,0:T(8,128)(2,1)S(1)} %add_convert_fusion.2), channel_id=1, source_target_pairs={{8,16},{16,8},{9,17},{17,9},{10,18},{18,10},{11,19},{19,11},{12,20... | collective-permute-start | bytes 3538952 | tf_op jit(solution)/shard_map/ppermute | solution.py:720
  306.5 24.8 %collective-permute-start.15 = (bf16[512,1152]{1,0:T(8,128)(2,1)S(1)}, bf16[512,1152]{1,0:T(8,128)(2,1)S(1)}, u32[]{:S(2)}, u32[]{:S(2)}) collective-permute-start(bf16[512,1152]{1,0:T(8,128)(2,1)S(1)} %add_convert_fusion.3), channel_id=1, source_target_pairs={{0,8},{8,0},{16,24},{24,16},{1,9},{9,1},{17,25},{25,17},{2,10},{10... | collective-permute-start | bytes 3538952 | tf_op jit(solution)/shard_map/ppermute | solution.py:724
  334.7 9.4 %collective-permute-start.19 = (bf16[512,1024]{1,0:T(8,128)(2,1)S(1)}, bf16[512,1024]{1,0:T(8,128)(2,1)S(1)}, u32[]{:S(2)}, u32[]{:S(2)}) collective-permute-start(bf16[512,1024]{1,0:T(8,128)(2,1)S(1)} %subtract_convert_fusion.refs_0_), channel_id=1, source_target_pairs={{0,1},{1,0},{2,3},{3,2},{4,5},{5,4},{6,7},{7,6},{8,9},{9,8},{10,11... | collective-permute-start | bytes 3145736 | tf_op jit(solution)/shard_map/ppermute | solution.py:666
  334.8 29.8 %collective-permute-start.21 = (bf16[512,1024]{1,0:T(8,128)(2,1)S(1)}, bf16[512,1024]{1,0:T(8,128)(2,1)S(1)}, u32[]{:S(2)}, u32[]{:S(2)}) collective-permute-start(bf16[512,1024]{1,0:T(8,128)(2,1)S(1)} %get-tuple-element.244), channel_id=1, source_target_pairs={{0,8},{24,16},{1,9},{25,17},{2,10},{26,18},{3,11},{27,19},{4,12},{... | collective-permute-start | bytes 3145736 | tf_op jit(solution)/shard_map/ppermute | solution.py:712
  341.2 45.5 %collective-permute-start.20 = (bf16[512,1024]{1,0:T(8,128)(2,1)S(1)}, bf16[512,1024]{1,0:T(8,128)(2,1)S(1)}, u32[]{:S(2)}, u32[]{:S(2)}) collective-permute-start(bf16[512,1024]{1,0:T(8,128)(2,1)S(1)} %get-tuple-element.248), channel_id=1, source_target_pairs={{0,8},{24,16},{1,9},{25,17},{2,10},{26,18},{3,11},{27,19},{4,12},{... | collective-permute-start | bytes 3145736 | tf_op jit(solution)/shard_map/ppermute | solution.py:712
  342.6 48.4 %collective-permute-start.18 = (bf16[512,1024]{1,0:T(8,128)(2,1)S(1)}, bf16[512,1024]{1,0:T(8,128)(2,1)}, u32[]{:S(2)}, u32[]{:S(2)}) collective-permute-start(bf16[512,1024]{1,0:T(8,128)(2,1)S(1)} %subtract_convert_fusion.refs_0_), channel_id=1, source_target_pairs={{0,2},{2,0},{1,3},{3,1},{4,6},{6,4},{5,7},{7,5},{8,10},{10,8},{9,1... | collective-permute-start | bytes 3145736 | tf_op jit(solution)/shard_map/ppermute | solution.py:666
  392.8 57.9 %collective-permute-start.23 = (bf16[512,1024]{1,0:T(8,128)(2,1)}, bf16[512,1024]{1,0:T(8,128)(2,1)S(1)}, u32[]{:S(2)}, u32[]{:S(2)}) collective-permute-start(bf16[512,1024]{1,0:T(8,128)(2,1)} %get-tuple-element.265), channel_id=1, source_target_pairs={{8,16},{16,8},{9,17},{17,9},{10,18},{18,10},{11,19},{19,11},{12,20... | collective-permute-start | bytes 3145736 | tf_op jit(solution)/shard_map/ppermute | solution.py:870
  393.7 57.1 %collective-permute-start.24 = (bf16[512,1024]{1,0:T(8,128)(2,1)}, bf16[512,1024]{1,0:T(8,128)(2,1)}, u32[]{:S(2)}, u32[]{:S(2)}) collective-permute-start(bf16[512,1024]{1,0:T(8,128)(2,1)} %get-tuple-element.266), channel_id=1, source_target_pairs={{8,16},{16,8},{9,17},{17,9},{10,18},{18,10},{11,19},{19,11},{12,20... | collective-permute-start | bytes 3145736 | tf_op jit(solution)/shard_map/ppermute | solution.py:870
  455.5 116.7 %all-gather.4.cloned.1.call-start = ((), (), s32[]{:S(2)}) async-start(), calls=%async_computation.4 | async-start | bytes 1769472 | tf_op jit(solution)/shard_map/all_gather | solution.py:896
  463.1 62.2 %collective-permute-start.26 = (bf16[2,512,1024]{2,1,0:T(8,128)(2,1)S(1)}, bf16[2,512,1024]{2,1,0:T(8,128)(2,1)}, u32[]{:S(2)}, u32[]{:S(2)}) collective-permute-start(bf16[2,512,1024]{2,1,0:T(8,128)(2,1)S(1)} %add_convert_fusion.1), channel_id=1, source_target_pairs={{0,2},{2,0},{1,3},{3,1},{4,6},{6,4},{5,7},{7,5},{8,10},{10,8},{9,1... | collective-permute-start | bytes 6291464 | tf_op jit(solution)/shard_map/ppermute | solution.py:666
  465.2 37.6 %collective-permute-start.27 = (bf16[512,1024]{1,0:T(8,128)(2,1)S(1)}, bf16[512,1024]{1,0:T(8,128)(2,1)S(1)}, u32[]{:S(2)}, u32[]{:S(2)}) collective-permute-start(bf16[512,1024]{1,0:T(8,128)(2,1)S(1)} %add_convert_fusion.6), channel_id=1, source_target_pairs={{0,8},{8,0},{16,24},{24,16},{1,9},{9,1},{17,25},{25,17},{2,10},{10... | collective-permute-start | bytes 3145736 | tf_op jit(solution)/shard_map/ppermute | solution.py:724
  528.2 27.6 %collective-permute-start.28 = (bf16[2,512,1024]{2,1,0:T(8,128)(2,1)S(1)}, bf16[2,512,1024]{2,1,0:T(8,128)(2,1)S(1)}, u32[]{:S(2)}, u32[]{:S(2)}) collective-permute-start(bf16[2,512,1024]{2,1,0:T(8,128)(2,1)S(1)} %add_convert_fusion), channel_id=1, source_target_pairs={{0,1},{1,0},{2,3},{3,2},{4,5},{5,4},{6,7},{7,6},{8,9},{9,8},{10,11... | collective-permute-start | bytes 6291464 | tf_op jit(solution)/shard_map/ppermute | solution.py:666
  538.9 6.7 %collective-permute-start.32 = (bf16[40,1024]{1,0:T(8,128)(2,1)S(1)}, bf16[40,1024]{1,0:T(8,128)(2,1)S(1)}, u32[]{:S(2)}, u32[]{:S(2)}) collective-permute-start(bf16[40,1024]{1,0:T(8,128)(2,1)S(1)} %add_convert_fusion.11), channel_id=1, source_target_pairs={{0,8},{8,0},{16,24},{24,16},{1,9},{9,1},{17,25},{25,17},{2,10},{10... | collective-permute-start | bytes 245768 | tf_op jit(solution)/shard_map/ppermute | solution.py:666
  545.6 9.0 %collective-permute-start.33 = (bf16[40,1024]{1,0:T(8,128)(2,1)S(1)}, bf16[40,1024]{1,0:T(8,128)(2,1)S(1)}, u32[]{:S(2)}, u32[]{:S(2)}) collective-permute-start(bf16[40,1024]{1,0:T(8,128)(2,1)S(1)} %add_convert_fusion.10), channel_id=1, source_target_pairs={{0,16},{8,24},{16,0},{24,8},{1,17},{9,25},{17,1},{25,9},{2,18},{10... | collective-permute-start | bytes 245768 | tf_op jit(solution)/shard_map/ppermute | solution.py:666
  (71 other events, 682.9 us)
Sparse Core Ops, SparseCore 0:
  11.3 149.3 all-gather.5
  271.1 178.8 reduce-scatter.2
  455.6 69.6 reduce-scatter.4
  527.6 44.4 all-gather.3
